TPU v7x, 32 devices: a whole 2x2x4 slice. The times are simulated.
32 devices in a mesh: down: 16 (over z, y, core), cross: 2 (over x).
Axes of the slice: x: 2, y: 2, z: 4, core: 2. Of those that a mesh axis runs over, the one named last changes fastest.
Arguments:
- particles: float32 [4096, 12, 128], P(('down', 'cross')), may hold values from -4 to 14.5, as said below
- anchor_down: int32 [2, 4096], P(None, ('down', 'cross')), may hold values from -4 to 12
- anchor_cross: int32 [2, 4096], P(None, ('down', 'cross')), may hold values from -4 to 244
- move_count: int32 [2, 4, 16, 2], P(None, None, 'down', 'cross'), may hold values from 0 to 13, as said below
- move_slots: int32 [2, 4, 13, 16, 2], P(None, None, None, 'down', 'cross'), may hold values from 0 to 127, as said below
Outputs:
- moved_particles: float32 [4096, 12, 128], P(('down', 'cross'))
Inputs may be any that keep to these rules, and one draw needn't show every extreme that they name: `move_count`: entry 0 of tile (i, j) equals entry 1 of tile (i + 1, j), and entry 2 of (i, j) equals entry 3 of (i, j + 1); entries toward the outside of the grid are 0; in every step some link carries 13. `move_slots`: for each step and tile the 52 slot numbers are different. `particles`: field 0 lies in [0.5, 8 - 1.5] and field 1 in [0.5, 16 - 1.5]; fields 7 to 10 are positive.
All inputs are finite; a program needn't handle non-finite values.
Results may differ from a plain program's by a relative error of at most 0.0003.
Values sent between devices are 32-bit elements; how exact they have to be, the bound alone decides.
No kernel may reach another device: no remote copies, remote signals or barrier semaphores. Data moves between devices by JAX's collectives and lax.ppermute only.
A program may use at most 64 MiB of HBM per device.

v0:
```python
import math

import jax
import jax.numpy as jnp
from jax import lax
from jax.sharding import PartitionSpec as P

WIN_DOWN = 8
WIN_CROSS = 16
GHOST = 4
STEPS = 2
MOVE_CAP = 13
TILE_DOWN = 16
TILE_CROSS = 256


TIME_STEP = 0.1
GRAVITY = 5.6
MASS_FLOOR = 0.5
HIGHEST = lax.Precision.HIGHEST
group_limit = 8


def padded(x, sides, width):
    for axis, dim in sides:
        size, length = (lax.axis_size(axis), x.shape[dim])
        up = [(i, (i + 1) % size) for i in range(size - 1)]
        down = [(j, i) for i, j in up]
        last = lax.slice_in_dim(x, length - width, length, axis=dim)
        initial = lax.slice_in_dim(x, 0, width, axis=dim)
        before = lax.ppermute(last, axis, up)
        after = lax.ppermute(initial, axis, down)
        x = jnp.concatenate([before, x, after], axis=dim)
    return x


def spline_pair(distance):
    magnitude = jnp.abs(distance)
    inside = 0.75 - distance * distance
    remote = 0.5 * (1.5 - magnitude) * (1.5 - magnitude)
    spline_value = jnp.where(magnitude < 0.5, inside, jnp.where(magnitude < 1.5, remote, 0.0))
    slope_far = jnp.where(distance > 0.0, distance - 1.5, distance + 1.5)
    spline_slope = jnp.where(
        magnitude < 0.5, -2.0 * distance, jnp.where(magnitude < 1.5, slope_far, 0.0)
    )
    return (spline_value, spline_slope)


def block_weights(block_group):
    node_index = jnp.arange(WIN_DOWN * WIN_CROSS)
    node_row = (node_index // WIN_CROSS).astype(block_group.dtype)
    node_col = (node_index % WIN_CROSS).astype(block_group.dtype)
    down_value, down_slope = spline_pair(block_group[:, 0, :, None] - node_row)
    cross_value, cross_slope = spline_pair(block_group[:, 1, :, None] - node_col)
    return (down_value * cross_value, down_slope * cross_value, down_value * cross_slope)


def scatter_terms(block_group):
    weight, grad_down, grad_cross = block_weights(block_group)
    mass_value = block_group[:, 7]
    volume_value = block_group[:, 8]
    carried = jnp.stack(
        [mass_value, mass_value * block_group[:, 2], mass_value * block_group[:, 3]], axis=1
    )
    stress_down = jnp.stack(
        [-volume_value * block_group[:, 4], -volume_value * block_group[:, 5]], axis=1
    )
    stress_cross = jnp.stack(
        [-volume_value * block_group[:, 5], -volume_value * block_group[:, 6]], axis=1
    )
    lumped = jnp.einsum("bcp,bpn->bcn", carried, weight, precision=HIGHEST)
    force_sum = jnp.einsum("bcp,bpn->bcn", stress_down, grad_down, precision=HIGHEST)
    force_sum = force_sum + jnp.einsum("bcp,bpn->bcn", stress_cross, grad_cross, precision=HIGHEST)
    return jnp.concatenate([lumped, force_sum], axis=1)


def advance(block_group, particle_vel, along_down, along_cross):
    rate_dd = along_down[:, 0]
    rate_cc = along_cross[:, 1]
    rate_dc = 0.5 * (along_cross[:, 0] + along_down[:, 1])
    trace_rate = rate_dd + rate_cc
    shear_value = block_group[:, 9]
    lame_value = block_group[:, 10]
    stress_dd = block_group[:, 4] + TIME_STEP * (
        lame_value * trace_rate + 2.0 * shear_value * rate_dd
    )
    stress_dc = block_group[:, 5] + TIME_STEP * (2.0 * shear_value * rate_dc)
    stress_cc = block_group[:, 6] + TIME_STEP * (
        lame_value * trace_rate + 2.0 * shear_value * rate_cc
    )
    offset_down = jnp.clip(block_group[:, 0] + TIME_STEP * particle_vel[:, 0], 0.5, WIN_DOWN - 1.5)
    offset_cross = jnp.clip(
        block_group[:, 1] + TIME_STEP * particle_vel[:, 1], 0.5, WIN_CROSS - 1.5
    )
    volume_value = block_group[:, 8] * (1.0 + TIME_STEP * trace_rate)
    strain_value = block_group[:, 11] + TIME_STEP * (
        rate_dd * rate_dd + rate_cc * rate_cc + 2.0 * rate_dc * rate_dc
    )
    return jnp.stack(
        [
            offset_down,
            offset_cross,
            particle_vel[:, 0],
            particle_vel[:, 1],
            stress_dd,
            stress_dc,
            stress_cc,
            block_group[:, 7],
            volume_value,
            shear_value,
            lame_value,
            strain_value,
        ],
        axis=1,
    )


def gather_terms(block_group, window_vel):
    weight, grad_down, grad_cross = block_weights(block_group)
    particle_vel = jnp.einsum("bcn,bpn->bcp", window_vel, weight, precision=HIGHEST)
    along_down = jnp.einsum("bcn,bpn->bcp", window_vel, grad_down, precision=HIGHEST)
    along_cross = jnp.einsum("bcn,bpn->bcp", window_vel, grad_cross, precision=HIGHEST)
    return advance(block_group, particle_vel, along_down, along_cross)


def by_groups(block_task, particle_state, *extra_args):
    block_count = particle_state.shape[0]
    group_size = math.gcd(block_count, group_limit)
    packed = tuple(
        (
            member.reshape((block_count // group_size, group_size) + member.shape[1:])
            for member in (particle_state,) + extra_args
        )
    )

    def run_group(pieces):
        return block_task(*pieces)

    result = lax.map(run_group, packed)
    return result.reshape((block_count,) + result.shape[2:])


def node_velocity(node_sums, keep_mask):
    mass_sum = node_sums[0]
    moved_sum = jnp.stack(
        [
            node_sums[1] + TIME_STEP * (node_sums[3] + GRAVITY * mass_sum),
            node_sums[2] + TIME_STEP * node_sums[4],
        ]
    )
    return jnp.where(keep_mask, moved_sum / jnp.maximum(mass_sum, MASS_FLOOR), 0.0)


def inside_mask(row_global, col_global, total_rows, total_cols):
    keep_rows = (row_global > 0) & (row_global < total_rows - 1)
    keep_cols = (col_global > 0) & (col_global < total_cols - 1)
    return keep_rows[:, None] & keep_cols[None, :]


def settle(particle_state, slot_list, count_value, incoming):
    valid_mask = (jnp.arange(MOVE_CAP, dtype=jnp.int32) < count_value)[:, None, None]
    return particle_state.at[slot_list].set(
        jnp.where(valid_mask, incoming, particle_state[slot_list])
    )


def on_device(particles, anchor_down, anchor_cross, move_count, move_slots):
    particle_state = particles
    grid_width = TILE_CROSS + 2 * GHOST
    grid_height = TILE_DOWN + 2 * GHOST
    node_index = jnp.arange(WIN_DOWN * WIN_CROSS, dtype=jnp.int32)
    node_row = node_index // WIN_CROSS
    node_col = node_index % WIN_CROSS
    row_start = lax.axis_index("down") * TILE_DOWN
    col_start = lax.axis_index("cross") * TILE_CROSS
    total_rows = TILE_DOWN * lax.axis_size("down")
    total_cols = TILE_CROSS * lax.axis_size("cross")
    inner_rows = row_start + jnp.arange(TILE_DOWN, dtype=jnp.int32)
    inner_cols = col_start + jnp.arange(TILE_CROSS, dtype=jnp.int32)
    for step_index in range(STEPS):
        first_row = anchor_down[step_index][:, None] + GHOST + node_row[None, :]
        first_col = anchor_cross[step_index][:, None] + GHOST + node_col[None, :]
        flat_index = first_row * grid_width + first_col
        node_terms = by_groups(scatter_terms, particle_state)
        spread = jnp.transpose(node_terms, (1, 0, 2)).reshape(5, -1)
        node_sums = (
            jnp.zeros((5, grid_height * grid_width), jnp.float32)
            .at[:, flat_index.reshape(-1)]
            .add(spread)
        )
        node_sums = node_sums.reshape(5, grid_height, grid_width)
        rim_band = jnp.concatenate(
            [node_sums[:, :GHOST], node_sums[:, TILE_DOWN + GHOST :]], axis=1
        )
        rim_sums = padded(rim_band, (("down", 1),), GHOST)
        core_sums = node_sums[:, GHOST : GHOST + TILE_DOWN]
        core_sums = core_sums.at[:, :GHOST].add(rim_sums[:, :GHOST])
        core_sums = core_sums.at[:, TILE_DOWN - GHOST :].add(rim_sums[:, 3 * GHOST :])
        rim_band = jnp.concatenate(
            [core_sums[:, :, :GHOST], core_sums[:, :, TILE_CROSS + GHOST :]], axis=2
        )
        rim_sums = padded(rim_band, (("cross", 2),), GHOST)
        core_sums = core_sums[:, :, GHOST : GHOST + TILE_CROSS]
        core_sums = core_sums.at[:, :, :GHOST].add(rim_sums[:, :, :GHOST])
        core_sums = core_sums.at[:, :, TILE_CROSS - GHOST :].add(rim_sums[:, :, 3 * GHOST :])
        core_velocity = node_velocity(
            core_sums, inside_mask(inner_rows, inner_cols, total_rows, total_cols)
        )
        window_grid = padded(core_velocity, (("down", 1), ("cross", 2)), GHOST)
        window_vel = jnp.transpose(window_grid.reshape(2, -1)[:, flat_index], (1, 0, 2))
        particle_state = by_groups(gather_terms, particle_state, window_vel)
        slot_list = move_slots[step_index][:, :, 0, 0]
        count_list = move_count[step_index][:, 0, 0]
        outgoing = jnp.concatenate(
            [particle_state[slot_list[1]], particle_state[slot_list[0]]], axis=0
        )
        arrived = padded(outgoing, (("down", 0),), MOVE_CAP)
        particle_state = settle(particle_state, slot_list[1], count_list[1], arrived[:MOVE_CAP])
        particle_state = settle(
            particle_state, slot_list[0], count_list[0], arrived[3 * MOVE_CAP :]
        )
        outgoing = jnp.concatenate(
            [particle_state[slot_list[3]], particle_state[slot_list[2]]], axis=0
        )
        arrived = padded(outgoing, (("cross", 0),), MOVE_CAP)
        particle_state = settle(particle_state, slot_list[3], count_list[3], arrived[:MOVE_CAP])
        particle_state = settle(
            particle_state, slot_list[2], count_list[2], arrived[3 * MOVE_CAP :]
        )
    return particle_state


def solution(mesh):
    return jax.shard_map(
        on_device,
        mesh=mesh,
        in_specs=(
            P(("down", "cross"), None, None),
            P(None, ("down", "cross")),
            P(None, ("down", "cross")),
            P(None, None, "down", "cross"),
            P(None, None, None, "down", "cross"),
        ),
        out_specs=P(("down", "cross"), None, None),
        check_vma=False,
    )
```

profile of v0, /device:TPU:11, one launch (start us, length us, event | category | flops | bytes accessed | tf_op | source)
XLA Modules:
  0.0 713.7 jit_solution(9118341691291579690)
XLA Ops:
  1.0 61.5 %while.60 = (s32[]{:T(128)}, f32[16,8,5,128]{3,2,1,0:T(8,128)S(1)}, f32[16,8,12,128]{3,1,0,2:T(8,128)}, s32[]{:T(128)}) while((s32[]{:T(128)}, f32[16,8,5,128]{3,2,1,0:T(8,128)S(1)}, f32[16,8,12,128]{3,1,0,2:T(8,128)}, s32[]{:T(128)}) %tuple.241), condition=%wide.region_1.2_spmd, body=%wide.region_0.1_spmd.sunk | while | flops 20079360 | bytes 417853 | solution.py:139
  62.6 4.9 copy.110
  67.4 88.4 %scatter_custom_fusion = f32[5,6336]{0,1:T(8,128)S(1)} fusion(s32[16384]{0:T(1024)S(1)} %bitcast.269, f32[16384,5]{1,0:T(8,128)} %bitcast.220, f32[]{:T(128)} %constant.678.clone.1), kind=kCustom, calls=%fused_computation.511 | custom fusion | flops 81920 | bytes 127232 | tf_op jit(solution)/shard_map/scatter-add | solution.py:189
  157.1 1.9 copy.150
  159.0 3.7 collective-permute-start
  162.7 1.3 copy.151
  164.0 1.9 collective-permute-start.1
  169.9 1.5 slice.904
  171.4 1.3 copy.149
  172.7 2.5 copy.148
  178.3 4.0 collective-permute-start.3
  184.4 4.8 collective-permute-start.4
  189.2 1.9 collective-permute-start.5
  191.8 2.3 collective-permute-done.5
  195.5 4.2 collective-permute-start.7
  200.5 1.8 copy.115
  202.4 54.8 %gather_fusion = f32[16384,2]{1,0:T(8,128)} fusion(f32[2,6336]{0,1:T(8,128)S(1)} %bitcast.222, s32[16384]{0:T(1024)S(1)} %get-tuple-element.538), kind=kCustom, calls=%fused_computation | custom fusion | bytes 327680 | tf_op jit(solution)/shard_map/gather | solution.py:210
  257.2 5.6 copy.116
  262.7 78.5 %while.61 = (s32[]{:T(128)}, f32[16,8,12,128]{3,1,0,2:T(8,128)S(1)}, f32[16,8,12,128]{3,1,0,2:T(8,128)}, f32[16,8,2,128]{3,2,1,0:T(2,128)S(1)}, s32[]{:T(128)}) while((s32[]{:T(128)}, f32[16,8,12,128]{3,1,0,2:T(8,128)S(1)}, f32[16,8,12,128]{3,1,0,2:T(8,128)}, f32[16,8,2,128]{3,2,1,0:T(2,128)S(1)}, s32[]{:T(128)}) %tuple.244), condition=%wide.region_4.5_spmd, body=%wide.region_3.4_spmd.sunk | while | flops 18522880 | bytes 516177 | solution.py:139
  342.5 3.2 collective-permute-start.8
  347.0 2.5 collective-permute-start.9
  351.3 2.2 collective-permute-done.9
  357.8 4.0 collective-permute-start.11
  364.8 48.7 %while.62 = (s32[]{:T(128)}, f32[16,8,5,128]{3,2,1,0:T(8,128)S(1)}, f32[16,8,12,128]{3,2,1,0:T(8,128)S(1)}, s32[]{:T(128)}) while((s32[]{:T(128)}, f32[16,8,5,128]{3,2,1,0:T(8,128)S(1)}, f32[16,8,12,128]{3,2,1,0:T(8,128)S(1)}, s32[]{:T(128)}) %tuple.238), condition=%wide.region_10.11_spmd, body=%wide.region_9.10_spmd.sunk | while | flops 20079360 | bytes 319549 | solution.py:139
  413.5 4.9 copy.124
  418.3 88.6 %scatter_custom_fusion.5 = f32[5,6336]{0,1:T(8,128)S(1)} fusion(s32[16384]{0:T(1024)S(1)} %bitcast.268, f32[16384,5]{1,0:T(8,128)} %bitcast.219, f32[]{:T(128)} %constant.678.clone.1), kind=kCustom, calls=%fused_computation.509 | custom fusion | flops 81920 | bytes 127232 | tf_op jit(solution)/shard_map/scatter-add | solution.py:189
  508.2 1.3 copy.154
  509.5 2.9 collective-permute-start.12
  512.4 1.5 slice.923
  513.9 2.6 copy.152
  516.5 1.3 copy.153
  517.8 1.3 copy.155
  519.1 3.0 collective-permute-start.13
  522.1 3.3 collective-permute-done.13
  527.0 4.0 collective-permute-start.15
  533.0 3.1 collective-permute-start.16
  536.2 2.7 collective-permute-start.17
  539.5 2.3 collective-permute-done.17
  543.2 4.0 collective-permute-start.19
  549.1 1.8 copy.129
  550.9 54.8 %gather_fusion.7 = f32[16384,2]{1,0:T(8,128)} fusion(f32[2,6336]{0,1:T(8,128)S(1)} %bitcast.221, s32[16384]{0:T(1024)S(1)} %get-tuple-element.537), kind=kCustom, calls=%fused_computation.7 | custom fusion | bytes 327680 | tf_op jit(solution)/shard_map/gather | solution.py:210
  605.7 5.6 copy.130
  611.3 78.5 %while.63 = (s32[]{:T(128)}, f32[16,8,12,128]{3,1,2,0:T(8,128)S(1)}, f32[16,8,12,128]{3,1,2,0:T(8,128)}, f32[16,8,2,128]{3,2,1,0:T(2,128)S(1)}, s32[]{:T(128)}) while((s32[]{:T(128)}, f32[16,8,12,128]{3,1,2,0:T(8,128)S(1)}, f32[16,8,12,128]{3,1,2,0:T(8,128)}, f32[16,8,2,128]{3,2,1,0:T(2,128)S(1)}, s32[]{:T(128)}) %tuple.243), condition=%wide.region_13.14_spmd, body=%wide.region_12.13_spmd.sunk | while | flops 18522880 | bytes 516177 | solution.py:139
  690.6 2.9 collective-permute-start.20
  694.6 2.5 collective-permute-start.21
  698.8 2.9 collective-permute-done.21
  703.3 1.3 collective-permute-start.22
  705.8 4.0 collective-permute-start.23
  (1037 shorter events, 306.8 us)
Async XLA Ops:
  67.4 98.7 %copy-start.19 = (s32[2,4,13,1,1]{2,4,3,1,0:T(1,128)S(1)}, s32[2,4,13,1,1]{2,4,3,1,0:T(1,128)}, u32[]{:S(2)}) copy-start(s32[2,4,13,1,1]{2,4,3,1,0:T(1,128)} %param.33) | copy-start | bytes 1252
  67.4 100.4 %copy-start.4 = (s32[2,4,1,1]{1,3,2,0:T(1,128)S(1)}, s32[2,4,1,1]{1,3,2,0:T(1,128)}, u32[]{:S(2)}) copy-start(s32[2,4,1,1]{1,3,2,0:T(1,128)} %param.32) | copy-start | bytes 100
  159.0 16.3 %collective-permute-start = (f32[5,4,264]{2,1,0:T(4,128)}, f32[5,4,264]{2,1,0:T(4,128)}, u32[]{:S(2)}, u32[]{:S(2)}) collective-permute-start(f32[5,4,264]{2,1,0:T(4,128)} %copy.150), channel_id=1, source_target_pairs={{0,2},{2,4},{4,6},{6,8},{8,10},{10,12},{12,14},{14,16},{16,18},{18... | collective-permute-start | bytes 63368 | tf_op jit(solution)/shard_map/ppermute | solution.py:31
  164.0 12.1 %collective-permute-start.1 = (f32[5,4,264]{2,1,0:T(4,128)S(1)}, f32[5,4,264]{2,1,0:T(4,128)}, u32[]{:S(2)}, u32[]{:S(2)}) collective-permute-start(f32[5,4,264]{2,1,0:T(4,128)S(1)} %copy.151), channel_id=1, source_target_pairs={{2,0},{4,2},{6,4},{8,6},{10,8},{12,10},{14,12},{16,14},{18,16},{20... | collective-permute-start | bytes 63368 | tf_op jit(solution)/shard_map/ppermute | solution.py:32
  166.6 3.1 copy-start.11
  166.6 3.1 copy-start.13
  166.6 3.1 copy-start.15
  166.7 3.1 copy-start.17
  166.7 8.6 %copy-start.7 = (s32[13]{0:T(128)}, s32[13]{0:T(128)S(1)}, u32[]{:S(2)}) copy-start(s32[13]{0:T(128)S(1)} %get-tuple-element.522) | copy-start | bytes 160
  166.7 11.5 %copy-start.9 = (s32[13]{0:T(128)}, s32[13]{0:T(128)S(1)}, u32[]{:S(2)}) copy-start(s32[13]{0:T(128)S(1)} %get-tuple-element.523) | copy-start | bytes 160
  176.9 5.4 collective-permute-start.2
  178.3 5.1 collective-permute-start.3
  184.4 7.4 %collective-permute-start.4 = (f32[2,4,256]{2,1,0:T(4,128)S(1)}, f32[2,4,256]{2,1,0:T(4,128)S(1)}, u32[]{:S(2)}, u32[]{:S(2)}) collective-permute-start(f32[2,4,256]{2,1,0:T(4,128)S(1)} %get-tuple-element.519), channel_id=1, source_target_pairs={{0,2},{2,4},{4,6},{6,8},{8,10},{10,12},{12,14},{14,16},{16,18},{18... | collective-permute-start | bytes 24584 | tf_op jit(solution)/shard_map/ppermute | solution.py:31
  189.2 5.0 collective-permute-start.5
  194.2 6.1 collective-permute-start.6
  195.5 4.9 collective-permute-start.7
  257.2 5.6 copy-start.3
  262.7 86.9 %copy-start.18 = (s32[13]{0:T(128)S(1)}, s32[13]{0:T(128)}, u32[]{:S(2)}) copy-start(s32[13]{0:T(128)} %copy-done.17) | copy-start | bytes 160
  341.3 12.3 %copy-start.16 = (s32[13]{0:T(128)S(1)}, s32[13]{0:T(128)}, u32[]{:S(2)}) copy-start(s32[13]{0:T(128)} %copy-done.15) | copy-start | bytes 160
  341.3 20.7 %copy-start.14 = (s32[13]{0:T(128)S(1)}, s32[13]{0:T(128)}, u32[]{:S(2)}) copy-start(s32[13]{0:T(128)} %copy-done.13) | copy-start | bytes 160
  341.3 22.4 %copy-start.12 = (s32[13]{0:T(128)S(1)}, s32[13]{0:T(128)}, u32[]{:S(2)}) copy-start(s32[13]{0:T(128)} %copy-done.11) | copy-start | bytes 160
  342.5 7.0 collective-permute-start.8
  347.0 6.5 collective-permute-start.9
  355.2 6.6 collective-permute-start.10
  357.8 5.8 collective-permute-start.11
  413.4 4.9 copy-start
  418.3 94.0 %copy-start.5 = (s32[13]{0:T(128)S(1)}, s32[13]{0:T(128)}, u32[]{:S(2)}) copy-start(s32[13]{0:T(128)} %get-tuple-element.521) | copy-start | bytes 160
  509.5 12.6 %collective-permute-start.12 = (f32[5,4,264]{2,1,0:T(4,128)S(1)}, f32[5,4,264]{2,1,0:T(4,128)S(1)}, u32[]{:S(2)}, u32[]{:S(2)}) collective-permute-start(f32[5,4,264]{2,1,0:T(4,128)S(1)} %copy.154), channel_id=1, source_target_pairs={{0,2},{2,4},{4,6},{6,8},{8,10},{10,12},{12,14},{14,16},{16,18},{18... | collective-permute-start | bytes 63368 | tf_op jit(solution)/shard_map/ppermute | solution.py:31
  512.4 14.5 %copy-start.6 = (s32[13]{0:T(128)S(1)}, s32[13]{0:T(128)}, u32[]{:S(2)}) copy-start(s32[13]{0:T(128)} %get-tuple-element.528) | copy-start | bytes 160
  513.9 34.0 %copy-start.1 = (f32[16,8,12,128]{3,2,1,0:T(8,128)S(1)}, f32[16,8,12,128]{3,2,1,0:T(8,128)}, u32[]{:S(2)}) copy-start(f32[16,8,12,128]{3,2,1,0:T(8,128)} %copy-done) | copy-start | bytes 2359300
  519.1 6.3 collective-permute-start.13
  525.6 5.4 collective-permute-start.14
  527.0 5.1 collective-permute-start.15
  533.0 6.5 collective-permute-start.16
  536.2 5.7 collective-permute-start.17
  541.9 7.1 collective-permute-start.18
  543.2 5.8 collective-permute-start.19
  605.7 5.6 copy-start.2
  611.3 86.0 %copy-start.10 = (s32[13]{0:T(128)S(1)}, s32[13]{0:T(128)}, u32[]{:S(2)}) copy-start(s32[13]{0:T(128)} %copy-done.9) | copy-start | bytes 160
  689.8 11.9 %copy-start.8 = (s32[13]{0:T(128)S(1)}, s32[13]{0:T(128)}, u32[]{:S(2)}) copy-start(s32[13]{0:T(128)} %copy-done.7) | copy-start | bytes 160
  690.6 6.6 collective-permute-start.20
  694.6 7.0 collective-permute-start.21
  703.3 6.5 collective-permute-start.22
  705.8 5.7 collective-permute-start.23
where the time goes:
time: 721 us; the launch traced here: 714 us
  matrix products  217 us (30%)
  local copies, waits for them, and re-layouts  216 us (30%)
  other arithmetic  193 us (27%)
  starting transfers between devices  66.8 us (9%)
  waiting for transfers between devices  14.5 us (2%)
    scatter-add x2, other arithmetic, on_device(): node_sums = jnp.zeros((5, grid_height * grid_width), jnp.float32).at[:, f...  177 us
    gather x2, local copies, waits for them, and re-layouts, on_device(): window_grid.reshape(2, -1)[:, flat_index]  110 us
    dot_general x32, matrix products, gather_terms(): jnp.einsum('bcn,bpn->bcp', window_vel, grad_down, precision=HIGHEST)  41.3 us
    dot_general x32, matrix products, gather_terms(): jnp.einsum('bcn,bpn->bcp', window_vel, grad_cross, precision=HIGHEST)  41.3 us
    dot_general x32, matrix products, gather_terms(): jnp.einsum('bcn,bpn->bcp', window_vel, weight, precision=HIGHEST)  41.1 us
    ppermute x12, starting transfers between devices, padded(): after = lax.ppermute(initial, axis, down)  38.6 us
    dot_general x32, matrix products, scatter_terms(): jnp.einsum('bcp,bpn->bcn', stress_cross, grad_cross, precision=HIGHEST)  31.4 us
    dot_general x32, matrix products, scatter_terms(): jnp.einsum('bcp,bpn->bcn', stress_down, grad_down, precision=HIGHEST)  31.3 us
  transfers between devices with their start and end apart: 24, of which 9 were waited for; matrix products, arithmetic and copies ran while one was open for 5% of the time, Pallas kernels for 0%

commit v1 on v0

v1 whole, which is shorter than its diff:
```python
import functools

import jax
import jax.numpy as jnp
from jax import lax
from jax.experimental import pallas as pl
from jax.experimental.pallas import tpu as pltpu
from jax.sharding import PartitionSpec as P

WIN_DOWN = 8
WIN_CROSS = 16
GHOST = 4
STEPS = 2
TILE_DOWN = 16
TILE_CROSS = 256
TIME_STEP = 0.1
GRAVITY = 5.6
MASS_FLOOR = 0.5
LANES = 128
CHANNELS = 3
STRIDE = 32
BAND = 2 * GHOST
UNROLL = 4


def spline_pair(distance):
    near = jnp.clip(distance, -0.5, 0.5)
    far = jnp.clip(distance - near, -1.0, 1.0)
    twice = near + near
    slope = far - twice
    return slope * slope + (1.5 - 1.5 * twice * twice), slope


def low_part(x):
    return x - x.astype(jnp.bfloat16).astype(jnp.float32)


def node_rows(count):
    return lax.broadcasted_iota(jnp.int32, (count, LANES), 0).astype(jnp.float32)


def cross_weights(w, cols):
    value, slope = spline_pair(w - cols)
    both = jnp.concatenate([value, slope], axis=1)
    high = both.astype(jnp.bfloat16)
    low = (both - high.astype(jnp.float32)).astype(jnp.bfloat16)
    return jnp.concatenate([high, low], axis=0)


def scatter_block(state, sums, b, first_row, first_col, rows, cols, keep):
    u, w, vd, vc = (state[b, f : f + 1, :] for f in range(4))
    sdd, sdc, scc, mass, vol = (state[b, f : f + 1, :] for f in range(4, 9))
    value, slope = spline_pair(u - rows)
    quarter = 0.25 * mass
    push = (-0.5 * TIME_STEP) * vol
    push_dc = push * sdc
    zero = jnp.zeros_like(value)
    parts = (
        (quarter * value, zero),
        (quarter * (vd + TIME_STEP * GRAVITY) * value + (push * sdd) * slope, push_dc * value),
        (quarter * vc * value + push_dc * slope, (push * scc) * value),
    )
    gap = jnp.zeros((16, 2 * LANES), jnp.bfloat16)
    pieces = []
    for along, across in parts:
        both = jnp.concatenate([along, across], axis=1)
        pieces += [jnp.concatenate([both, low_part(both)], axis=0).astype(jnp.bfloat16), gap]
    loads = jnp.concatenate(pieces, axis=0)
    found = lax.dot_general(
        cross_weights(w, cols), loads, (((1,), (1,)), ((), ())), preferred_element_type=jnp.float32
    )
    found = found[:WIN_CROSS] + found[WIN_CROSS:]
    found = jnp.concatenate(
        [found, jnp.zeros((WIN_CROSS, LANES - CHANNELS * STRIDE), jnp.float32)], axis=1
    )
    found = jnp.where(keep, found + pltpu.roll(found, LANES - WIN_DOWN, 1), 0.0)
    found = pltpu.roll(found, first_row, 1)
    spot = pl.ds(first_col, WIN_CROSS)
    sums[spot, :] = sums[spot, :] + found


def scatter_all(state, sums, anchor_down, anchor_cross, step, blocks):
    sums[...] = jnp.zeros_like(sums)
    rows = node_rows(WIN_DOWN)
    cols = node_rows(WIN_CROSS)
    lane = lax.broadcasted_iota(jnp.int32, (WIN_CROSS, LANES), 1)
    keep = (lane & (STRIDE - 1)) < WIN_DOWN

    def several(q, carry):
        for k in range(UNROLL):
            b = q * UNROLL + k
            scatter_block(
                state,
                sums,
                b,
                anchor_down[step, b] + GHOST,
                anchor_cross[step, b] + GHOST,
                rows,
                cols,
                keep,
            )
        return carry

    lax.fori_loop(0, blocks // UNROLL, several, 0)


def write_grid(sums, grid, pay, height, tiles):
    for t in range(tiles):
        turned = jnp.transpose(sums[t * LANES : (t + 1) * LANES, :])
        for c in range(CHANNELS):
            grid[t, c * height : (c + 1) * height, :] = turned[c * STRIDE : c * STRIDE + height]
    odd = lax.rem(lax.axis_index("down"), 2)
    for t in range(tiles):
        for c in range(CHANNELS):
            last = grid[t, (c + 1) * height - BAND : (c + 1) * height, :]
            first = grid[t, c * height : c * height + BAND, :]
            pay[odd, t, c * BAND : (c + 1) * BAND, :] = last
            pay[1 - odd, t, c * BAND : (c + 1) * BAND, :] = first


def first_kernel(step, anchor_down, anchor_cross, state, grid, pay, sums):
    blocks = state.shape[0]
    tiles = grid.shape[0]
    scatter_all(state, sums, anchor_down, anchor_cross, step, blocks)
    write_grid(sums, grid, pay, grid.shape[1] // CHANNELS, tiles)


def settle(state, arrived, slots, counts, step, cross_links):
    cap = slots.shape[2]
    for link in range(2 + cross_links):
        side = link_side(link)
        count = counts[step, side]

        def put(m, carry, link=link, side=side):
            state[slots[step, side, m]] = arrived[link][m]
            return carry

        lax.fori_loop(0, count, put, 0)


def link_side(link):
    axis, second = divmod(link, 2)
    odd = lax.rem(lax.axis_index(("down", "cross")[axis]), 2)
    return 2 * axis + (1 - odd if second else odd)


def next_kernel(step, cross_links, anchor_down, anchor_cross, slots, counts, old, *rest):
    arrived = rest[: 2 + cross_links]
    state, grid, pay, sums = rest[2 + cross_links :]
    state[...] = old[...]
    settle(state, arrived, slots, counts, step - 1, cross_links)
    blocks = state.shape[0]
    scatter_all(state, sums, anchor_down, anchor_cross, step, blocks)
    write_grid(sums, grid, pay, grid.shape[1] // CHANNELS, grid.shape[0])


def last_kernel(step, cross_links, slots, counts, old, *rest):
    arrived = rest[: 2 + cross_links]
    state = rest[2 + cross_links]
    state[...] = old[...]
    settle(state, arrived, slots, counts, step, cross_links)


def add_bands(total, bands, height, tiles):
    odd = lax.rem(lax.axis_index("down"), 2)
    for t in range(tiles):
        for c in range(CHANNELS):
            for link in range(2):
                band = bands[link][t, c * BAND : (c + 1) * BAND, :]
                at_first = odd if link == 0 else 1 - odd
                start = c * height + (1 - at_first) * (height - BAND)
                spot = pl.ds(pl.multiple_of(start, 8), BAND)
                total[t, spot, :] = total[t, spot, :] + band


def cross_kernel(width, grid, band0, band1, total, pay):
    tiles, rows, _ = grid.shape
    height = rows // CHANNELS
    total[...] = grid[...]
    add_bands(total, (band0, band1), height, tiles)
    odd = lax.rem(lax.axis_index("cross"), 2)
    start = width - BAND
    tile, lane = divmod(start, LANES)
    last = pltpu.roll(total[tile], LANES - lane, 1) if lane else total[tile]
    pay[odd] = last
    pay[1 - odd] = total[0]


def node_velocity(total, bands, cross_links, speed, width):
    tiles, rows, _ = total.shape
    height = rows // CHANNELS
    odd = lax.rem(lax.axis_index("cross"), 2)
    col = lax.broadcasted_iota(jnp.int32, (rows, LANES), 1)
    start = width - BAND
    tile, lane = divmod(start, LANES)
    for link in range(cross_links):
        band = jnp.where(col < BAND, bands[link][...], 0.0)
        at_first = odd if link == 0 else 1 - odd
        total[0] = total[0] + jnp.where(at_first == 1, band, 0.0)
        shifted = pltpu.roll(band, lane, 1) if lane else band
        total[tile] = total[tile] + jnp.where(at_first == 0, shifted, 0.0)
    tile_down = height - 2 * GHOST
    tile_cross = width - 2 * GHOST
    row_global = (
        lax.broadcasted_iota(jnp.int32, (height, LANES), 0)
        + lax.axis_index("down") * tile_down
        - GHOST
    )
    col_first = lax.broadcasted_iota(jnp.int32, (height, LANES), 1) - GHOST
    total_rows = tile_down * lax.axis_size("down")
    total_cols = tile_cross * lax.axis_size("cross")
    keep_rows = (row_global > 0) & (row_global < total_rows - 1)
    for t in range(tiles):
        col_global = col_first + (lax.axis_index("cross") * tile_cross + t * LANES)
        kept = keep_rows & (col_global > 0) & (col_global < total_cols - 1)
        mass = jnp.maximum(total[t, :height, :], MASS_FLOOR)
        for c in range(2):
            value = total[t, (c + 1) * height : (c + 2) * height, :] / mass
            speed[t, c] = jnp.where(kept, value, 0.0)


def gather_block(state, speed, b, first_row, first_col, rows, cols, lane):
    tile = first_col // LANES
    shift = first_col - tile * LANES
    spot = pl.ds(first_row, WIN_DOWN)
    here = jnp.concatenate([speed[tile, 0, spot, :], speed[tile, 1, spot, :]], axis=0)
    after = jnp.concatenate([speed[tile + 1, 0, spot, :], speed[tile + 1, 1, spot, :]], axis=0)
    window = jnp.where(lane >= shift, here, after)
    window = jnp.where(
        lane < WIN_CROSS,
        pltpu.roll(window, (LANES - shift) & (LANES - 1), 1),
        pltpu.roll(window, (WIN_CROSS + LANES - shift) & (LANES - 1), 1),
    )
    window = jnp.concatenate([window, low_part(window)], axis=0).astype(jnp.bfloat16)
    field = [state[b, f : f + 1, :] for f in range(12)]
    found = jnp.dot(
        window[:, : 2 * WIN_CROSS],
        cross_weights(field[1], cols),
        preferred_element_type=jnp.float32,
    )
    found = found[: 2 * WIN_DOWN] + found[2 * WIN_DOWN :]
    value, slope = spline_pair(field[0] - rows)

    def summed(weight, terms, scale):
        return scale * jnp.sum(weight * terms, axis=0, keepdims=True)

    along = found[:, :LANES]
    across = found[:, LANES:]
    vel_d = summed(value, along[:WIN_DOWN], 0.25)
    vel_c = summed(value, along[WIN_DOWN:], 0.25)
    l_dd = summed(slope, along[:WIN_DOWN], 0.5)
    l_cd = summed(slope, along[WIN_DOWN:], 0.5)
    l_dc = summed(value, across[:WIN_DOWN], 0.5)
    l_cc = summed(value, across[WIN_DOWN:], 0.5)
    rate_dc = 0.5 * (l_dc + l_cd)
    trace = l_dd + l_cc
    shear, lame = field[9], field[10]
    spread = lame * trace
    return [
        jnp.clip(field[0] + TIME_STEP * vel_d, 0.5, WIN_DOWN - 1.5),
        jnp.clip(field[1] + TIME_STEP * vel_c, 0.5, WIN_CROSS - 1.5),
        vel_d,
        vel_c,
        field[4] + TIME_STEP * (spread + 2.0 * shear * l_dd),
        field[5] + TIME_STEP * (2.0 * shear * rate_dc),
        field[6] + TIME_STEP * (spread + 2.0 * shear * l_cc),
        field[7],
        field[8] * (1.0 + TIME_STEP * trace),
        shear,
        lame,
        field[11] + TIME_STEP * (l_dd * l_dd + l_cc * l_cc + 2.0 * rate_dc * rate_dc),
    ]


def gather_kernel(step, cross_links, width, anchor_down, anchor_cross, slots, *rest):
    state, total = rest[:2]
    bands = rest[2 : 2 + cross_links]
    moved = rest[2 + cross_links]
    sent = rest[3 + cross_links : 5 + 2 * cross_links]
    speed, sums = rest[5 + 2 * cross_links :]
    blocks = state.shape[0]
    sums[...] = total[...]
    node_velocity(sums, bands, cross_links, speed, width)
    rows = node_rows(WIN_DOWN)
    cols = node_rows(WIN_CROSS)
    lane = lax.broadcasted_iota(jnp.int32, (2 * WIN_DOWN, LANES), 1)

    def several(q, carry):
        for k in range(UNROLL):
            b = q * UNROLL + k
            out = gather_block(
                state,
                speed,
                b,
                anchor_down[step, b] + GHOST,
                anchor_cross[step, b] + GHOST,
                rows,
                cols,
                lane,
            )
            for f in range(12):
                moved[b, f : f + 1, :] = out[f]
        return carry

    lax.fori_loop(0, blocks // UNROLL, several, 0)
    cap = slots.shape[2]
    for link in range(2 + cross_links):
        side = link_side(link)

        def take(m, carry, link=link, side=side):
            sent[link][m] = moved[slots[step, side, m]]
            return carry

        lax.fori_loop(0, cap, take, 0)


def swap_pairs(size, first):
    pairs = []
    for i in range(first, size - 1, 2):
        pairs += [(i, i + 1), (i + 1, i)]
    return pairs


def solution(mesh):
    size_down, size_cross = mesh.shape["down"], mesh.shape["cross"]
    cross_links = 1 if size_cross <= 2 else 2
    smem = pl.BlockSpec(memory_space=pltpu.SMEM)
    vmem = pl.BlockSpec(memory_space=pltpu.VMEM)
    params = pltpu.CompilerParams(vmem_limit_bytes=40 * 1024 * 1024)
    f32 = jnp.float32

    def swap(x, link):
        axis, second = divmod(link, 2)
        name, size = (("down", size_down), ("cross", size_cross))[axis]
        return lax.ppermute(x, name, swap_pairs(size, second))

    def on_device(particles, anchor_down, anchor_cross, move_count, move_slots):
        blocks = particles.shape[0]
        cap = move_slots.shape[2]
        slots = move_slots.reshape(STEPS, 4, cap)
        counts = move_count.reshape(STEPS, 4)
        height = TILE_DOWN + 2 * GHOST
        width = TILE_CROSS + 2 * GHOST
        tiles = -(-width // LANES)
        grid_type = jax.ShapeDtypeStruct((tiles, CHANNELS * height, LANES), f32)
        band_type = jax.ShapeDtypeStruct((2, tiles, CHANNELS * BAND, LANES), f32)
        state_type = jax.ShapeDtypeStruct(particles.shape, f32)
        sent_type = jax.ShapeDtypeStruct((cap,) + particles.shape[1:], f32)
        sums_scratch = pltpu.VMEM((tiles * LANES, LANES), f32)
        state = particles
        for step in range(STEPS):
            if step == 0:
                grid, pay = pl.pallas_call(
                    functools.partial(first_kernel, step),
                    out_shape=(grid_type, band_type),
                    in_specs=[smem, smem, vmem],
                    out_specs=(vmem, vmem),
                    scratch_shapes=[sums_scratch],
                    compiler_params=params,
                    name="scatter_first",
                )(anchor_down, anchor_cross, state)
            else:
                state, grid, pay = pl.pallas_call(
                    functools.partial(next_kernel, step, cross_links),
                    out_shape=(state_type, grid_type, band_type),
                    in_specs=[smem] * 4 + [vmem] * (3 + cross_links),
                    out_specs=(vmem, vmem, vmem),
                    scratch_shapes=[sums_scratch],
                    compiler_params=params,
                    name="scatter_next",
                )(anchor_down, anchor_cross, slots, counts, state, *arrived)
            band0 = swap(pay[0], 0)
            band1 = swap(pay[1], 1)
            total, pay = pl.pallas_call(
                functools.partial(cross_kernel, width),
                out_shape=(
                    grid_type,
                    jax.ShapeDtypeStruct((2, CHANNELS * height, LANES), f32),
                ),
                in_specs=[vmem] * 3,
                out_specs=(vmem, vmem),
                compiler_params=params,
                name="add_down",
            )(grid, band0, band1)
            bands = [swap(pay[k], 2 + k) for k in range(cross_links)]
            state, *sent = pl.pallas_call(
                functools.partial(gather_kernel, step, cross_links, width),
                out_shape=(state_type,) + (sent_type,) * (2 + cross_links),
                in_specs=[smem] * 3 + [vmem] * (2 + cross_links),
                out_specs=(vmem,) * (3 + cross_links),
                scratch_shapes=[
                    pltpu.VMEM((tiles, 2, height, LANES), f32),
                    pltpu.VMEM(grid_type.shape, f32),
                ],
                compiler_params=params,
                name="gather",
            )(anchor_down, anchor_cross, slots, state, total, *bands)
            arrived = [swap(sent[k], k) for k in range(2 + cross_links)]
        return pl.pallas_call(
            functools.partial(last_kernel, STEPS - 1, cross_links),
            out_shape=state_type,
            in_specs=[smem] * 2 + [vmem] * (3 + cross_links),
            out_specs=vmem,
            compiler_params=params,
            name="settle_last",
        )(slots, counts, state, *arrived)

    return jax.shard_map(
        on_device,
        mesh=mesh,
        in_specs=(
            P(("down", "cross"), None, None),
            P(None, ("down", "cross")),
            P(None, ("down", "cross")),
            P(None, None, "down", "cross"),
            P(None, None, None, "down", "cross"),
        ),
        out_specs=P(("down", "cross"), None, None),
        check_vma=False,
    )
```

time: 721 us -> 82.9 us (0.11)
  matrix products: 217 us -> 0 us
  local copies, waits for them, and re-layouts: 216 us -> 3.47 us
  other arithmetic: 193 us -> 0 us
  starting transfers between devices: 66.8 us -> 18.6 us
  Pallas kernels: 0 us -> 42 us
    dot_general x192 -> x0, matrix products: 217 us -> none  [the longest x32 41.3 us: gather_terms(): jnp.einsum('bcn,bpn->bcp', window_vel, grad_down, precision=HIGHEST)]
    scatter-add x6 -> x0, other arithmetic: 179 us -> none  [the longest x2 177 us: on_device(): node_sums = jnp.zeros((5, grid_height * grid_width), jnp.float32).at[:, f...]
    gather x14 -> x0, local copies, waits for them, and re-layouts: 117 us -> none  [the longest x2 110 us: on_device(): window_grid.reshape(2, -1)[:, flat_index]]
    ppermute x24 -> x12, starting transfers between devices: 66.8 us -> 18.6 us  [swap(): return lax.ppermute(x, name, swap_pairs(size, second))]
    pallas_call x0 -> x7, Pallas kernels: none -> 42 us  [the longest x2 18.5 us: on_device(): pl.pallas_call(functools.partial(gather_kernel, step, cross_links, width)...]
    squeeze x48 -> x4, local copies, waits for them, and re-layouts: 26 us -> 0.02 us  [the longest x2 0.01 us: on_device(): band1 = swap(pay[1], 1)]
    transpose x4 -> x0, local copies, waits for them, and re-layouts: 20.9 us -> none  [the longest x2 11.1 us: on_device(): jnp.transpose(window_grid.reshape(2, -1)[:, flat_index], (1, 0, 2))]
    dynamic_slice x32 -> x0, local copies, waits for them, and re-layouts: 13.1 us -> none  [by_groups(): result = lax.map(run_group, packed)]
  transfers between devices with their start and end apart: 24 -> 12, of which waited for: 9 -> 6; matrix products, arithmetic and copies ran while one was open for 5% -> 0% of each run, Pallas kernels for 0% -> 0%
where the time goes in v1:
time: 82.9 us; the launch traced here: 81.7 us
  Pallas kernels  42 us (51%)
  starting transfers between devices  18.6 us (22%)
  waiting for transfers between devices  17.5 us (21%)
  local copies, waits for them, and re-layouts  3.47 us (4%)
    ppermute x12, starting transfers between devices, swap(): return lax.ppermute(x, name, swap_pairs(size, second))  18.6 us
    pallas_call x2, Pallas kernels, on_device(): pl.pallas_call(functools.partial(gather_kernel, step, cross_links, width)...  18.5 us
    ppermute x12, waiting for transfers between devices, swap(): return lax.ppermute(x, name, swap_pairs(size, second))  17.5 us
    pallas_call x1, Pallas kernels, on_device(): pl.pallas_call(functools.partial(next_kernel, step, cross_links), out_sha...  11.4 us
    pallas_call x1, Pallas kernels, on_device(): pl.pallas_call(functools.partial(first_kernel, step), out_shape=(grid_typ...  11.1 us
    unnamed x9, local copies, waits for them, and re-layouts  2.33 us
  transfers between devices with their start and end apart: 12, of which 6 were waited for; matrix products, arithmetic and copies ran while one was open for 0% of the time, Pallas kernels for 0%

profile of v1, /device:TPU:11, one launch (start us, length us, event | category | flops | bytes accessed | tf_op | source)
XLA Modules:
  0.0 81.7 jit_solution(14992007914344775111)
XLA Ops:
  0.0 0.0 copy-start.2
  0.0 0.0 copy-start.1
  0.0 1.6 %copy.7.state.rest_0_ = f32[128,12,128]{2,1,0:T(8,128)S(1)} copy(f32[128,12,128]{2,0,1:T(8,128)} %param.5) | data formatting | bytes 1572864 | tf_op args[0]
  1.6 0.0 copy-done.2
  1.7 0.0 copy-done.1
  1.7 11.1 %scatter_first.1 = (f32[3,72,128]{2,1,0:T(8,128)S(1)}, f32[2,3,24,128]{3,2,1,0:T(8,128)S(1)}) custom-call(s32[2,128]{1,0:T(2,128)S(1)} %copy-done.1, s32[2,128]{1,0:T(2,128)S(1)} %copy-done.2, f32[128,12,128]{2,1,0:T(8,128)S(1)} %copy.7.state.rest_0_), custom_call_target="tpu_custom_call" | custom-call | tf_op jit(solution)/shard_map/scatter_first/pallas_call | solution.py:353
  12.8 3.7 %collective-permute-start.1 = (f32[3,24,128]{2,1,0:T(8,128)S(1)}, f32[3,24,128]{2,1,0:T(8,128)S(1)}, u32[]{:S(2)}, u32[]{:S(2)}) collective-permute-start(f32[3,24,128]{2,1,0:T(8,128)S(1)} %get-tuple-element.41), channel_id=1, source_target_pairs={{2,4},{4,2},{6,8},{8,6},{10,12},{12,10},{14,16},{16,14},{18,20},{2... | collective-permute-start | bytes 110600 | tf_op jit(solution)/shard_map/ppermute | solution.py:335
  16.5 0.1 collective-permute-start
  16.6 1.5 %collective-permute-done.1.band1 = f32[3,24,128]{2,1,0:T(8,128)S(1)} collective-permute-done((f32[3,24,128]{2,1,0:T(8,128)S(1)}, f32[3,24,128]{2,1,0:T(8,128)S(1)}, u32[]{:S(2)}, u32[]{:S(2)}) %collective-permute-start.1) | collective-permute-done | bytes 36896 | tf_op jit(solution)/shard_map/ppermute | solution.py:335
  18.1 0.0 collective-permute-done.band0
  18.1 0.0 copy-start
  18.2 0.3 collective-permute-start.2
  18.5 2.6 %collective-permute-done.2.rest_2_ = f32[72,128]{1,0:T(8,128)S(1)} collective-permute-done((f32[72,128]{1,0:T(8,128)S(1)}, f32[72,128]{1,0:T(8,128)S(1)}, u32[]{:S(2)}, u32[]{:S(2)}) %collective-permute-start.2) | collective-permute-done | bytes 36896 | tf_op jit(solution)/shard_map/ppermute | solution.py:335
  21.0 0.0 copy-done
  21.1 9.2 %gather.2 = (f32[128,12,128]{2,1,0:T(8,128)S(1)}, f32[13,12,128]{2,1,0:T(8,128)S(1)}, f32[13,12,128]{2,1,0:T(8,128)S(1)}, f32[13,12,128]{2,1,0:T(8,128)S(1)}) custom-call(s32[2,128]{1,0:T(2,128)S(1)} %copy-done.1, s32[2,128]{1,0:T(2,128)S(1)} %copy-done.2, s32[2,4,13]{2,1,0:T(4,128)S(1)} %bitcast.14, f32[128,12,128]{2,1,0:T(8,128)S(1)} %copy.7.state.rest_0_, ...), custom_call_target="tpu_custom_call" | custom-call | tf_op jit(solution)/shard_map/gather/pallas_call | solution.py:386
  30.3 2.7 %collective-permute-start.3 = (f32[13,12,128]{2,1,0:T(8,128)S(1)}, f32[13,12,128]{2,1,0:T(8,128)S(1)}, u32[]{:S(2)}, u32[]{:S(2)}) collective-permute-start(f32[13,12,128]{2,1,0:T(8,128)S(1)} %get-tuple-element.27), channel_id=1, source_target_pairs={{0,2},{2,0},{4,6},{6,4},{8,10},{10,8},{12,14},{14,12},{16,18},{18,... | collective-permute-start | bytes 239624 | tf_op jit(solution)/shard_map/ppermute | solution.py:335
  33.0 2.3 %collective-permute-start.4 = (f32[13,12,128]{2,1,0:T(8,128)S(1)}, f32[13,12,128]{2,1,0:T(8,128)S(1)}, u32[]{:S(2)}, u32[]{:S(2)}) collective-permute-start(f32[13,12,128]{2,1,0:T(8,128)S(1)} %get-tuple-element.28), channel_id=1, source_target_pairs={{2,4},{4,2},{6,8},{8,6},{10,12},{12,10},{14,16},{16,14},{18,20},{2... | collective-permute-start | bytes 239624 | tf_op jit(solution)/shard_map/ppermute | solution.py:335
  35.3 0.3 collective-permute-start.5
  35.6 0.0 collective-permute-done.3.rest_0_
  35.6 4.7 %collective-permute-done.4.rest_1_ = f32[13,12,128]{2,1,0:T(8,128)S(1)} collective-permute-done((f32[13,12,128]{2,1,0:T(8,128)S(1)}, f32[13,12,128]{2,1,0:T(8,128)S(1)}, u32[]{:S(2)}, u32[]{:S(2)}) %collective-permute-start.4) | collective-permute-done | bytes 79904 | tf_op jit(solution)/shard_map/ppermute | solution.py:335
  40.4 0.0 collective-permute-done.5.rest_2_
  40.4 0.0 copy-start.3
  40.4 0.7 copy-done.3
  41.1 11.4 %scatter_next.1 = (f32[128,12,128]{2,1,0:T(8,128)S(1)}, f32[3,72,128]{2,1,0:T(8,128)S(1)}, f32[2,3,24,128]{3,2,1,0:T(8,128)S(1)}) custom-call(s32[2,128]{1,0:T(2,128)S(1)} %copy-done.1, s32[2,128]{1,0:T(2,128)S(1)} %copy-done.2, s32[2,4,13]{2,1,0:T(4,128)S(1)} %bitcast.15, s32[2,4]{1,0:T(2,128)S(1)} %bitcast.18, f32[128,12,128]{2,1,0:T(8,128)S(1)} %get-tuple-element.26.old, ...), custom_call_target="tpu_custom_call" | custom-call | tf_op jit(solution)/shard_map/scatter_next/pallas_call | solution.py:363
  52.5 4.0 %collective-permute-start.7 = (f32[3,24,128]{2,1,0:T(8,128)S(1)}, f32[3,24,128]{2,1,0:T(8,128)S(1)}, u32[]{:S(2)}, u32[]{:S(2)}) collective-permute-start(f32[3,24,128]{2,1,0:T(8,128)S(1)} %get-tuple-element.39), channel_id=1, source_target_pairs={{2,4},{4,2},{6,8},{8,6},{10,12},{12,10},{14,16},{16,14},{18,20},{2... | collective-permute-start | bytes 110600 | tf_op jit(solution)/shard_map/ppermute | solution.py:335
  56.5 0.1 collective-permute-start.6
  56.6 2.0 %collective-permute-done.7.band1 = f32[3,24,128]{2,1,0:T(8,128)S(1)} collective-permute-done((f32[3,24,128]{2,1,0:T(8,128)S(1)}, f32[3,24,128]{2,1,0:T(8,128)S(1)}, u32[]{:S(2)}, u32[]{:S(2)}) %collective-permute-start.7) | collective-permute-done | bytes 36896 | tf_op jit(solution)/shard_map/ppermute | solution.py:335
  58.6 0.0 collective-permute-done.6.band0
  58.6 0.1 collective-permute-start.8
  58.7 2.8 %collective-permute-done.8.rest_2_ = f32[72,128]{1,0:T(8,128)S(1)} collective-permute-done((f32[72,128]{1,0:T(8,128)S(1)}, f32[72,128]{1,0:T(8,128)S(1)}, u32[]{:S(2)}, u32[]{:S(2)}) %collective-permute-start.8) | collective-permute-done | bytes 36896 | tf_op jit(solution)/shard_map/ppermute | solution.py:335
  61.5 9.3 %gather.3 = (f32[128,12,128]{2,1,0:T(8,128)S(1)}, f32[13,12,128]{2,1,0:T(8,128)S(1)}, f32[13,12,128]{2,1,0:T(8,128)S(1)}, f32[13,12,128]{2,1,0:T(8,128)S(1)}) custom-call(s32[2,128]{1,0:T(2,128)S(1)} %copy-done.1, s32[2,128]{1,0:T(2,128)S(1)} %copy-done.2, s32[2,4,13]{2,1,0:T(4,128)S(1)} %bitcast.16, f32[128,12,128]{2,1,0:T(8,128)S(1)} %get-tuple-element.30.rest_0_, ...), custom_call_target="tpu_custom_call" | custom-call | tf_op jit(solution)/shard_map/gather/pallas_call | solution.py:386
  70.9 1.7 %collective-permute-start.9 = (f32[13,12,128]{2,1,0:T(8,128)S(1)}, f32[13,12,128]{2,1,0:T(8,128)S(1)}, u32[]{:S(2)}, u32[]{:S(2)}) collective-permute-start(f32[13,12,128]{2,1,0:T(8,128)S(1)} %get-tuple-element.36), channel_id=1, source_target_pairs={{0,2},{2,0},{4,6},{6,4},{8,10},{10,8},{12,14},{14,12},{16,18},{18,... | collective-permute-start | bytes 239624 | tf_op jit(solution)/shard_map/ppermute | solution.py:335
  72.6 3.1 %collective-permute-start.10 = (f32[13,12,128]{2,1,0:T(8,128)S(1)}, f32[13,12,128]{2,1,0:T(8,128)S(1)}, u32[]{:S(2)}, u32[]{:S(2)}) collective-permute-start(f32[13,12,128]{2,1,0:T(8,128)S(1)} %get-tuple-element.37), channel_id=1, source_target_pairs={{2,4},{4,2},{6,8},{8,6},{10,12},{12,10},{14,16},{16,14},{18,20},{2... | collective-permute-start | bytes 239624 | tf_op jit(solution)/shard_map/ppermute | solution.py:335
  75.7 0.2 collective-permute-start.11
  75.9 0.0 collective-permute-done.9.rest_0_
  75.9 3.9 %collective-permute-done.10.rest_1_ = f32[13,12,128]{2,1,0:T(8,128)S(1)} collective-permute-done((f32[13,12,128]{2,1,0:T(8,128)S(1)}, f32[13,12,128]{2,1,0:T(8,128)S(1)}, u32[]{:S(2)}, u32[]{:S(2)}) %collective-permute-start.10) | collective-permute-done | bytes 79904 | tf_op jit(solution)/shard_map/ppermute | solution.py:335
  79.7 0.0 collective-permute-done.11.rest_2_
  79.7 0.8 %settle_last.1 = f32[128,12,128]{2,1,0:T(8,128)S(1)} custom-call(s32[2,4,13]{2,1,0:T(4,128)S(1)} %bitcast.17, s32[2,4]{1,0:T(2,128)S(1)} %bitcast.19, f32[128,12,128]{2,1,0:T(8,128)S(1)} %get-tuple-element.35.old, f32[13,12,128]{2,1,0:T(8,128)S(1)} %collective-permute-done.9.rest_0_, f32[13,12,128]{2,1,0:T(8,128)S(1)} %collective-permute-done.10.rest_1_, ...), custom_call_target="tpu_custom_call" | custom-call | tf_op jit(solution)/shard_map/settle_last/pallas_call | solution.py:399
  80.6 1.1 %copy.8 = f32[128,12,128]{2,0,1:T(8,128)} copy(f32[128,12,128]{2,1,0:T(8,128)S(1)} %settle_last.1) | data formatting | bytes 1572864 | tf_op jit(solution)/shard_map/settle_last/pallas_call | solution.py:399
  (6 shorter events, 0.1 us)
Async XLA Ops:
  0.0 1.6 %copy-start.2 = (s32[2,128]{1,0:T(2,128)S(1)}, s32[2,128]{1,0:T(2,128)}, u32[]{:S(2)}) copy-start(s32[2,128]{1,0:T(2,128)} %anchor_cross.7) | copy-start | bytes 3076
  0.0 1.6 %copy-start.1 = (s32[2,128]{1,0:T(2,128)S(1)}, s32[2,128]{1,0:T(2,128)}, u32[]{:S(2)}) copy-start(s32[2,128]{1,0:T(2,128)} %anchor_down.7) | copy-start | bytes 3076
  12.8 5.3 %collective-permute-start.1 = (f32[3,24,128]{2,1,0:T(8,128)S(1)}, f32[3,24,128]{2,1,0:T(8,128)S(1)}, u32[]{:S(2)}, u32[]{:S(2)}) collective-permute-start(f32[3,24,128]{2,1,0:T(8,128)S(1)} %get-tuple-element.41), channel_id=1, source_target_pairs={{2,4},{4,2},{6,8},{8,6},{10,12},{12,10},{14,16},{16,14},{18,20},{2... | collective-permute-start | bytes 110600 | tf_op jit(solution)/shard_map/ppermute | solution.py:335
  16.5 1.6 %collective-permute-start = (f32[3,24,128]{2,1,0:T(8,128)S(1)}, f32[3,24,128]{2,1,0:T(8,128)S(1)}, u32[]{:S(2)}, u32[]{:S(2)}) collective-permute-start(f32[3,24,128]{2,1,0:T(8,128)S(1)} %get-tuple-element.42), channel_id=1, source_target_pairs={{0,2},{2,0},{4,6},{6,4},{8,10},{10,8},{12,14},{14,12},{16,18},{18,... | collective-permute-start | bytes 110600 | tf_op jit(solution)/shard_map/ppermute | solution.py:335
  18.1 2.9 %copy-start = (s32[2,4,13,1,1]{2,4,3,1,0:T(1,128)S(1)}, s32[2,4,13,1,1]{2,4,3,1,0:T(1,128)}, u32[]{:S(2)}) copy-start(s32[2,4,13,1,1]{2,4,3,1,0:T(1,128)} %param.9) | copy-start | bytes 1252
  18.2 2.9 %collective-permute-start.2 = (f32[72,128]{1,0:T(8,128)S(1)}, f32[72,128]{1,0:T(8,128)S(1)}, u32[]{:S(2)}, u32[]{:S(2)}) collective-permute-start(f32[72,128]{1,0:T(8,128)S(1)} %slice_bitcast_fusion.3), channel_id=1, source_target_pairs={{0,1},{1,0},{2,3},{3,2},{4,5},{5,4},{6,7},{7,6},{8,9},{9,8},{10,11... | collective-permute-start | bytes 110600 | tf_op jit(solution)/shard_map/ppermute | solution.py:335
  30.3 5.4 %collective-permute-start.3 = (f32[13,12,128]{2,1,0:T(8,128)S(1)}, f32[13,12,128]{2,1,0:T(8,128)S(1)}, u32[]{:S(2)}, u32[]{:S(2)}) collective-permute-start(f32[13,12,128]{2,1,0:T(8,128)S(1)} %get-tuple-element.27), channel_id=1, source_target_pairs={{0,2},{2,0},{4,6},{6,4},{8,10},{10,8},{12,14},{14,12},{16,18},{18,... | collective-permute-start | bytes 239624 | tf_op jit(solution)/shard_map/ppermute | solution.py:335
  33.0 7.4 %collective-permute-start.4 = (f32[13,12,128]{2,1,0:T(8,128)S(1)}, f32[13,12,128]{2,1,0:T(8,128)S(1)}, u32[]{:S(2)}, u32[]{:S(2)}) collective-permute-start(f32[13,12,128]{2,1,0:T(8,128)S(1)} %get-tuple-element.28), channel_id=1, source_target_pairs={{2,4},{4,2},{6,8},{8,6},{10,12},{12,10},{14,16},{16,14},{18,20},{2... | collective-permute-start | bytes 239624 | tf_op jit(solution)/shard_map/ppermute | solution.py:335
  35.3 5.1 %collective-permute-start.5 = (f32[13,12,128]{2,1,0:T(8,128)S(1)}, f32[13,12,128]{2,1,0:T(8,128)S(1)}, u32[]{:S(2)}, u32[]{:S(2)}) collective-permute-start(f32[13,12,128]{2,1,0:T(8,128)S(1)} %get-tuple-element.29), channel_id=1, source_target_pairs={{0,1},{1,0},{2,3},{3,2},{4,5},{5,4},{6,7},{7,6},{8,9},{9,8},{10,11... | collective-permute-start | bytes 239624 | tf_op jit(solution)/shard_map/ppermute | solution.py:335
  40.4 0.7 copy-start.3
  52.5 6.1 %collective-permute-start.7 = (f32[3,24,128]{2,1,0:T(8,128)S(1)}, f32[3,24,128]{2,1,0:T(8,128)S(1)}, u32[]{:S(2)}, u32[]{:S(2)}) collective-permute-start(f32[3,24,128]{2,1,0:T(8,128)S(1)} %get-tuple-element.39), channel_id=1, source_target_pairs={{2,4},{4,2},{6,8},{8,6},{10,12},{12,10},{14,16},{16,14},{18,20},{2... | collective-permute-start | bytes 110600 | tf_op jit(solution)/shard_map/ppermute | solution.py:335
  56.5 2.1 %collective-permute-start.6 = (f32[3,24,128]{2,1,0:T(8,128)S(1)}, f32[3,24,128]{2,1,0:T(8,128)S(1)}, u32[]{:S(2)}, u32[]{:S(2)}) collective-permute-start(f32[3,24,128]{2,1,0:T(8,128)S(1)} %get-tuple-element.40), channel_id=1, source_target_pairs={{0,2},{2,0},{4,6},{6,4},{8,10},{10,8},{12,14},{14,12},{16,18},{18,... | collective-permute-start | bytes 110600 | tf_op jit(solution)/shard_map/ppermute | solution.py:335
  58.6 2.9 %collective-permute-start.8 = (f32[72,128]{1,0:T(8,128)S(1)}, f32[72,128]{1,0:T(8,128)S(1)}, u32[]{:S(2)}, u32[]{:S(2)}) collective-permute-start(f32[72,128]{1,0:T(8,128)S(1)} %slice_bitcast_fusion), channel_id=1, source_target_pairs={{0,1},{1,0},{2,3},{3,2},{4,5},{5,4},{6,7},{7,6},{8,9},{9,8},{10,11... | collective-permute-start | bytes 110600 | tf_op jit(solution)/shard_map/ppermute | solution.py:335
  70.9 5.0 %collective-permute-start.9 = (f32[13,12,128]{2,1,0:T(8,128)S(1)}, f32[13,12,128]{2,1,0:T(8,128)S(1)}, u32[]{:S(2)}, u32[]{:S(2)}) collective-permute-start(f32[13,12,128]{2,1,0:T(8,128)S(1)} %get-tuple-element.36), channel_id=1, source_target_pairs={{0,2},{2,0},{4,6},{6,4},{8,10},{10,8},{12,14},{14,12},{16,18},{18,... | collective-permute-start | bytes 239624 | tf_op jit(solution)/shard_map/ppermute | solution.py:335
  72.6 7.2 %collective-permute-start.10 = (f32[13,12,128]{2,1,0:T(8,128)S(1)}, f32[13,12,128]{2,1,0:T(8,128)S(1)}, u32[]{:S(2)}, u32[]{:S(2)}) collective-permute-start(f32[13,12,128]{2,1,0:T(8,128)S(1)} %get-tuple-element.37), channel_id=1, source_target_pairs={{2,4},{4,2},{6,8},{8,6},{10,12},{12,10},{14,16},{16,14},{18,20},{2... | collective-permute-start | bytes 239624 | tf_op jit(solution)/shard_map/ppermute | solution.py:335
  75.7 4.1 %collective-permute-start.11 = (f32[13,12,128]{2,1,0:T(8,128)S(1)}, f32[13,12,128]{2,1,0:T(8,128)S(1)}, u32[]{:S(2)}, u32[]{:S(2)}) collective-permute-start(f32[13,12,128]{2,1,0:T(8,128)S(1)} %get-tuple-element.38), channel_id=1, source_target_pairs={{0,1},{1,0},{2,3},{3,2},{4,5},{5,4},{6,7},{7,6},{8,9},{9,8},{10,11... | collective-permute-start | bytes 239624 | tf_op jit(solution)/shard_map/ppermute | solution.py:335

commit v2 on v1

v2 whole, which is shorter than its diff:
```python
import functools

import jax
import jax.numpy as jnp
from jax import lax
from jax.experimental import pallas as pl
from jax.experimental.pallas import tpu as pltpu
from jax.sharding import PartitionSpec as P

WIN_DOWN = 8
WIN_CROSS = 16
GHOST = 4
STEPS = 2
TILE_DOWN = 16
TILE_CROSS = 256
TIME_STEP = 0.1
GRAVITY = 5.6
MASS_FLOOR = 0.5
FIELDS = 12
LANES = 128
ROWS = 8
CHANNELS = 3
STRIDE = 32
BAND = 2 * GHOST
LOADS = 6
GROUP = 64


def spline_pair(distance):
    near = jnp.clip(distance, -0.5, 0.5)
    far = jnp.clip(distance - near, -1.0, 1.0)
    twice = near + near
    slope = far - twice
    return slope * slope + (1.5 - 1.5 * twice * twice), slope


def low_part(x):
    return x - x.astype(jnp.bfloat16).astype(jnp.float32)


def node_rows(count):
    return lax.broadcasted_iota(jnp.int32, (count, LANES), 0).astype(jnp.float32)


def cross_weights(w, cols):
    value, slope = spline_pair(w - cols)
    both = jnp.concatenate([value, slope], axis=1)
    high = both.astype(jnp.bfloat16)
    low = (both - high.astype(jnp.float32)).astype(jnp.bfloat16)
    return jnp.concatenate([high, low], axis=0)


def particle_loads(state, loads, blocks, keep=None):
    def several(q, carry):
        spot = pl.ds(pl.multiple_of(q * ROWS, ROWS), ROWS)
        vd, vc, sdd, sdc, scc, mass, vol = (state[f, spot, :] for f in range(2, 9))
        quarter = 0.25 * mass
        push = (-0.5 * TIME_STEP) * vol
        terms = (
            quarter,
            quarter * (vd + TIME_STEP * GRAVITY),
            quarter * vc,
            push * sdd,
            push * sdc,
            push * scc,
        )
        for k, term in enumerate(terms):
            loads[k, spot, :] = term if keep is None else term * keep[spot, :]
        return carry

    lax.fori_loop(0, blocks // ROWS, several, 0, unroll=4)


def scatter_block(u, w, load, sums, first_row, first_col, rows, cols, inside):
    value, slope = spline_pair(u - rows)
    zero = jnp.zeros_like(value)
    load_dc = load(4)
    parts = (
        (load(0) * value, zero),
        (load(1) * value + load(3) * slope, load_dc * value),
        (load(2) * value + load_dc * slope, load(5) * value),
    )
    gap = jnp.zeros((16, 2 * LANES), jnp.bfloat16)
    pieces = []
    for along, across in parts:
        both = jnp.concatenate([along, across], axis=1)
        pieces += [jnp.concatenate([both, low_part(both)], axis=0).astype(jnp.bfloat16), gap]
    found = lax.dot_general(
        cross_weights(w, cols),
        jnp.concatenate(pieces, axis=0),
        (((1,), (1,)), ((), ())),
        preferred_element_type=jnp.float32,
    )
    found = found[:WIN_CROSS] + found[WIN_CROSS:]
    found = jnp.concatenate(
        [found, jnp.zeros((WIN_CROSS, LANES - CHANNELS * STRIDE), jnp.float32)], axis=1
    )
    found = jnp.where(inside, found + pltpu.roll(found, LANES - WIN_DOWN, 1), 0.0)
    found = pltpu.roll(found, first_row, 1)
    spot = pl.ds(first_col, WIN_CROSS)
    sums[spot, :] = sums[spot, :] + found


def scatter_rows(state, loads, sums, place, blocks, group):
    rows = node_rows(WIN_DOWN)
    cols = node_rows(WIN_CROSS)
    lane = lax.broadcasted_iota(jnp.int32, (WIN_CROSS, LANES), 1)
    inside = (lane & (STRIDE - 1)) < WIN_DOWN

    def several(q, carry):
        for k in range(group):
            m = q * group + k
            row = pl.ds(m, 1)
            first_row, first_col = place(m)
            scatter_block(
                state[0, row, :],
                state[1, row, :],
                lambda f, row=row: loads[f, row, :],
                sums,
                first_row,
                first_col,
                rows,
                cols,
                inside,
            )
        return carry

    lax.fori_loop(0, blocks // group, several, 0)


def window_place(anchor_down, anchor_cross, step):
    return lambda b: (anchor_down[step, b] + GHOST, anchor_cross[step, b] + GHOST)


def write_grid(sums, grid, pay):
    tiles, rows, _ = grid.shape
    height = rows // CHANNELS
    odd = lax.rem(lax.axis_index("down"), 2)
    for t in range(tiles):
        turned = jnp.transpose(sums[t * LANES : (t + 1) * LANES, :])
        for c in range(CHANNELS):
            part = turned[c * STRIDE : c * STRIDE + height]
            grid[t, c * height : (c + 1) * height, :] = part
            spot = slice(c * BAND, (c + 1) * BAND)
            pay[odd, t, spot, :] = part[height - BAND :]
            pay[1 - odd, t, spot, :] = part[:BAND]


def first_kernel(step, anchor_down, anchor_cross, state, grid, pay, sums, loads):
    blocks = state.shape[1]
    sums[...] = jnp.zeros_like(sums)
    particle_loads(state, loads, blocks)
    scatter_rows(
        state, loads, sums, window_place(anchor_down, anchor_cross, step), blocks, GROUP
    )
    write_grid(sums, grid, pay)


def link_side(link):
    axis, second = divmod(link, 2)
    odd = lax.rem(lax.axis_index(("down", "cross")[axis]), 2)
    return 2 * axis + (1 - odd if second else odd)


def settle(state, arrived, slots, counts, step):
    for link, came in enumerate(arrived):
        side = link_side(link)

        def put(m, carry, came=came, side=side):
            slot = pl.ds(slots[step, side, m], 1)
            state[:, slot, :] = came[:, pl.ds(m, 1), :]
            return carry

        lax.fori_loop(0, counts[step, side], put, 0)


def next_kernel(step, links, anchor_down, anchor_cross, slots, counts, old, *rest):
    arrived = rest[:links]
    state, grid, pay, sums, loads = rest[links:]
    blocks = state.shape[1]
    state[...] = old[...]
    settle(state, arrived, slots, counts, step - 1)
    sums[...] = jnp.zeros_like(sums)
    particle_loads(state, loads, blocks)
    scatter_rows(
        state, loads, sums, window_place(anchor_down, anchor_cross, step), blocks, GROUP
    )
    write_grid(sums, grid, pay)


def last_kernel(step, links, slots, counts, old, *rest):
    arrived = rest[:links]
    state = rest[links]
    state[...] = old[...]
    settle(state, arrived, slots, counts, step)


def cross_kernel(width, grid, band0, band1, total, pay):
    tiles, rows, _ = grid.shape
    height = rows // CHANNELS
    odd = lax.rem(lax.axis_index("down"), 2)
    index = lax.axis_index("down")
    size = lax.axis_size("down")
    total[...] = grid[...]
    partner = index - 1 + 2 * odd
    there = (partner >= 0) & (partner < size)
    for t in range(tiles):
        for c in range(CHANNELS):
            spot = slice(c * BAND, (c + 1) * BAND)
            for link in range(2):
                if link == 0:
                    band = band0[t, spot, :]
                else:
                    band = jnp.where(there, band1[odd, t, spot, :], 0.0)
                at_first = odd if link == 0 else 1 - odd
                start = c * height + (1 - at_first) * (height - BAND)
                place = pl.ds(pl.multiple_of(start, 8), BAND)
                total[t, place, :] = total[t, place, :] + band
    odd = lax.rem(lax.axis_index("cross"), 2)
    tile, lane = divmod(width - BAND, LANES)
    last = pltpu.roll(total[tile], LANES - lane, 1) if lane else total[tile]
    pad = jnp.zeros((LANES - rows, LANES), jnp.float32)
    pay[odd] = jnp.transpose(jnp.concatenate([last, pad], axis=0))[:BAND]
    pay[1 - odd] = jnp.transpose(jnp.concatenate([total[0], pad], axis=0))[:BAND]


def node_velocity(total, bands, speed, width):
    tiles, rows, _ = total.shape
    height = rows // CHANNELS
    odd = lax.rem(lax.axis_index("cross"), 2)
    tile, lane = divmod(width - BAND, LANES)
    pad = jnp.zeros((LANES - BAND, LANES), jnp.float32)
    for link, came in enumerate(bands):
        band = jnp.transpose(jnp.concatenate([came[...], pad], axis=0))[:rows]
        at_first = odd if link == 0 else 1 - odd
        total[0] = total[0] + jnp.where(at_first == 1, band, 0.0)
        shifted = pltpu.roll(band, lane, 1) if lane else band
        total[tile] = total[tile] + jnp.where(at_first == 0, shifted, 0.0)
    tile_down = height - 2 * GHOST
    tile_cross = width - 2 * GHOST
    row_global = (
        lax.broadcasted_iota(jnp.int32, (height, LANES), 0)
        + lax.axis_index("down") * tile_down
        - GHOST
    )
    col_first = lax.broadcasted_iota(jnp.int32, (height, LANES), 1) - GHOST
    total_rows = tile_down * lax.axis_size("down")
    total_cols = tile_cross * lax.axis_size("cross")
    keep_rows = (row_global > 0) & (row_global < total_rows - 1)
    for t in range(tiles):
        col_global = col_first + (lax.axis_index("cross") * tile_cross + t * LANES)
        kept = keep_rows & (col_global > 0) & (col_global < total_cols - 1)
        mass = jnp.maximum(total[t, :height, :], MASS_FLOOR)
        for c in range(2):
            value = total[t, (c + 1) * height : (c + 2) * height, :] / mass
            speed[t, c] = jnp.where(kept, value, 0.0)


def row_sums(terms, row):
    half = row < 4
    four = [
        jnp.where(half, terms[k], terms[k + 4])
        + pltpu.roll(jnp.where(half, terms[k + 4], terms[k]), 4, 0)
        for k in range(4)
    ]
    pair = (row & 2) == 0
    two = [
        jnp.where(
            pair, four[k] + pltpu.roll(four[k], 6, 0), four[k + 2] + pltpu.roll(four[k + 2], 2, 0)
        )
        for k in range(2)
    ]
    return jnp.where(
        (row & 1) == 0, two[0] + pltpu.roll(two[0], 7, 0), two[1] + pltpu.roll(two[1], 1, 0)
    )


def gather_terms(u, w, speed, first_row, first_col, rows, cols, lane):
    tile = first_col // LANES
    shift = first_col - tile * LANES
    spot = pl.ds(first_row, WIN_DOWN)
    here = jnp.concatenate([speed[tile, 0, spot, :], speed[tile, 1, spot, :]], axis=0)
    after = jnp.concatenate([speed[tile + 1, 0, spot, :], speed[tile + 1, 1, spot, :]], axis=0)
    window = jnp.where(lane >= shift, here, after)
    window = jnp.where(
        lane < WIN_CROSS,
        pltpu.roll(window, (LANES - shift) & (LANES - 1), 1),
        pltpu.roll(window, (WIN_CROSS + LANES - shift) & (LANES - 1), 1),
    )
    window = jnp.concatenate([window, low_part(window)], axis=0).astype(jnp.bfloat16)
    found = jnp.dot(
        window[:, : 2 * WIN_CROSS], cross_weights(w, cols), preferred_element_type=jnp.float32
    )
    found = found[: 2 * WIN_DOWN] + found[2 * WIN_DOWN :]
    value, slope = spline_pair(u - rows)
    along_d, along_c = found[:WIN_DOWN, :LANES], found[WIN_DOWN:, :LANES]
    across_d, across_c = found[:WIN_DOWN, LANES:], found[WIN_DOWN:, LANES:]
    return (
        value * along_d,
        value * along_c,
        slope * along_d,
        slope * along_c,
        value * across_d,
        value * across_c,
    )


def gather_rows(state, speed, place, blocks, group, out):
    rows = node_rows(WIN_DOWN)
    cols = node_rows(WIN_CROSS)
    lane = lax.broadcasted_iota(jnp.int32, (2 * WIN_DOWN, LANES), 1)
    row = lax.broadcasted_iota(jnp.int32, (ROWS, LANES), 0)

    def several(q, carry):
        for part in range(group // ROWS):
            base = q * group + part * ROWS
            terms = []
            for k in range(ROWS):
                one = pl.ds(base + k, 1)
                first_row, first_col = place(base + k)
                terms.append(
                    gather_terms(
                        state[0, one, :],
                        state[1, one, :],
                        speed,
                        first_row,
                        first_col,
                        rows,
                        cols,
                        lane,
                    )
                )
            vel_d, vel_c, l_dd, l_cd, l_dc, l_cc = (row_sums(t, row) for t in zip(*terms))
            vel_d, vel_c = 0.25 * vel_d, 0.25 * vel_c
            l_dd, l_cc = 0.5 * l_dd, 0.5 * l_cc
            rate_dc = 0.25 * (l_dc + l_cd)
            trace = l_dd + l_cc
            spot = pl.ds(pl.multiple_of(base, ROWS), ROWS)
            field = [state[f, spot, :] for f in range(FIELDS)]
            shear = (2.0 * TIME_STEP) * field[9]
            spread = (TIME_STEP * field[10]) * trace
            stretch = TIME_STEP * trace
            result = {
                0: jnp.clip(field[0] + TIME_STEP * vel_d, 0.5, WIN_DOWN - 1.5),
                1: jnp.clip(field[1] + TIME_STEP * vel_c, 0.5, WIN_CROSS - 1.5),
                2: vel_d,
                3: vel_c,
                4: field[4] + (spread + shear * l_dd),
                5: field[5] + shear * rate_dc,
                6: field[6] + (spread + shear * l_cc),
                8: field[8] + field[8] * stretch,
                11: field[11]
                + TIME_STEP * (l_dd * l_dd + l_cc * l_cc + 2.0 * rate_dc * rate_dc),
            }
            for f in range(FIELDS):
                out[f, spot, :] = result.get(f, field[f])
        return carry

    lax.fori_loop(0, blocks // group, several, 0)


def gather_kernel(step, links, width, anchor_down, anchor_cross, slots, *rest):
    state, total = rest[:2]
    bands = rest[2:links]
    moved = rest[links]
    sent = rest[links + 1 : 2 * links + 1]
    speed, sums = rest[2 * links + 1 :]
    blocks = state.shape[1]
    sums[...] = total[...]
    node_velocity(sums, bands, speed, width)
    gather_rows(
        state, speed, window_place(anchor_down, anchor_cross, step), blocks, GROUP, moved
    )
    cap = slots.shape[2]
    for link in range(links):
        side = link_side(link)
        for m in range(cap):
            sent[link][:, m : m + 1, :] = moved[:, pl.ds(slots[step, side, m], 1), :]


def swap_pairs(size, first):
    pairs = []
    for i in range(first, size - 1, 2):
        pairs += [(i, i + 1), (i + 1, i)]
    return pairs


def odd_groups(size_down, size_cross):
    groups = []
    for i in (0, size_down - 1):
        groups += [[i * size_cross + j, i * size_cross + j + 1] for j in range(0, size_cross, 2)]
    for i in range(1, size_down - 1, 2):
        groups += [[i * size_cross + j, (i + 1) * size_cross + j] for j in range(size_cross)]
    return groups


def solution(mesh):
    size_down, size_cross = mesh.shape["down"], mesh.shape["cross"]
    links = 3 if size_cross <= 2 else 4
    smem = pl.BlockSpec(memory_space=pltpu.SMEM)
    vmem = pl.BlockSpec(memory_space=pltpu.VMEM)
    params = pltpu.CompilerParams(vmem_limit_bytes=40 * 1024 * 1024)
    f32 = jnp.float32

    def swap(x, link):
        axis, second = divmod(link, 2)
        name, size = (("down", size_down), ("cross", size_cross))[axis]
        return lax.ppermute(x, name, swap_pairs(size, second))

    def on_device(particles, anchor_down, anchor_cross, move_count, move_slots):
        blocks = particles.shape[0]
        cap = move_slots.shape[2]
        slots = move_slots.reshape(STEPS, 4, cap)
        counts = move_count.reshape(STEPS, 4)
        height = TILE_DOWN + 2 * GHOST
        width = TILE_CROSS + 2 * GHOST
        tiles = -(-width // LANES)
        grid_type = jax.ShapeDtypeStruct((tiles, CHANNELS * height, LANES), f32)
        band_type = jax.ShapeDtypeStruct((2, tiles, CHANNELS * BAND, LANES), f32)
        state_type = jax.ShapeDtypeStruct((FIELDS, blocks, LANES), f32)
        sent_type = jax.ShapeDtypeStruct((FIELDS, cap, LANES), f32)
        sums_scratch = pltpu.VMEM((tiles * LANES, LANES), f32)
        loads_scratch = pltpu.VMEM((LOADS, blocks, LANES), f32)
        state = jnp.transpose(particles, (1, 0, 2))
        arrived = []
        for step in range(STEPS):
            if step == 0:
                grid, pay = pl.pallas_call(
                    functools.partial(first_kernel, step),
                    out_shape=(grid_type, band_type),
                    in_specs=[smem, smem, vmem],
                    out_specs=(vmem, vmem),
                    scratch_shapes=[sums_scratch, loads_scratch],
                    compiler_params=params,
                    name="scatter_first",
                )(anchor_down, anchor_cross, state)
            else:
                state, grid, pay = pl.pallas_call(
                    functools.partial(next_kernel, step, links),
                    out_shape=(state_type, grid_type, band_type),
                    in_specs=[smem] * 4 + [vmem] * (1 + links),
                    out_specs=(vmem, vmem, vmem),
                    scratch_shapes=[sums_scratch, loads_scratch],
                    compiler_params=params,
                    name="scatter_next",
                )(anchor_down, anchor_cross, slots, counts, state, *arrived)
            band0 = swap(pay[0], 0)
            band1 = lax.all_gather(
                pay[1], ("down", "cross"), axis_index_groups=odd_groups(size_down, size_cross)
            )
            total, pay = pl.pallas_call(
                functools.partial(cross_kernel, width),
                out_shape=(grid_type, jax.ShapeDtypeStruct((2, BAND, LANES), f32)),
                in_specs=[vmem] * 3,
                out_specs=(vmem, vmem),
                compiler_params=params,
                name="add_down",
            )(grid, band0, band1)
            bands = [swap(pay[k], 2 + k) for k in range(links - 2)]
            state, *sent = pl.pallas_call(
                functools.partial(gather_kernel, step, links, width),
                out_shape=(state_type,) + (sent_type,) * links,
                in_specs=[smem] * 3 + [vmem] * links,
                out_specs=(vmem,) * (1 + links),
                scratch_shapes=[
                    pltpu.VMEM((tiles, 2, height, LANES), f32),
                    pltpu.VMEM(grid_type.shape, f32),
                ],
                compiler_params=params,
                name="gather",
            )(anchor_down, anchor_cross, slots, state, total, *bands)
            arrived = [swap(sent[k], k) for k in range(links)]
        state = pl.pallas_call(
            functools.partial(last_kernel, STEPS - 1, links),
            out_shape=state_type,
            in_specs=[smem] * 2 + [vmem] * (1 + links),
            out_specs=vmem,
            compiler_params=params,
            name="settle_last",
        )(slots, counts, state, *arrived)
        return jnp.transpose(state, (1, 0, 2))

    return jax.shard_map(
        on_device,
        mesh=mesh,
        in_specs=(
            P(("down", "cross"), None, None),
            P(None, ("down", "cross")),
            P(None, ("down", "cross")),
            P(None, None, "down", "cross"),
            P(None, None, None, "down", "cross"),
        ),
        out_specs=P(("down", "cross"), None, None),
        check_vma=False,
    )
```

time: 82.9 us -> 51.4 us (0.62)
  Pallas kernels: 42 us -> 13.4 us
  blocking collectives: 0 us -> 9.31 us
  starting transfers between devices: 18.6 us -> 10.8 us
  waiting for transfers between devices: 17.5 us -> 13.5 us
    pallas_call x4, Pallas kernels: 30.8 us -> 10.5 us  [the longest x2 5.64 us: on_device(): pl.pallas_call(functools.partial(gather_kernel, step, links, width), out_...]
    all_gather x0 -> x2, blocking collectives: none -> 9.31 us  [on_device(): lax.all_gather(pay[1], ('down', 'cross'), axis_index_groups=odd_groups(si...]
    pallas_call x1, Pallas kernels: 11.1 us -> 2.69 us  [on_device(): pl.pallas_call(functools.partial(first_kernel, step), out_shape=(grid_typ...]
    ppermute x12 -> x10, starting transfers between devices: 18.6 us -> 10.8 us  [swap(): return lax.ppermute(x, name, swap_pairs(size, second))]
    ppermute x12 -> x10, waiting for transfers between devices: 17.5 us -> 13.5 us  [swap(): return lax.ppermute(x, name, swap_pairs(size, second))]
    unnamed x9 -> x14, local copies, waits for them, and re-layouts: 2.33 us -> 3.85 us
    pallas_call x1 -> x0, local copies, waits for them, and re-layouts: 1.12 us -> none  [on_device(): pl.pallas_call(functools.partial(last_kernel, STEPS - 1, cross_links), ou...]
  transfers between devices with their start and end apart: 12 -> 10, of which waited for: 6 -> 5; matrix products, arithmetic and copies ran while one was open for 0% -> 0% of each run, Pallas kernels for 0% -> 0%
where the time goes in v2:
time: 51.4 us; the launch traced here: 50.9 us
  waiting for transfers between devices  13.5 us (26%)
  Pallas kernels  13.4 us (26%)
  starting transfers between devices  10.8 us (21%)
  blocking collectives  9.31 us (18%)
  local copies, waits for them, and re-layouts  3.87 us (8%)
    ppermute x10, waiting for transfers between devices, swap(): return lax.ppermute(x, name, swap_pairs(size, second))  13.5 us
    ppermute x10, starting transfers between devices, swap(): return lax.ppermute(x, name, swap_pairs(size, second))  10.8 us
    all_gather x2, blocking collectives, on_device(): lax.all_gather(pay[1], ('down', 'cross'), axis_index_groups=odd_groups(si...  9.31 us
    pallas_call x2, Pallas kernels, on_device(): pl.pallas_call(functools.partial(gather_kernel, step, links, width), out_...  5.64 us
    unnamed x14, local copies, waits for them, and re-layouts  3.85 us
    pallas_call x1, Pallas kernels, on_device(): pl.pallas_call(functools.partial(next_kernel, step, links), out_shape=(st...  3.04 us
    pallas_call x1, Pallas kernels, on_device(): pl.pallas_call(functools.partial(first_kernel, step), out_shape=(grid_typ...  2.69 us
    pallas_call x1, Pallas kernels, on_device(): pl.pallas_call(functools.partial(last_kernel, STEPS - 1, links), out_shap...  1.81 us
  transfers between devices with their start and end apart: 10, of which 5 were waited for; matrix products, arithmetic and copies ran while one was open for 0% of the time, Pallas kernels for 0%

profile of v2, /device:TPU:11, one launch (start us, length us, event | category | flops | bytes accessed | tf_op | source)
XLA Modules:
  0.0 50.9 jit_solution(8734653947647776152)
XLA Ops:
  0.0 0.0 copy-start.3
  0.0 0.7 %copy-done.3 = s32[2,128]{1,0:T(2,128)S(1)} copy-done((s32[2,128]{1,0:T(2,128)S(1)}, s32[2,128]{1,0:T(2,128)}, u32[]{:S(2)}) %copy-start.3) | copy-done | bytes 1048
  0.7 0.0 copy-start
  0.7 1.1 %copy-done = f32[128,12,128]{2,0,1:T(8,128)S(1)} copy-done((f32[128,12,128]{2,0,1:T(8,128)S(1)}, f32[128,12,128]{2,0,1:T(8,128)}, u32[]{:S(2)}) %copy-start) | copy-done | bytes 786456
  1.8 0.0 copy-start.4
  1.8 0.7 %copy-done.4 = s32[2,128]{1,0:T(2,128)S(1)} copy-done((s32[2,128]{1,0:T(2,128)S(1)}, s32[2,128]{1,0:T(2,128)}, u32[]{:S(2)}) %copy-start.4) | copy-done | bytes 1048
  2.5 0.0 copy-start.1
  2.5 2.7 %scatter_first.1 = (f32[3,72,128]{2,1,0:T(8,128)S(1)}, f32[2,3,24,128]{3,2,1,0:T(8,128)S(1)}) custom-call(s32[2,128]{1,0:T(2,128)S(1)} %copy-done.3, s32[2,128]{1,0:T(2,128)S(1)} %copy-done.4, f32[12,128,128]{2,1,0:T(8,128)S(1)} %bitcast.12), custom_call_target="tpu_custom_call" | custom-call | tf_op jit(solution)/shard_map/scatter_first/pallas_call | solution.py:428
  5.2 0.7 %collective-permute-start = (f32[3,24,128]{2,1,0:T(8,128)S(1)}, f32[3,24,128]{2,1,0:T(8,128)S(1)}, u32[]{:S(2)}, u32[]{:S(2)}) collective-permute-start(f32[3,24,128]{2,1,0:T(8,128)S(1)} %get-tuple-element.42), channel_id=1, source_target_pairs={{0,2},{2,0},{4,6},{6,4},{8,10},{10,8},{12,14},{14,12},{16,18},{18,... | collective-permute-start | bytes 110600 | tf_op jit(solution)/shard_map/ppermute | solution.py:408
  6.0 4.6 %all_gather.6.band1 = f32[2,3,24,128]{3,2,1,0:T(8,128)S(1)} all-gather(f32[1,3,24,128]{3,2,1,0:T(8,128)S(1)} %get-tuple-element.41), channel_id=1, replica_groups={{0,1},{30,31},{2,4},{3,5},{6,8},{7,9},{10,12},{11,13},{14,16},{15,17},{..., dimensions={0}, use_global_device_ids=true | all-gather | bytes 110592 | tf_op jit(solution)/shard_map/all_gather | solution.py:448
  10.5 0.0 collective-permute-done.band0
  10.5 0.1 add_down.2
  10.6 0.0 copy-start.2
  10.6 0.3 collective-permute-start.1
  10.9 2.2 %collective-permute-done.1.rest_2_ = f32[8,128]{1,0:T(8,128)S(1)} collective-permute-done((f32[8,128]{1,0:T(8,128)S(1)}, f32[8,128]{1,0:T(8,128)S(1)}, u32[]{:S(2)}, u32[]{:S(2)}) %collective-permute-start.1) | collective-permute-done | bytes 4128 | tf_op jit(solution)/shard_map/ppermute | solution.py:408
  13.1 0.0 copy-start.5
  13.1 0.0 copy-done.1
  13.1 0.0 copy-done.2
  13.1 0.7 %copy-done.5 = s32[2,128]{1,0:T(2,128)S(1)} copy-done((s32[2,128]{1,0:T(2,128)S(1)}, s32[2,128]{1,0:T(2,128)}, u32[]{:S(2)}) %copy-start.5) | copy-done | bytes 1048
  13.8 2.8 %gather.2 = (f32[12,128,128]{2,1,0:T(8,128)S(1)}, f32[12,13,128]{2,1,0:T(8,128)S(1)}, f32[12,13,128]{2,1,0:T(8,128)S(1)}, f32[12,13,128]{2,1,0:T(8,128)S(1)}) custom-call(s32[2,128]{1,0:T(2,128)S(1)} %copy-done.3, s32[2,128]{1,0:T(2,128)S(1)} %copy-done.5, s32[2,4,13]{2,1,0:T(4,128)S(1)} %bitcast.14, f32[12,128,128]{2,1,0:T(8,128)S(1)} %bitcast.13, ...), custom_call_target="tpu_custom_call" | custom-call | tf_op jit(solution)/shard_map/gather/pallas_call | solution.py:460
  16.6 1.7 %collective-permute-start.2 = (f32[12,13,128]{2,1,0:T(8,128)S(1)}, f32[12,13,128]{2,1,0:T(8,128)S(1)}, u32[]{:S(2)}, u32[]{:S(2)}) collective-permute-start(f32[12,13,128]{2,1,0:T(8,128)S(1)} %get-tuple-element.27), channel_id=1, source_target_pairs={{0,2},{2,0},{4,6},{6,4},{8,10},{10,8},{12,14},{14,12},{16,18},{18,... | collective-permute-start | bytes 239624 | tf_op jit(solution)/shard_map/ppermute | solution.py:408
  18.3 2.2 %collective-permute-start.3 = (f32[12,13,128]{2,1,0:T(8,128)S(1)}, f32[12,13,128]{2,1,0:T(8,128)S(1)}, u32[]{:S(2)}, u32[]{:S(2)}) collective-permute-start(f32[12,13,128]{2,1,0:T(8,128)S(1)} %get-tuple-element.28), channel_id=1, source_target_pairs={{2,4},{4,2},{6,8},{8,6},{10,12},{12,10},{14,16},{16,14},{18,20},{2... | collective-permute-start | bytes 239624 | tf_op jit(solution)/shard_map/ppermute | solution.py:408
  20.6 0.3 collective-permute-start.4
  20.9 0.0 collective-permute-done.2.rest_0_
  20.9 4.6 %collective-permute-done.3.rest_1_ = f32[12,13,128]{2,1,0:T(8,128)S(1)} collective-permute-done((f32[12,13,128]{2,1,0:T(8,128)S(1)}, f32[12,13,128]{2,1,0:T(8,128)S(1)}, u32[]{:S(2)}, u32[]{:S(2)}) %collective-permute-start.3) | collective-permute-done | bytes 79904 | tf_op jit(solution)/shard_map/ppermute | solution.py:408
  25.4 0.0 collective-permute-done.4.rest_2_
  25.4 0.0 copy-start.6
  25.4 0.7 %copy-done.6 = s32[2,4,1,1]{1,3,2,0:T(1,128)S(1)} copy-done((s32[2,4,1,1]{1,3,2,0:T(1,128)S(1)}, s32[2,4,1,1]{1,3,2,0:T(1,128)}, u32[]{:S(2)}) %copy-start.6) | copy-done | bytes 56
  26.1 3.0 %scatter_next.1 = (f32[12,128,128]{2,1,0:T(8,128)S(1)}, f32[3,72,128]{2,1,0:T(8,128)S(1)}, f32[2,3,24,128]{3,2,1,0:T(8,128)S(1)}) custom-call(s32[2,128]{1,0:T(2,128)S(1)} %copy-done.3, s32[2,128]{1,0:T(2,128)S(1)} %copy-done.5, s32[2,4,13]{2,1,0:T(4,128)S(1)} %bitcast.15, s32[2,4]{1,0:T(2,128)S(1)} %bitcast.18, f32[12,128,128]{2,1,0:T(8,128)S(1)} %get-tuple-element.26.old, ...), custom_call_target="tpu_custom_call" | custom-call | tf_op jit(solution)/shard_map/scatter_next/pallas_call | solution.py:438
  29.2 0.4 collective-permute-start.5
  29.6 4.7 %all_gather.7.band1 = f32[2,3,24,128]{3,2,1,0:T(8,128)S(1)} all-gather(f32[1,3,24,128]{3,2,1,0:T(8,128)S(1)} %get-tuple-element.39), channel_id=1, replica_groups={{0,1},{30,31},{2,4},{3,5},{6,8},{7,9},{10,12},{11,13},{14,16},{15,17},{..., dimensions={0}, use_global_device_ids=true | all-gather | bytes 110592 | tf_op jit(solution)/shard_map/all_gather | solution.py:448
  34.3 0.0 collective-permute-done.5.band0
  34.3 0.1 add_down.3
  34.4 0.2 collective-permute-start.6
  34.6 2.3 %collective-permute-done.6.rest_2_ = f32[8,128]{1,0:T(8,128)S(1)} collective-permute-done((f32[8,128]{1,0:T(8,128)S(1)}, f32[8,128]{1,0:T(8,128)S(1)}, u32[]{:S(2)}, u32[]{:S(2)}) %collective-permute-start.6) | collective-permute-done | bytes 4128 | tf_op jit(solution)/shard_map/ppermute | solution.py:408
  36.9 2.9 %gather.3 = (f32[12,128,128]{2,1,0:T(8,128)S(1)}, f32[12,13,128]{2,1,0:T(8,128)S(1)}, f32[12,13,128]{2,1,0:T(8,128)S(1)}, f32[12,13,128]{2,1,0:T(8,128)S(1)}) custom-call(s32[2,128]{1,0:T(2,128)S(1)} %copy-done.3, s32[2,128]{1,0:T(2,128)S(1)} %copy-done.5, s32[2,4,13]{2,1,0:T(4,128)S(1)} %bitcast.16, f32[12,128,128]{2,1,0:T(8,128)S(1)} %get-tuple-element.30.rest_0_, ...), custom_call_target="tpu_custom_call" | custom-call | tf_op jit(solution)/shard_map/gather/pallas_call | solution.py:460
  39.8 1.7 %collective-permute-start.7 = (f32[12,13,128]{2,1,0:T(8,128)S(1)}, f32[12,13,128]{2,1,0:T(8,128)S(1)}, u32[]{:S(2)}, u32[]{:S(2)}) collective-permute-start(f32[12,13,128]{2,1,0:T(8,128)S(1)} %get-tuple-element.36), channel_id=1, source_target_pairs={{0,2},{2,0},{4,6},{6,4},{8,10},{10,8},{12,14},{14,12},{16,18},{18,... | collective-permute-start | bytes 239624 | tf_op jit(solution)/shard_map/ppermute | solution.py:408
  41.5 2.8 %collective-permute-start.8 = (f32[12,13,128]{2,1,0:T(8,128)S(1)}, f32[12,13,128]{2,1,0:T(8,128)S(1)}, u32[]{:S(2)}, u32[]{:S(2)}) collective-permute-start(f32[12,13,128]{2,1,0:T(8,128)S(1)} %get-tuple-element.37), channel_id=1, source_target_pairs={{2,4},{4,2},{6,8},{8,6},{10,12},{12,10},{14,16},{16,14},{18,20},{2... | collective-permute-start | bytes 239624 | tf_op jit(solution)/shard_map/ppermute | solution.py:408
  44.3 0.3 collective-permute-start.9
  44.6 0.0 collective-permute-done.7.rest_0_
  44.6 4.2 %collective-permute-done.8.rest_1_ = f32[12,13,128]{2,1,0:T(8,128)S(1)} collective-permute-done((f32[12,13,128]{2,1,0:T(8,128)S(1)}, f32[12,13,128]{2,1,0:T(8,128)S(1)}, u32[]{:S(2)}, u32[]{:S(2)}) %collective-permute-start.8) | collective-permute-done | bytes 79904 | tf_op jit(solution)/shard_map/ppermute | solution.py:408
  48.7 0.3 collective-permute-done.9.rest_2_
  49.1 1.8 %settle_last.1 = f32[12,128,128]{2,1,0:T(8,128)} custom-call(s32[2,4,13]{2,1,0:T(4,128)S(1)} %bitcast.17, s32[2,4]{1,0:T(2,128)S(1)} %bitcast.19, f32[12,128,128]{2,1,0:T(8,128)S(1)} %get-tuple-element.35.old, f32[12,13,128]{2,1,0:T(8,128)S(1)} %collective-permute-done.7.rest_0_, f32[12,13,128]{2,1,0:T(8,128)S(1)} %collective-permute-done.8.rest_1_, ...), custom_call_target="tpu_custom_call" | custom-call | tf_op jit(solution)/shard_map/settle_last/pallas_call | solution.py:473
  (4 shorter events, 0.0 us)
Async XLA Ops:
  0.0 0.7 %copy-start.3 = (s32[2,128]{1,0:T(2,128)S(1)}, s32[2,128]{1,0:T(2,128)}, u32[]{:S(2)}) copy-start(s32[2,128]{1,0:T(2,128)} %anchor_down.7) | copy-start | bytes 3076
  0.7 1.1 %copy-start = (f32[128,12,128]{2,0,1:T(8,128)S(1)}, f32[128,12,128]{2,0,1:T(8,128)}, u32[]{:S(2)}) copy-start(f32[128,12,128]{2,0,1:T(8,128)} %param.5) | copy-start | bytes 2359300
  1.8 0.7 %copy-start.4 = (s32[2,128]{1,0:T(2,128)S(1)}, s32[2,128]{1,0:T(2,128)}, u32[]{:S(2)}) copy-start(s32[2,128]{1,0:T(2,128)} %anchor_cross.7) | copy-start | bytes 3076
  2.5 10.6 %copy-start.1 = (f32[128,12,128]{2,0,1:T(8,128)S(1)}, f32[128,12,128]{2,0,1:T(8,128)}, u32[]{:S(2)}) copy-start(f32[128,12,128]{2,0,1:T(8,128)} %param.5) | copy-start | bytes 2359300
  5.2 5.3 %collective-permute-start = (f32[3,24,128]{2,1,0:T(8,128)S(1)}, f32[3,24,128]{2,1,0:T(8,128)S(1)}, u32[]{:S(2)}, u32[]{:S(2)}) collective-permute-start(f32[3,24,128]{2,1,0:T(8,128)S(1)} %get-tuple-element.42), channel_id=1, source_target_pairs={{0,2},{2,0},{4,6},{6,4},{8,10},{10,8},{12,14},{14,12},{16,18},{18,... | collective-permute-start | bytes 110600 | tf_op jit(solution)/shard_map/ppermute | solution.py:408
  10.6 2.5 %copy-start.2 = (s32[2,4,13,1,1]{2,4,3,1,0:T(1,128)S(1)}, s32[2,4,13,1,1]{2,4,3,1,0:T(1,128)}, u32[]{:S(2)}) copy-start(s32[2,4,13,1,1]{2,4,3,1,0:T(1,128)} %param.9) | copy-start | bytes 1252
  10.6 2.5 %collective-permute-start.1 = (f32[8,128]{1,0:T(8,128)S(1)}, f32[8,128]{1,0:T(8,128)S(1)}, u32[]{:S(2)}, u32[]{:S(2)}) collective-permute-start(f32[8,128]{1,0:T(8,128)S(1)} %slice_bitcast_fusion.3), channel_id=1, source_target_pairs={{0,1},{1,0},{2,3},{3,2},{4,5},{5,4},{6,7},{7,6},{8,9},{9,8},{10,11... | collective-permute-start | bytes 12296 | tf_op jit(solution)/shard_map/ppermute | solution.py:408
  13.1 0.7 %copy-start.5 = (s32[2,128]{1,0:T(2,128)S(1)}, s32[2,128]{1,0:T(2,128)}, u32[]{:S(2)}) copy-start(s32[2,128]{1,0:T(2,128)} %anchor_cross.7) | copy-start | bytes 3076
  16.6 4.3 %collective-permute-start.2 = (f32[12,13,128]{2,1,0:T(8,128)S(1)}, f32[12,13,128]{2,1,0:T(8,128)S(1)}, u32[]{:S(2)}, u32[]{:S(2)}) collective-permute-start(f32[12,13,128]{2,1,0:T(8,128)S(1)} %get-tuple-element.27), channel_id=1, source_target_pairs={{0,2},{2,0},{4,6},{6,4},{8,10},{10,8},{12,14},{14,12},{16,18},{18,... | collective-permute-start | bytes 239624 | tf_op jit(solution)/shard_map/ppermute | solution.py:408
  18.3 7.1 %collective-permute-start.3 = (f32[12,13,128]{2,1,0:T(8,128)S(1)}, f32[12,13,128]{2,1,0:T(8,128)S(1)}, u32[]{:S(2)}, u32[]{:S(2)}) collective-permute-start(f32[12,13,128]{2,1,0:T(8,128)S(1)} %get-tuple-element.28), channel_id=1, source_target_pairs={{2,4},{4,2},{6,8},{8,6},{10,12},{12,10},{14,16},{16,14},{18,20},{2... | collective-permute-start | bytes 239624 | tf_op jit(solution)/shard_map/ppermute | solution.py:408
  20.6 4.9 %collective-permute-start.4 = (f32[12,13,128]{2,1,0:T(8,128)S(1)}, f32[12,13,128]{2,1,0:T(8,128)S(1)}, u32[]{:S(2)}, u32[]{:S(2)}) collective-permute-start(f32[12,13,128]{2,1,0:T(8,128)S(1)} %get-tuple-element.29), channel_id=1, source_target_pairs={{0,1},{1,0},{2,3},{3,2},{4,5},{5,4},{6,7},{7,6},{8,9},{9,8},{10,11... | collective-permute-start | bytes 239624 | tf_op jit(solution)/shard_map/ppermute | solution.py:408
  25.4 0.7 %copy-start.6 = (s32[2,4,1,1]{1,3,2,0:T(1,128)S(1)}, s32[2,4,1,1]{1,3,2,0:T(1,128)}, u32[]{:S(2)}) copy-start(s32[2,4,1,1]{1,3,2,0:T(1,128)} %param.8) | copy-start | bytes 100
  29.2 5.1 %collective-permute-start.5 = (f32[3,24,128]{2,1,0:T(8,128)S(1)}, f32[3,24,128]{2,1,0:T(8,128)S(1)}, u32[]{:S(2)}, u32[]{:S(2)}) collective-permute-start(f32[3,24,128]{2,1,0:T(8,128)S(1)} %get-tuple-element.40), channel_id=1, source_target_pairs={{0,2},{2,0},{4,6},{6,4},{8,10},{10,8},{12,14},{14,12},{16,18},{18,... | collective-permute-start | bytes 110600 | tf_op jit(solution)/shard_map/ppermute | solution.py:408
  34.4 2.5 %collective-permute-start.6 = (f32[8,128]{1,0:T(8,128)S(1)}, f32[8,128]{1,0:T(8,128)S(1)}, u32[]{:S(2)}, u32[]{:S(2)}) collective-permute-start(f32[8,128]{1,0:T(8,128)S(1)} %slice_bitcast_fusion.2), channel_id=1, source_target_pairs={{0,1},{1,0},{2,3},{3,2},{4,5},{5,4},{6,7},{7,6},{8,9},{9,8},{10,11... | collective-permute-start | bytes 12296 | tf_op jit(solution)/shard_map/ppermute | solution.py:408
  39.8 4.8 %collective-permute-start.7 = (f32[12,13,128]{2,1,0:T(8,128)S(1)}, f32[12,13,128]{2,1,0:T(8,128)S(1)}, u32[]{:S(2)}, u32[]{:S(2)}) collective-permute-start(f32[12,13,128]{2,1,0:T(8,128)S(1)} %get-tuple-element.36), channel_id=1, source_target_pairs={{0,2},{2,0},{4,6},{6,4},{8,10},{10,8},{12,14},{14,12},{16,18},{18,... | collective-permute-start | bytes 239624 | tf_op jit(solution)/shard_map/ppermute | solution.py:408
  41.5 7.3 %collective-permute-start.8 = (f32[12,13,128]{2,1,0:T(8,128)S(1)}, f32[12,13,128]{2,1,0:T(8,128)S(1)}, u32[]{:S(2)}, u32[]{:S(2)}) collective-permute-start(f32[12,13,128]{2,1,0:T(8,128)S(1)} %get-tuple-element.37), channel_id=1, source_target_pairs={{2,4},{4,2},{6,8},{8,6},{10,12},{12,10},{14,16},{16,14},{18,20},{2... | collective-permute-start | bytes 239624 | tf_op jit(solution)/shard_map/ppermute | solution.py:408
  44.3 4.8 %collective-permute-start.9 = (f32[12,13,128]{2,1,0:T(8,128)S(1)}, f32[12,13,128]{2,1,0:T(8,128)S(1)}, u32[]{:S(2)}, u32[]{:S(2)}) collective-permute-start(f32[12,13,128]{2,1,0:T(8,128)S(1)} %get-tuple-element.38), channel_id=1, source_target_pairs={{0,1},{1,0},{2,3},{3,2},{4,5},{5,4},{6,7},{7,6},{8,9},{9,8},{10,11... | collective-permute-start | bytes 239624 | tf_op jit(solution)/shard_map/ppermute | solution.py:408

commit v3 on v2

--- a/solution.py
+++ b/solution.py
@@ -24,6 +24,7 @@
 BAND = 2 * GHOST
 LOADS = 6
 GROUP = 64
+VMEM_BYTES = 32 * 1024 * 1024
 
 
 def spline_pair(distance):
@@ -51,8 +52,8 @@
 
 
 def particle_loads(state, loads, blocks, keep=None):
-    def several(q, carry):
-        spot = pl.ds(pl.multiple_of(q * ROWS, ROWS), ROWS)
+    for base in range(0, blocks, ROWS):
+        spot = pl.ds(base, ROWS)
         vd, vc, sdd, sdc, scc, mass, vol = (state[f, spot, :] for f in range(2, 9))
         quarter = 0.25 * mass
         push = (-0.5 * TIME_STEP) * vol
@@ -66,27 +67,29 @@
         )
         for k, term in enumerate(terms):
             loads[k, spot, :] = term if keep is None else term * keep[spot, :]
-        return carry
-
-    lax.fori_loop(0, blocks // ROWS, several, 0, unroll=4)
-
-
-def scatter_block(u, w, load, sums, first_row, first_col, rows, cols, inside):
+
+
+def scatter_block(u, w, load, sums, weights, slot, first_row, first_col, rows, cols, inside):
     value, slope = spline_pair(u - rows)
-    zero = jnp.zeros_like(value)
+    across_weights = cross_weights(w, cols)
+    if weights is not None:
+        weights[0][slot] = across_weights
+        weights[1][slot, :WIN_DOWN, :] = value
+        weights[1][slot, WIN_DOWN:, :] = slope
     load_dc = load(4)
     parts = (
-        (load(0) * value, zero),
+        (load(0) * value,),
         (load(1) * value + load(3) * slope, load_dc * value),
         (load(2) * value + load_dc * slope, load(5) * value),
     )
     gap = jnp.zeros((16, 2 * LANES), jnp.bfloat16)
+    none = jnp.zeros((16, LANES), jnp.bfloat16)
     pieces = []
-    for along, across in parts:
-        both = jnp.concatenate([along, across], axis=1)
-        pieces += [jnp.concatenate([both, low_part(both)], axis=0).astype(jnp.bfloat16), gap]
+    for part in parts:
+        halves = [jnp.concatenate([x, low_part(x)], axis=0).astype(jnp.bfloat16) for x in part]
+        pieces += [jnp.concatenate((halves + [none])[:2], axis=1), gap]
     found = lax.dot_general(
-        cross_weights(w, cols),
+        across_weights,
         jnp.concatenate(pieces, axis=0),
         (((1,), (1,)), ((), ())),
         preferred_element_type=jnp.float32,
@@ -101,7 +104,7 @@
     sums[spot, :] = sums[spot, :] + found
 
 
-def scatter_rows(state, loads, sums, place, blocks, group):
+def scatter_rows(state, loads, sums, weights, slot_of, place, first, count, group):
     rows = node_rows(WIN_DOWN)
     cols = node_rows(WIN_CROSS)
     lane = lax.broadcasted_iota(jnp.int32, (WIN_CROSS, LANES), 1)
@@ -109,14 +112,17 @@
 
     def several(q, carry):
         for k in range(group):
-            m = q * group + k
+            m = first + q * group + k
             row = pl.ds(m, 1)
-            first_row, first_col = place(m)
+            slot = slot_of(m)
+            first_row, first_col = place(slot)
             scatter_block(
                 state[0, row, :],
                 state[1, row, :],
                 lambda f, row=row: loads[f, row, :],
                 sums,
+                weights,
+                slot,
                 first_row,
                 first_col,
                 rows,
@@ -125,7 +131,11 @@
             )
         return carry
 
-    lax.fori_loop(0, blocks // group, several, 0)
+    steps = count // group
+    if steps == 1:
+        several(0, 0)
+    else:
+        lax.fori_loop(0, steps, several, 0)
 
 
 def window_place(anchor_down, anchor_cross, step):
@@ -146,13 +156,68 @@
             pay[1 - odd, t, spot, :] = part[:BAND]
 
 
-def first_kernel(step, anchor_down, anchor_cross, state, grid, pay, sums, loads):
-    blocks = state.shape[1]
+def first_kernel(
+    step,
+    parts,
+    down_in,
+    cross_in,
+    slots_in,
+    counts_in,
+    particles,
+    state,
+    grid,
+    pay,
+    wide,
+    tall,
+    anchor_down,
+    anchor_cross,
+    slots,
+    counts,
+    sums,
+    loads,
+    down_scalar,
+    cross_scalar,
+    sems,
+):
+    blocks = particles.shape[1]
+    size = blocks // parts
+    scalars = [
+        pltpu.make_async_copy(src, dst, sems.at[k])
+        for k, (src, dst) in enumerate(((down_in, down_scalar), (cross_in, cross_scalar)))
+    ]
+    whole = [
+        pltpu.make_async_copy(
+            particles.at[:, pl.ds(k * size, size), :],
+            state.at[:, pl.ds(k * size, size), :],
+            sems.at[2 + k],
+        )
+        for k in range(parts)
+    ]
+    others = [
+        pltpu.make_async_copy(src, dst, sems.at[2 + parts + k])
+        for k, (src, dst) in enumerate(
+            (
+                (down_in, anchor_down),
+                (cross_in, anchor_cross),
+                (slots_in, slots),
+                (counts_in, counts),
+            )
+        )
+    ]
+    for copy in scalars + whole + others:
+        copy.start()
     sums[...] = jnp.zeros_like(sums)
-    particle_loads(state, loads, blocks)
-    scatter_rows(
-        state, loads, sums, window_place(anchor_down, anchor_cross, step), blocks, GROUP
-    )
+    for copy in scalars:
+        copy.wait()
+    place = window_place(down_scalar, cross_scalar, step)
+    for k in range(parts):
+        whole[k].wait()
+        particle_loads(state.at[:, pl.ds(k * size, size), :], loads.at[:, pl.ds(k * size, size), :], size)
+        scatter_rows(
+            state, loads, sums, (wide, tall), lambda m: m, place, k * size, size, min(GROUP, size)
+        )
+    for copy in others:
+        copy.wait()
     write_grid(sums, grid, pay)
 
 
@@ -162,37 +227,82 @@
     return 2 * axis + (1 - odd if second else odd)
 
 
-def settle(state, arrived, slots, counts, step):
+def settle(state, field, arrived, slots, counts, step, blocks):
+    cap = slots.shape[2]
     for link, came in enumerate(arrived):
         side = link_side(link)
-
-        def put(m, carry, came=came, side=side):
-            slot = pl.ds(slots[step, side, m], 1)
-            state[:, slot, :] = came[:, pl.ds(m, 1), :]
-            return carry
-
-        lax.fori_loop(0, counts[step, side], put, 0)
+        for m in range(cap):
+            slot = jnp.where(m < counts[step, side], slots[step, side, m], blocks)
+            state[field, pl.ds(slot, 1), :] = came[field * cap + m : field * cap + m + 1, :]
+
+
+def pick_arrived(refs):
+    odd = lax.rem(lax.axis_index("down"), 2)
+    return [ref.at[odd] if link == 1 else ref for link, ref in enumerate(refs)]
 
 
 def next_kernel(step, links, anchor_down, anchor_cross, slots, counts, old, *rest):
-    arrived = rest[:links]
-    state, grid, pay, sums, loads = rest[links:]
-    blocks = state.shape[1]
-    state[...] = old[...]
-    settle(state, arrived, slots, counts, step - 1)
+    arrived = pick_arrived(rest[:links])
+    state, grid, pay, wide, tall, sums, loads = rest[links:]
+    blocks = loads.shape[1]
+    state[:, :blocks, :] = old[:, :blocks, :]
+    for f in range(FIELDS):
+        settle(state, f, arrived, slots, counts, step - 1, blocks)
     sums[...] = jnp.zeros_like(sums)
     particle_loads(state, loads, blocks)
     scatter_rows(
-        state, loads, sums, window_place(anchor_down, anchor_cross, step), blocks, GROUP
+        state,
+        loads,
+        sums,
+        (wide, tall),
+        lambda m: m,
+        window_place(anchor_down, anchor_cross, step),
+        0,
+        blocks,
+        min(GROUP, blocks),
     )
     write_grid(sums, grid, pay)
 
 
+def gather_kernel(step, links, width, anchor_down, anchor_cross, slots, state, total, *rest):
+    bands = rest[: links - 2]
+    wide, tall, after = rest[links - 2 : links + 1]
+    sent = rest[links + 1 : 2 * links + 1]
+    speed, sums = rest[2 * links + 1 :]
+    blocks = wide.shape[0]
+    sums[...] = total[...]
+    node_velocity(sums, bands, speed, width)
+    gather_rows(
+        state,
+        speed,
+        (wide, tall),
+        lambda m: m,
+        window_place(anchor_down, anchor_cross, step),
+        blocks,
+        min(GROUP, blocks),
+        after,
+    )
+    cap = slots.shape[2]
+    for link in range(links):
+        side = link_side(link)
+        for m in range(cap):
+            slot = pl.ds(slots[step, side, m], 1)
+            for f in range(FIELDS):
+                sent[link][f * cap + m : f * cap + m + 1, :] = after[f, slot, :]
+
+
 def last_kernel(step, links, slots, counts, old, *rest):
-    arrived = rest[:links]
-    state = rest[links]
-    state[...] = old[...]
-    settle(state, arrived, slots, counts, step)
+    arrived = pick_arrived(rest[:links])
+    out, state, sems = rest[links:]
+    blocks = out.shape[1]
+    copies = []
+    for f in range(FIELDS):
+        state[f, :blocks, :] = old[f, :blocks, :]
+        settle(state, f, arrived, slots, counts, step, blocks)
+        copies.append(pltpu.make_async_copy(state.at[f, pl.ds(0, blocks), :], out.at[f], sems.at[f]))
+        copies[-1].start()
+    for copy in copies:
+        copy.wait()
 
 
 def cross_kernel(width, grid, band0, band1, total, pay):
@@ -275,7 +385,7 @@
     )
 
 
-def gather_terms(u, w, speed, first_row, first_col, rows, cols, lane):
+def gather_terms(weights, speed, slot, first_row, first_col, lane):
     tile = first_col // LANES
     shift = first_col - tile * LANES
     spot = pl.ds(first_row, WIN_DOWN)
@@ -289,10 +399,10 @@
     )
     window = jnp.concatenate([window, low_part(window)], axis=0).astype(jnp.bfloat16)
     found = jnp.dot(
-        window[:, : 2 * WIN_CROSS], cross_weights(w, cols), preferred_element_type=jnp.float32
+        window[:, : 2 * WIN_CROSS], weights[0][slot], preferred_element_type=jnp.float32
     )
     found = found[: 2 * WIN_DOWN] + found[2 * WIN_DOWN :]
-    value, slope = spline_pair(u - rows)
+    value, slope = weights[1][slot, :WIN_DOWN, :], weights[1][slot, WIN_DOWN:, :]
     along_d, along_c = found[:WIN_DOWN, :LANES], found[WIN_DOWN:, :LANES]
     across_d, across_c = found[:WIN_DOWN, LANES:], found[WIN_DOWN:, LANES:]
     return (
@@ -305,9 +415,7 @@
     )
 
 
-def gather_rows(state, speed, place, blocks, group, out):
-    rows = node_rows(WIN_DOWN)
-    cols = node_rows(WIN_CROSS)
+def gather_rows(state, speed, weights, slot_of, place, blocks, group, out):
     lane = lax.broadcasted_iota(jnp.int32, (2 * WIN_DOWN, LANES), 1)
     row = lax.broadcasted_iota(jnp.int32, (ROWS, LANES), 0)
 
@@ -316,26 +424,15 @@
             base = q * group + part * ROWS
             terms = []
             for k in range(ROWS):
-                one = pl.ds(base + k, 1)
-                first_row, first_col = place(base + k)
-                terms.append(
-                    gather_terms(
-                        state[0, one, :],
-                        state[1, one, :],
-                        speed,
-                        first_row,
-                        first_col,
-                        rows,
-                        cols,
-                        lane,
-                    )
-                )
+                slot = slot_of(base + k)
+                first_row, first_col = place(slot)
+                terms.append(gather_terms(weights, speed, slot, first_row, first_col, lane))
             vel_d, vel_c, l_dd, l_cd, l_dc, l_cc = (row_sums(t, row) for t in zip(*terms))
             vel_d, vel_c = 0.25 * vel_d, 0.25 * vel_c
             l_dd, l_cc = 0.5 * l_dd, 0.5 * l_cc
             rate_dc = 0.25 * (l_dc + l_cd)
             trace = l_dd + l_cc
-            spot = pl.ds(pl.multiple_of(base, ROWS), ROWS)
+            spot = pl.ds(base if isinstance(base, int) else pl.multiple_of(base, ROWS), ROWS)
             field = [state[f, spot, :] for f in range(FIELDS)]
             shear = (2.0 * TIME_STEP) * field[9]
             spread = (TIME_STEP * field[10]) * trace
@@ -356,26 +453,11 @@
                 out[f, spot, :] = result.get(f, field[f])
         return carry
 
-    lax.fori_loop(0, blocks // group, several, 0)
-
-
-def gather_kernel(step, links, width, anchor_down, anchor_cross, slots, *rest):
-    state, total = rest[:2]
-    bands = rest[2:links]
-    moved = rest[links]
-    sent = rest[links + 1 : 2 * links + 1]
-    speed, sums = rest[2 * links + 1 :]
-    blocks = state.shape[1]
-    sums[...] = total[...]
-    node_velocity(sums, bands, speed, width)
-    gather_rows(
-        state, speed, window_place(anchor_down, anchor_cross, step), blocks, GROUP, moved
-    )
-    cap = slots.shape[2]
-    for link in range(links):
-        side = link_side(link)
-        for m in range(cap):
-            sent[link][:, m : m + 1, :] = moved[:, pl.ds(slots[step, side, m], 1), :]
+    steps = blocks // group
+    if steps == 1:
+        several(0, 0)
+    else:
+        lax.fori_loop(0, steps, several, 0)
 
 
 def swap_pairs(size, first):
@@ -399,7 +481,7 @@
     links = 3 if size_cross <= 2 else 4
     smem = pl.BlockSpec(memory_space=pltpu.SMEM)
     vmem = pl.BlockSpec(memory_space=pltpu.VMEM)
-    params = pltpu.CompilerParams(vmem_limit_bytes=40 * 1024 * 1024)
+    hbm = pl.BlockSpec(memory_space=pltpu.HBM)
     f32 = jnp.float32
 
     def swap(x, link):
@@ -407,77 +489,105 @@
         name, size = (("down", size_down), ("cross", size_cross))[axis]
         return lax.ppermute(x, name, swap_pairs(size, second))
 
+    def gather_pairs(x):
+        return lax.all_gather(
+            x, ("down", "cross"), axis_index_groups=odd_groups(size_down, size_cross)
+        )
+
+    def call(name, kernel, outs, in_specs, scratch=()):
+        return pl.pallas_call(
+            kernel,
+            out_shape=outs,
+            in_specs=in_specs,
+            out_specs=tuple(hbm if isinstance(x, pl.MemoryRef) else vmem for x in outs),
+            scratch_shapes=scratch,
+            compiler_params=pltpu.CompilerParams(vmem_limit_bytes=VMEM_BYTES),
+            name=name,
+        )
+
     def on_device(particles, anchor_down, anchor_cross, move_count, move_slots):
         blocks = particles.shape[0]
         cap = move_slots.shape[2]
-        slots = move_slots.reshape(STEPS, 4, cap)
-        counts = move_count.reshape(STEPS, 4)
         height = TILE_DOWN + 2 * GHOST
         width = TILE_CROSS + 2 * GHOST
         tiles = -(-width // LANES)
-        grid_type = jax.ShapeDtypeStruct((tiles, CHANNELS * height, LANES), f32)
-        band_type = jax.ShapeDtypeStruct((2, tiles, CHANNELS * BAND, LANES), f32)
-        state_type = jax.ShapeDtypeStruct((FIELDS, blocks, LANES), f32)
-        sent_type = jax.ShapeDtypeStruct((FIELDS, cap, LANES), f32)
-        sums_scratch = pltpu.VMEM((tiles * LANES, LANES), f32)
-        loads_scratch = pltpu.VMEM((LOADS, blocks, LANES), f32)
-        state = jnp.transpose(particles, (1, 0, 2))
-        arrived = []
+
+        def array(*shape, dtype=f32):
+            return jax.ShapeDtypeStruct(shape, dtype)
+
+        grid_type = array(tiles, CHANNELS * height, LANES)
+        band_type = array(2, tiles, CHANNELS * BAND, LANES)
+        state_type = array(FIELDS, blocks + ROWS, LANES)
+        sent_type = array(-(-FIELDS * cap // 8) * 8, LANES)
+        weight_types = (
+            array(blocks, 2 * WIN_CROSS, 2 * LANES, dtype=jnp.bfloat16),
+            array(blocks, 2 * WIN_DOWN, LANES),
+        )
+        scatter_scratch = [
+            pltpu.VMEM((tiles * LANES, LANES), f32),
+            pltpu.VMEM((LOADS, blocks, LANES), f32),
+        ]
+        ints = (
+            anchor_down,
+            anchor_cross,
+            move_slots.reshape(STEPS, 4, cap),
+            move_count.reshape(STEPS, 4),
+        )
+        given = ints + (jnp.transpose(particles, (1, 0, 2)),)
+        parts = 2
+        state, grid, pay, *rest = call(
+            "scatter_first",
+            functools.partial(first_kernel, 0, parts),
+            (state_type, grid_type, band_type)
+            + weight_types
+            + tuple(array(*x.shape, dtype=x.dtype) for x in ints),
+            [hbm] * 5,
+            scatter_scratch
+            + [
+                pltpu.SMEM(anchor_down.shape, jnp.int32),
+                pltpu.SMEM(anchor_cross.shape, jnp.int32),
+                pltpu.SemaphoreType.DMA((6 + parts,)),
+            ],
+        )(*(pltpu.with_memory_space_constraint(x, pltpu.HBM) for x in given))
+        weights, ints = rest[:2], rest[2:]
         for step in range(STEPS):
-            if step == 0:
-                grid, pay = pl.pallas_call(
-                    functools.partial(first_kernel, step),
-                    out_shape=(grid_type, band_type),
-                    in_specs=[smem, smem, vmem],
-                    out_specs=(vmem, vmem),
-                    scratch_shapes=[sums_scratch, loads_scratch],
-                    compiler_params=params,
-                    name="scatter_first",
-                )(anchor_down, anchor_cross, state)
-            else:
-                state, grid, pay = pl.pallas_call(
+            if step:
+                state, grid, pay, *weights = call(
+                    "scatter_next",
                     functools.partial(next_kernel, step, links),
-                    out_shape=(state_type, grid_type, band_type),
-                    in_specs=[smem] * 4 + [vmem] * (1 + links),
-                    out_specs=(vmem, vmem, vmem),
-                    scratch_shapes=[sums_scratch, loads_scratch],
-                    compiler_params=params,
-                    name="scatter_next",
-                )(anchor_down, anchor_cross, slots, counts, state, *arrived)
+                    (state_type, grid_type, band_type) + weight_types,
+                    [smem] * 4 + [vmem] * (links + 1),
+                    scatter_scratch,
+                )(*ints, state, *arrived)
             band0 = swap(pay[0], 0)
-            band1 = lax.all_gather(
-                pay[1], ("down", "cross"), axis_index_groups=odd_groups(size_down, size_cross)
-            )
-            total, pay = pl.pallas_call(
+            band1 = gather_pairs(pay[1])
+            total, pay = call(
+                "add_down",
                 functools.partial(cross_kernel, width),
-                out_shape=(grid_type, jax.ShapeDtypeStruct((2, BAND, LANES), f32)),
-                in_specs=[vmem] * 3,
-                out_specs=(vmem, vmem),
-                compiler_params=params,
-                name="add_down",
+                (grid_type, array(2, BAND, LANES)),
+                [vmem] * 3,
             )(grid, band0, band1)
             bands = [swap(pay[k], 2 + k) for k in range(links - 2)]
-            state, *sent = pl.pallas_call(
+            state, *sent = call(
+                "gather",
                 functools.partial(gather_kernel, step, links, width),
-                out_shape=(state_type,) + (sent_type,) * links,
-                in_specs=[smem] * 3 + [vmem] * links,
-                out_specs=(vmem,) * (1 + links),
-                scratch_shapes=[
+                (state_type,) + (sent_type,) * links,
+                [smem] * 3 + [vmem] * (2 + links),
+                [
                     pltpu.VMEM((tiles, 2, height, LANES), f32),
                     pltpu.VMEM(grid_type.shape, f32),
                 ],
-                compiler_params=params,
-                name="gather",
-            )(anchor_down, anchor_cross, slots, state, total, *bands)
-            arrived = [swap(sent[k], k) for k in range(links)]
-        state = pl.pallas_call(
+            )(*ints[:3], state, total, *bands, *weights)
+            arrived = [
+                gather_pairs(x) if link == 1 else swap(x, link) for link, x in enumerate(sent)
+            ]
+        (state,) = call(
+            "settle_last",
             functools.partial(last_kernel, STEPS - 1, links),
-            out_shape=state_type,
-            in_specs=[smem] * 2 + [vmem] * (1 + links),
-            out_specs=vmem,
-            compiler_params=params,
-            name="settle_last",
-        )(slots, counts, state, *arrived)
+            (pltpu.HBM((FIELDS, blocks, LANES), f32),),
+            [smem] * 2 + [vmem] * (links + 1),
+            [pltpu.VMEM(state_type.shape, f32), pltpu.SemaphoreType.DMA((FIELDS,))],
+        )(*ints[2:], state, *arrived)
         return jnp.transpose(state, (1, 0, 2))
 
     return jax.shard_map(

time: 51.4 us -> 45.9 us (0.89)
  blocking collectives: 9.31 us -> 20 us
  waiting for transfers between devices: 13.5 us -> 3.47 us
  local copies, waits for them, and re-layouts: 3.87 us -> 0.03 us
  starting transfers between devices: 10.8 us -> 7.7 us
  Pallas kernels: 13.4 us -> 14.5 us
    all_gather x2 -> x4, blocking collectives: 9.31 us -> 20 us  [gather_pairs(): lax.all_gather(x, ('down', 'cross'), axis_index_groups=odd_groups(size_do...]
    ppermute x10 -> x8, waiting for transfers between devices: 13.5 us -> 3.47 us  [swap(): return lax.ppermute(x, name, swap_pairs(size, second))]
    unnamed x14 -> x0, local copies, waits for them, and re-layouts: 3.85 us -> none
    ppermute x10 -> x8, starting transfers between devices: 10.8 us -> 7.7 us  [swap(): return lax.ppermute(x, name, swap_pairs(size, second))]
    pallas_call x7, Pallas kernels: 13.4 us -> 14.5 us  [the longest x2 5 us: on_device(): call('gather', functools.partial(gather_kernel, step, links, width), (sta...]
  transfers between devices with their start and end apart: 10 -> 8, of which waited for: 5 -> 2; matrix products, arithmetic and copies ran while one was open for 0% -> 0% of each run, Pallas kernels for 0% -> 0%
where the time goes in v3:
time: 45.9 us; the launch traced here: 45.7 us
  blocking collectives  20 us (44%)
  Pallas kernels  14.5 us (32%)
  starting transfers between devices  7.7 us (17%)
  waiting for transfers between devices  3.47 us (8%)
    all_gather x4, blocking collectives, gather_pairs(): lax.all_gather(x, ('down', 'cross'), axis_index_groups=odd_groups(size_do...  20 us
    ppermute x8, starting transfers between devices, swap(): return lax.ppermute(x, name, swap_pairs(size, second))  7.7 us
    pallas_call x2, Pallas kernels, on_device(): call('gather', functools.partial(gather_kernel, step, links, width), (sta...  5 us
    pallas_call x1, Pallas kernels, on_device(): call('scatter_next', functools.partial(next_kernel, step, links), (state_...  3.69 us
    ppermute x8, waiting for transfers between devices, swap(): return lax.ppermute(x, name, swap_pairs(size, second))  3.47 us
    pallas_call x1, Pallas kernels, on_device(): call('scatter_first', functools.partial(first_kernel, 0, parts), (state_t...  3.3 us
    pallas_call x1, Pallas kernels, on_device(): call('settle_last', functools.partial(last_kernel, STEPS - 1, links), (pl...  2.35 us
  transfers between devices with their start and end apart: 8, of which 2 were waited for; matrix products, arithmetic and copies ran while one was open for 0% of the time, Pallas kernels for 0%

profile of v3, /device:TPU:11, one launch (start us, length us, event | category | flops | bytes accessed | tf_op | source)
XLA Modules:
  0.0 45.7 jit_solution(2870605671130919620)
XLA Ops:
  0.0 3.3 %scatter_first.1 = (f32[12,136,128]{2,1,0:T(8,128)S(1)}, f32[3,72,128]{2,1,0:T(8,128)S(1)}, f32[2,3,24,128]{3,2,1,0:T(8,128)S(1)}, bf16[128,32,256]{2,1,0:T(8,12...) custom-call(s32[2,128]{1,0:T(2,128)} %down_in.1, ...), custom_call_target="tpu_custom_call" | custom-call | tf_op jit(solution)/shard_map/scatter_first/pallas_call | solution.py:538
  3.3 0.7 %collective-permute-start = (f32[3,24,128]{2,1,0:T(8,128)S(1)}, f32[3,24,128]{2,1,0:T(8,128)S(1)}, u32[]{:S(2)}, u32[]{:S(2)}) collective-permute-start(f32[3,24,128]{2,1,0:T(8,128)S(1)} %get-tuple-element.60), channel_id=1, source_target_pairs={{0,2},{2,0},{4,6},{6,4},{8,10},{10,8},{12,14},{14,12},{16,18},{18,... | collective-permute-start | bytes 110600 | tf_op jit(solution)/shard_map/ppermute | solution.py:490
  4.1 4.6 %all_gather.18.band1 = f32[2,3,24,128]{3,2,1,0:T(8,128)S(1)} all-gather(f32[1,3,24,128]{3,2,1,0:T(8,128)S(1)} %get-tuple-element.59), channel_id=1, replica_groups={{0,1},{30,31},{2,4},{3,5},{6,8},{7,9},{10,12},{11,13},{14,16},{15,17},{..., dimensions={0}, use_global_device_ids=true | all-gather | bytes 110592 | tf_op jit(solution)/shard_map/all_gather | solution.py:493
  8.6 0.0 collective-permute-done.band0
  8.6 0.1 add_down.2
  8.7 0.3 collective-permute-start.1
  9.0 2.2 %collective-permute-done.1.rest_0_ = f32[8,128]{1,0:T(8,128)S(1)} collective-permute-done((f32[8,128]{1,0:T(8,128)S(1)}, f32[8,128]{1,0:T(8,128)S(1)}, u32[]{:S(2)}, u32[]{:S(2)}) %collective-permute-start.1) | collective-permute-done | bytes 4128 | tf_op jit(solution)/shard_map/ppermute | solution.py:490
  11.2 2.4 %gather.2 = (f32[12,136,128]{2,1,0:T(8,128)S(1)}, f32[160,128]{1,0:T(8,128)S(1)}, f32[160,128]{1,0:T(8,128)S(1)}, f32[160,128]{1,0:T(8,128)S(1)}) custom-call(s32[2,128]{1,0:T(2,128)S(1)} %get-tuple-element.33.anchor_down, s32[2,128]{1,0:T(2,128)S(1)} %get-tuple-element.34.anchor_cross, s32[2,4,13]{2,1,0:T(4,128)S(1)} %get-tuple-element.31.slots, ...), custom_call_target="tpu_custom_call" | custom-call | tf_op jit(solution)/shard_map/gather/pallas_call | solution.py:571
  13.6 1.7 %collective-permute-start.2 = (f32[160,128]{1,0:T(8,128)S(1)}, f32[160,128]{1,0:T(8,128)S(1)}, u32[]{:S(2)}, u32[]{:S(2)}) collective-permute-start(f32[160,128]{1,0:T(8,128)S(1)} %get-tuple-element.43), channel_id=1, source_target_pairs={{0,2},{2,0},{4,6},{6,4},{8,10},{10,8},{12,14},{14,12},{16,18},{18,... | collective-permute-start | bytes 245768 | tf_op jit(solution)/shard_map/ppermute | solution.py:490
  15.4 0.3 collective-permute-start.3
  15.6 5.4 %all-gather = f32[320,128]{1,0:T(8,128)S(1)} all-gather(f32[160,128]{1,0:T(8,128)S(1)} %get-tuple-element.44), channel_id=2, replica_groups={{0,1},{30,31},{2,4},{3,5},{6,8},{7,9},{10,12},{11,13},{14,16},{15,17},{..., dimensions={0}, use_global_device_ids=true | all-gather | bytes 245760 | tf_op jit(solution)/shard_map/all_gather | solution.py:493
  21.0 0.0 collective-permute-done.2.rest_0_
  21.0 0.0 collective-permute-done.3.rest_2_
  21.1 3.7 %scatter_next.1 = (f32[12,136,128]{2,1,0:T(8,128)S(1)}, f32[3,72,128]{2,1,0:T(8,128)S(1)}, f32[2,3,24,128]{3,2,1,0:T(8,128)S(1)}, bf16[128,32,256]{2,1,0:T(8,128)(2,1)S(1)}, f32[128,16,128]{2,1,0:T(8,128)S(1)}) custom-call(s32[2,128]{1,0:T(2,128)S(1)} %get-tuple-element.33.anchor_down, s32[2,128]{1,0:T(2,128)S(1)} %get-tuple-element.34.anchor_cross, ...), custom_call_target="tpu_custom_call" | custom-call | tf_op jit(solution)/shard_map/scatter_next/pallas_call | solution.py:555
  24.8 0.5 %collective-permute-start.4 = (f32[3,24,128]{2,1,0:T(8,128)S(1)}, f32[3,24,128]{2,1,0:T(8,128)S(1)}, u32[]{:S(2)}, u32[]{:S(2)}) collective-permute-start(f32[3,24,128]{2,1,0:T(8,128)S(1)} %get-tuple-element.58), channel_id=1, source_target_pairs={{0,2},{2,0},{4,6},{6,4},{8,10},{10,8},{12,14},{14,12},{16,18},{18,... | collective-permute-start | bytes 110600 | tf_op jit(solution)/shard_map/ppermute | solution.py:490
  25.3 4.6 %all_gather.21.band1 = f32[2,3,24,128]{3,2,1,0:T(8,128)S(1)} all-gather(f32[1,3,24,128]{3,2,1,0:T(8,128)S(1)} %get-tuple-element.57), channel_id=1, replica_groups={{0,1},{30,31},{2,4},{3,5},{6,8},{7,9},{10,12},{11,13},{14,16},{15,17},{..., dimensions={0}, use_global_device_ids=true | all-gather | bytes 110592 | tf_op jit(solution)/shard_map/all_gather | solution.py:493
  29.9 0.0 collective-permute-done.4.band0
  29.9 0.1 add_down.3
  30.0 1.2 %collective-permute-start.5 = (f32[8,128]{1,0:T(8,128)S(1)}, f32[8,128]{1,0:T(8,128)S(1)}, u32[]{:S(2)}, u32[]{:S(2)}) collective-permute-start(f32[8,128]{1,0:T(8,128)S(1)} %slice_bitcast_fusion.2), channel_id=1, source_target_pairs={{0,1},{1,0},{2,3},{3,2},{4,5},{5,4},{6,7},{7,6},{8,9},{9,8},{10,11... | collective-permute-start | bytes 12296 | tf_op jit(solution)/shard_map/ppermute | solution.py:490
  31.2 1.3 %collective-permute-done.5.rest_0_ = f32[8,128]{1,0:T(8,128)S(1)} collective-permute-done((f32[8,128]{1,0:T(8,128)S(1)}, f32[8,128]{1,0:T(8,128)S(1)}, u32[]{:S(2)}, u32[]{:S(2)}) %collective-permute-start.5) | collective-permute-done | bytes 4128 | tf_op jit(solution)/shard_map/ppermute | solution.py:490
  32.5 2.6 %gather.3 = (f32[12,136,128]{2,1,0:T(8,128)S(1)}, f32[160,128]{1,0:T(8,128)S(1)}, f32[160,128]{1,0:T(8,128)S(1)}, f32[160,128]{1,0:T(8,128)S(1)}) custom-call(s32[2,128]{1,0:T(2,128)S(1)} %get-tuple-element.33.anchor_down, s32[2,128]{1,0:T(2,128)S(1)} %get-tuple-element.34.anchor_cross, s32[2,4,13]{2,1,0:T(4,128)S(1)} %get-tuple-element.31.slots, ...), custom_call_target="tpu_custom_call" | custom-call | tf_op jit(solution)/shard_map/gather/pallas_call | solution.py:571
  35.0 1.7 %collective-permute-start.6 = (f32[160,128]{1,0:T(8,128)S(1)}, f32[160,128]{1,0:T(8,128)S(1)}, u32[]{:S(2)}, u32[]{:S(2)}) collective-permute-start(f32[160,128]{1,0:T(8,128)S(1)} %get-tuple-element.54), channel_id=1, source_target_pairs={{0,2},{2,0},{4,6},{6,4},{8,10},{10,8},{12,14},{14,12},{16,18},{18,... | collective-permute-start | bytes 245768 | tf_op jit(solution)/shard_map/ppermute | solution.py:490
  36.8 1.2 %collective-permute-start.7 = (f32[160,128]{1,0:T(8,128)S(1)}, f32[160,128]{1,0:T(8,128)S(1)}, u32[]{:S(2)}, u32[]{:S(2)}) collective-permute-start(f32[160,128]{1,0:T(8,128)S(1)} %get-tuple-element.56), channel_id=1, source_target_pairs={{0,1},{1,0},{2,3},{3,2},{4,5},{5,4},{6,7},{7,6},{8,9},{9,8},{10,11... | collective-permute-start | bytes 245768 | tf_op jit(solution)/shard_map/ppermute | solution.py:490
  38.0 5.4 %all-gather.1 = f32[320,128]{1,0:T(8,128)S(1)} all-gather(f32[160,128]{1,0:T(8,128)S(1)} %get-tuple-element.55), channel_id=3, replica_groups={{0,1},{30,31},{2,4},{3,5},{6,8},{7,9},{10,12},{11,13},{14,16},{15,17},{..., dimensions={0}, use_global_device_ids=true | all-gather | bytes 245760 | tf_op jit(solution)/shard_map/all_gather | solution.py:493
  43.4 0.0 collective-permute-done.6.rest_0_
  43.4 0.0 collective-permute-done.7.rest_2_
  43.4 2.3 %settle_last.1 = f32[12,128,128]{2,1,0:T(8,128)} custom-call(s32[2,4,13]{2,1,0:T(4,128)S(1)} %get-tuple-element.31.slots, s32[2,4]{1,0:T(2,128)S(1)} %get-tuple-element.32.counts, f32[12,136,128]{2,1,0:T(8,128)S(1)} %get-tuple-element.53.old, f32[160,128]{1,0:T(8,128)S(1)} %collective-permute-done.6.rest_0_, f32[2,160,128]{2,1,0:T(8,128)S(1)} %bitcast.14, ...), custom_call_target="tpu_custom_call" | custom-call | tf_op jit(solution)/shard_map/settle_last/pallas_call | solution.py:584
  (4 shorter events, 0.0 us)
Async XLA Ops:
  3.3 5.3 %collective-permute-start = (f32[3,24,128]{2,1,0:T(8,128)S(1)}, f32[3,24,128]{2,1,0:T(8,128)S(1)}, u32[]{:S(2)}, u32[]{:S(2)}) collective-permute-start(f32[3,24,128]{2,1,0:T(8,128)S(1)} %get-tuple-element.60), channel_id=1, source_target_pairs={{0,2},{2,0},{4,6},{6,4},{8,10},{10,8},{12,14},{14,12},{16,18},{18,... | collective-permute-start | bytes 110600 | tf_op jit(solution)/shard_map/ppermute | solution.py:490
  8.7 2.5 %collective-permute-start.1 = (f32[8,128]{1,0:T(8,128)S(1)}, f32[8,128]{1,0:T(8,128)S(1)}, u32[]{:S(2)}, u32[]{:S(2)}) collective-permute-start(f32[8,128]{1,0:T(8,128)S(1)} %slice_bitcast_fusion.3), channel_id=1, source_target_pairs={{0,1},{1,0},{2,3},{3,2},{4,5},{5,4},{6,7},{7,6},{8,9},{9,8},{10,11... | collective-permute-start | bytes 12296 | tf_op jit(solution)/shard_map/ppermute | solution.py:490
  13.6 7.4 %collective-permute-start.2 = (f32[160,128]{1,0:T(8,128)S(1)}, f32[160,128]{1,0:T(8,128)S(1)}, u32[]{:S(2)}, u32[]{:S(2)}) collective-permute-start(f32[160,128]{1,0:T(8,128)S(1)} %get-tuple-element.43), channel_id=1, source_target_pairs={{0,2},{2,0},{4,6},{6,4},{8,10},{10,8},{12,14},{14,12},{16,18},{18,... | collective-permute-start | bytes 245768 | tf_op jit(solution)/shard_map/ppermute | solution.py:490
  15.4 5.7 %collective-permute-start.3 = (f32[160,128]{1,0:T(8,128)S(1)}, f32[160,128]{1,0:T(8,128)S(1)}, u32[]{:S(2)}, u32[]{:S(2)}) collective-permute-start(f32[160,128]{1,0:T(8,128)S(1)} %get-tuple-element.45), channel_id=1, source_target_pairs={{0,1},{1,0},{2,3},{3,2},{4,5},{5,4},{6,7},{7,6},{8,9},{9,8},{10,11... | collective-permute-start | bytes 245768 | tf_op jit(solution)/shard_map/ppermute | solution.py:490
  24.8 5.1 %collective-permute-start.4 = (f32[3,24,128]{2,1,0:T(8,128)S(1)}, f32[3,24,128]{2,1,0:T(8,128)S(1)}, u32[]{:S(2)}, u32[]{:S(2)}) collective-permute-start(f32[3,24,128]{2,1,0:T(8,128)S(1)} %get-tuple-element.58), channel_id=1, source_target_pairs={{0,2},{2,0},{4,6},{6,4},{8,10},{10,8},{12,14},{14,12},{16,18},{18,... | collective-permute-start | bytes 110600 | tf_op jit(solution)/shard_map/ppermute | solution.py:490
  30.0 2.5 %collective-permute-start.5 = (f32[8,128]{1,0:T(8,128)S(1)}, f32[8,128]{1,0:T(8,128)S(1)}, u32[]{:S(2)}, u32[]{:S(2)}) collective-permute-start(f32[8,128]{1,0:T(8,128)S(1)} %slice_bitcast_fusion.2), channel_id=1, source_target_pairs={{0,1},{1,0},{2,3},{3,2},{4,5},{5,4},{6,7},{7,6},{8,9},{9,8},{10,11... | collective-permute-start | bytes 12296 | tf_op jit(solution)/shard_map/ppermute | solution.py:490
  35.0 8.3 %collective-permute-start.6 = (f32[160,128]{1,0:T(8,128)S(1)}, f32[160,128]{1,0:T(8,128)S(1)}, u32[]{:S(2)}, u32[]{:S(2)}) collective-permute-start(f32[160,128]{1,0:T(8,128)S(1)} %get-tuple-element.54), channel_id=1, source_target_pairs={{0,2},{2,0},{4,6},{6,4},{8,10},{10,8},{12,14},{14,12},{16,18},{18,... | collective-permute-start | bytes 245768 | tf_op jit(solution)/shard_map/ppermute | solution.py:490
  36.8 6.6 %collective-permute-start.7 = (f32[160,128]{1,0:T(8,128)S(1)}, f32[160,128]{1,0:T(8,128)S(1)}, u32[]{:S(2)}, u32[]{:S(2)}) collective-permute-start(f32[160,128]{1,0:T(8,128)S(1)} %get-tuple-element.56), channel_id=1, source_target_pairs={{0,1},{1,0},{2,3},{3,2},{4,5},{5,4},{6,7},{7,6},{8,9},{9,8},{10,11... | collective-permute-start | bytes 245768 | tf_op jit(solution)/shard_map/ppermute | solution.py:490

commit v4 on v3

--- a/solution.py
+++ b/solution.py
@@ -18,21 +18,22 @@
 MASS_FLOOR = 0.5
 FIELDS = 12
 LANES = 128
+HALF_BITS = 6
+HALF = 1 << HALF_BITS
 ROWS = 8
 CHANNELS = 3
 STRIDE = 32
 BAND = 2 * GHOST
 LOADS = 6
-GROUP = 64
+GROUP = 128
 VMEM_BYTES = 32 * 1024 * 1024
 
 
 def spline_pair(distance):
-    near = jnp.clip(distance, -0.5, 0.5)
-    far = jnp.clip(distance - near, -1.0, 1.0)
-    twice = near + near
-    slope = far - twice
-    return slope * slope + (1.5 - 1.5 * twice * twice), slope
+    reach = jnp.clip(distance, -1.5, 1.5)
+    near = jnp.clip(3.0 * distance, -1.5, 1.5)
+    slope = reach - near
+    return (slope * slope + 1.5) - (2.0 / 3.0) * (near * near), slope
 
 
 def low_part(x):
@@ -138,8 +139,8 @@
         lax.fori_loop(0, steps, several, 0)
 
 
-def window_place(anchor_down, anchor_cross, step):
-    return lambda b: (anchor_down[step, b] + GHOST, anchor_cross[step, b] + GHOST)
+def window_place(first, second, step, add=0):
+    return lambda b: (first[step, b] + add, second[step, b] + add)
 
 
 def write_grid(sums, grid, pay):
@@ -169,12 +170,15 @@
     pay,
     wide,
     tall,
-    anchor_down,
-    anchor_cross,
+    first_row,
+    first_col,
+    window_row,
+    window_turn,
     slots,
     counts,
     sums,
     loads,
+    table,
     down_scalar,
     cross_scalar,
     sems,
@@ -193,32 +197,43 @@
         )
         for k in range(parts)
     ]
-    others = [
-        pltpu.make_async_copy(src, dst, sems.at[2 + parts + k])
-        for k, (src, dst) in enumerate(
-            (
-                (down_in, anchor_down),
-                (cross_in, anchor_cross),
-                (slots_in, slots),
-                (counts_in, counts),
-            )
-        )
+    anchors = [
+        pltpu.make_async_copy(src, table.at[k], sems.at[2 + parts + k])
+        for k, src in enumerate((down_in, cross_in))
     ]
-    for copy in scalars + whole + others:
+    moves = [
+        pltpu.make_async_copy(src, dst, sems.at[4 + parts + k])
+        for k, (src, dst) in enumerate(((slots_in, slots), (counts_in, counts)))
+    ]
+    for copy in scalars + whole[:1] + anchors + whole[1:] + moves:
         copy.start()
     sums[...] = jnp.zeros_like(sums)
+    for copy in anchors:
+        copy.wait()
+    row = table[0] + GHOST
+    col = table[1] + GHOST
+    table[0] = row
+    table[1] = col
+    table[2] = (col >> HALF_BITS) * (2 * (TILE_DOWN + 2 * GHOST)) + row
+    table[3] = (LANES - (col & (HALF - 1))) & (LANES - 1)
+    tables = [
+        pltpu.make_async_copy(table.at[k], dst, sems.at[6 + parts + k])
+        for k, dst in enumerate((first_row, first_col, window_row, window_turn))
+    ]
+    for copy in tables:
+        copy.start()
     for copy in scalars:
         copy.wait()
-    place = window_place(down_scalar, cross_scalar, step)
+    place = window_place(down_scalar, cross_scalar, step, GHOST)
     for k in range(parts):
         whole[k].wait()
         particle_loads(state.at[:, pl.ds(k * size, size), :], loads.at[:, pl.ds(k * size, size), :], size)
         scatter_rows(
             state, loads, sums, (wide, tall), lambda m: m, place, k * size, size, min(GROUP, size)
         )
-    for copy in others:
+    write_grid(sums, grid, pay)
+    for copy in tables + moves:
         copy.wait()
-    write_grid(sums, grid, pay)
 
 
 def link_side(link):
@@ -227,13 +242,15 @@
     return 2 * axis + (1 - odd if second else odd)
 
 
-def settle(state, field, arrived, slots, counts, step, blocks):
+def settle(state, arrived, slots, counts, step, blocks):
     cap = slots.shape[2]
     for link, came in enumerate(arrived):
         side = link_side(link)
+        count = counts[step, side]
         for m in range(cap):
-            slot = jnp.where(m < counts[step, side], slots[step, side, m], blocks)
-            state[field, pl.ds(slot, 1), :] = came[field * cap + m : field * cap + m + 1, :]
+            slot = pl.ds(jnp.where(m < count, slots[step, side, m], blocks), 1)
+            for f in range(FIELDS):
+                state[f, slot, :] = came[f * cap + m : f * cap + m + 1, :]
 
 
 def pick_arrived(refs):
@@ -241,13 +258,12 @@
     return [ref.at[odd] if link == 1 else ref for link, ref in enumerate(refs)]
 
 
-def next_kernel(step, links, anchor_down, anchor_cross, slots, counts, old, *rest):
+def next_kernel(step, links, first_row, first_col, slots, counts, old, *rest):
     arrived = pick_arrived(rest[:links])
     state, grid, pay, wide, tall, sums, loads = rest[links:]
     blocks = loads.shape[1]
     state[:, :blocks, :] = old[:, :blocks, :]
-    for f in range(FIELDS):
-        settle(state, f, arrived, slots, counts, step - 1, blocks)
+    settle(state, arrived, slots, counts, step - 1, blocks)
     sums[...] = jnp.zeros_like(sums)
     particle_loads(state, loads, blocks)
     scatter_rows(
@@ -256,7 +272,7 @@
         sums,
         (wide, tall),
         lambda m: m,
-        window_place(anchor_down, anchor_cross, step),
+        window_place(first_row, first_col, step),
         0,
         blocks,
         min(GROUP, blocks),
@@ -264,7 +280,7 @@
     write_grid(sums, grid, pay)
 
 
-def gather_kernel(step, links, width, anchor_down, anchor_cross, slots, state, total, *rest):
+def gather_kernel(step, links, width, window_row, window_turn, slots, state, total, *rest):
     bands = rest[: links - 2]
     wide, tall, after = rest[links - 2 : links + 1]
     sent = rest[links + 1 : 2 * links + 1]
@@ -277,7 +293,7 @@
         speed,
         (wide, tall),
         lambda m: m,
-        window_place(anchor_down, anchor_cross, step),
+        window_place(window_row, window_turn, step),
         blocks,
         min(GROUP, blocks),
         after,
@@ -295,14 +311,11 @@
     arrived = pick_arrived(rest[:links])
     out, state, sems = rest[links:]
     blocks = out.shape[1]
-    copies = []
-    for f in range(FIELDS):
-        state[f, :blocks, :] = old[f, :blocks, :]
-        settle(state, f, arrived, slots, counts, step, blocks)
-        copies.append(pltpu.make_async_copy(state.at[f, pl.ds(0, blocks), :], out.at[f], sems.at[f]))
-        copies[-1].start()
-    for copy in copies:
-        copy.wait()
+    state[:, :blocks, :] = old[:, :blocks, :]
+    settle(state, arrived, slots, counts, step, blocks)
+    copy = pltpu.make_async_copy(state.at[:, pl.ds(0, blocks), :], out, sems.at[0])
+    copy.start()
+    copy.wait()
 
 
 def cross_kernel(width, grid, band0, band1, total, pay):
@@ -357,13 +370,20 @@
     total_rows = tile_down * lax.axis_size("down")
     total_cols = tile_cross * lax.axis_size("cross")
     keep_rows = (row_global > 0) & (row_global < total_rows - 1)
+    halves = speed.shape[0] // (2 * height)
+    lane = lax.broadcasted_iota(jnp.int32, (2 * height, LANES), 1)
+    before = None
     for t in range(tiles):
         col_global = col_first + (lax.axis_index("cross") * tile_cross + t * LANES)
         kept = keep_rows & (col_global > 0) & (col_global < total_cols - 1)
-        mass = jnp.maximum(total[t, :height, :], MASS_FLOOR)
-        for c in range(2):
-            value = total[t, (c + 1) * height : (c + 2) * height, :] / mass
-            speed[t, c] = jnp.where(kept, value, 0.0)
+        factor = jnp.where(kept, 1.0 / jnp.maximum(total[t, :height, :], MASS_FLOOR), 0.0)
+        value = total[t, height:, :] * jnp.concatenate([factor, factor], axis=0)
+        turned = pltpu.roll(value, HALF, 1)
+        if 2 * t < halves:
+            speed[4 * t * height : (4 * t + 2) * height, :] = value
+        if t and 2 * t - 1 < halves:
+            speed[(4 * t - 2) * height : 4 * t * height, :] = jnp.where(lane < HALF, before, turned)
+        before = turned
 
 
 def row_sums(terms, row):
@@ -385,18 +405,14 @@
     )
 
 
-def gather_terms(weights, speed, slot, first_row, first_col, lane):
-    tile = first_col // LANES
-    shift = first_col - tile * LANES
-    spot = pl.ds(first_row, WIN_DOWN)
-    here = jnp.concatenate([speed[tile, 0, spot, :], speed[tile, 1, spot, :]], axis=0)
-    after = jnp.concatenate([speed[tile + 1, 0, spot, :], speed[tile + 1, 1, spot, :]], axis=0)
-    window = jnp.where(lane >= shift, here, after)
-    window = jnp.where(
-        lane < WIN_CROSS,
-        pltpu.roll(window, (LANES - shift) & (LANES - 1), 1),
-        pltpu.roll(window, (WIN_CROSS + LANES - shift) & (LANES - 1), 1),
-    )
+def gather_terms(weights, speed, slot, window_row, window_turn, lane):
+    height = TILE_DOWN + 2 * GHOST
+    window = jnp.concatenate(
+        [speed[pl.ds(window_row, WIN_DOWN), :], speed[pl.ds(window_row + height, WIN_DOWN), :]],
+        axis=0,
+    )
+    window = pltpu.roll(window, window_turn, 1)
+    window = jnp.where(lane < WIN_CROSS, window, pltpu.roll(window, WIN_CROSS, 1))
     window = jnp.concatenate([window, low_part(window)], axis=0).astype(jnp.bfloat16)
     found = jnp.dot(
         window[:, : 2 * WIN_CROSS], weights[0][slot], preferred_element_type=jnp.float32
@@ -425,8 +441,7 @@
             terms = []
             for k in range(ROWS):
                 slot = slot_of(base + k)
-                first_row, first_col = place(slot)
-                terms.append(gather_terms(weights, speed, slot, first_row, first_col, lane))
+                terms.append(gather_terms(weights, speed, slot, *place(slot), lane))
             vel_d, vel_c, l_dd, l_cd, l_dc, l_cc = (row_sums(t, row) for t in zip(*terms))
             vel_d, vel_c = 0.25 * vel_d, 0.25 * vel_c
             l_dd, l_cc = 0.5 * l_dd, 0.5 * l_cc
@@ -499,7 +514,7 @@
             kernel,
             out_shape=outs,
             in_specs=in_specs,
-            out_specs=tuple(hbm if isinstance(x, pl.MemoryRef) else vmem for x in outs),
+            out_specs=tuple(pl.BlockSpec(memory_space=x.memory_space) if isinstance(x, pl.MemoryRef) else vmem for x in outs),
             scratch_shapes=scratch,
             compiler_params=pltpu.CompilerParams(vmem_limit_bytes=VMEM_BYTES),
             name=name,
@@ -511,6 +526,7 @@
         height = TILE_DOWN + 2 * GHOST
         width = TILE_CROSS + 2 * GHOST
         tiles = -(-width // LANES)
+        halves = (width - WIN_CROSS) // HALF + 1
 
         def array(*shape, dtype=f32):
             return jax.ShapeDtypeStruct(shape, dtype)
@@ -534,22 +550,25 @@
             move_count.reshape(STEPS, 4),
         )
         given = ints + (jnp.transpose(particles, (1, 0, 2)),)
-        parts = 2
+        parts = 1
         state, grid, pay, *rest = call(
             "scatter_first",
             functools.partial(first_kernel, 0, parts),
             (state_type, grid_type, band_type)
             + weight_types
-            + tuple(array(*x.shape, dtype=x.dtype) for x in ints),
+            + tuple(pltpu.SMEM(x.shape, x.dtype) for x in ints[:2] * 2 + ints[2:]),
             [hbm] * 5,
             scatter_scratch
             + [
+                pltpu.VMEM((4,) + anchor_down.shape, jnp.int32),
                 pltpu.SMEM(anchor_down.shape, jnp.int32),
                 pltpu.SMEM(anchor_cross.shape, jnp.int32),
-                pltpu.SemaphoreType.DMA((6 + parts,)),
+                pltpu.SemaphoreType.DMA((10 + parts,)),
             ],
         )(*(pltpu.with_memory_space_constraint(x, pltpu.HBM) for x in given))
-        weights, ints = rest[:2], rest[2:]
+        weights = rest[:2]
+        rest = [pltpu.with_memory_space_constraint(x, pltpu.SMEM) for x in rest[2:]]
+        windows, moves = rest[:4], rest[4:]
         for step in range(STEPS):
             if step:
                 state, grid, pay, *weights = call(
@@ -558,7 +577,7 @@
                     (state_type, grid_type, band_type) + weight_types,
                     [smem] * 4 + [vmem] * (links + 1),
                     scatter_scratch,
-                )(*ints, state, *arrived)
+                )(*windows[:2], *moves, state, *arrived)
             band0 = swap(pay[0], 0)
             band1 = gather_pairs(pay[1])
             total, pay = call(
@@ -574,10 +593,10 @@
                 (state_type,) + (sent_type,) * links,
                 [smem] * 3 + [vmem] * (2 + links),
                 [
-                    pltpu.VMEM((tiles, 2, height, LANES), f32),
+                    pltpu.VMEM((halves * 2 * height, LANES), f32),
                     pltpu.VMEM(grid_type.shape, f32),
                 ],
-            )(*ints[:3], state, total, *bands, *weights)
+            )(*windows[2:], moves[0], state, total, *bands, *weights)
             arrived = [
                 gather_pairs(x) if link == 1 else swap(x, link) for link, x in enumerate(sent)
             ]
@@ -586,8 +605,8 @@
             functools.partial(last_kernel, STEPS - 1, links),
             (pltpu.HBM((FIELDS, blocks, LANES), f32),),
             [smem] * 2 + [vmem] * (links + 1),
-            [pltpu.VMEM(state_type.shape, f32), pltpu.SemaphoreType.DMA((FIELDS,))],
-        )(*ints[2:], state, *arrived)
+            [pltpu.VMEM(state_type.shape, f32), pltpu.SemaphoreType.DMA((1,))],
+        )(*moves, state, *arrived)
         return jnp.transpose(state, (1, 0, 2))
 
     return jax.shard_map(

time: 45.9 us -> 41.7 us (0.908)
  Pallas kernels: 14.5 us -> 10.2 us
    pallas_call x1, Pallas kernels: 3.69 us -> 2.15 us  [on_device(): call('scatter_next', functools.partial(next_kernel, step, links), (state_...]
    pallas_call x2, Pallas kernels: 5 us -> 3.62 us  [on_device(): call('gather', functools.partial(gather_kernel, step, links, width), (sta...]
    pallas_call x1, Pallas kernels: 2.35 us -> 1.11 us  [on_device(): call('settle_last', functools.partial(last_kernel, STEPS - 1, links), (pl...]
where the time goes in v4:
time: 41.7 us; the launch traced here: 41.5 us
  blocking collectives  20 us (48%)
  Pallas kernels  10.2 us (24%)
  starting transfers between devices  7.75 us (19%)
  waiting for transfers between devices  3.45 us (8%)
    all_gather x4, blocking collectives, gather_pairs(): lax.all_gather(x, ('down', 'cross'), axis_index_groups=odd_groups(size_do...  20 us
    ppermute x8, starting transfers between devices, swap(): return lax.ppermute(x, name, swap_pairs(size, second))  7.75 us
    pallas_call x2, Pallas kernels, on_device(): call('gather', functools.partial(gather_kernel, step, links, width), (sta...  3.62 us
    ppermute x8, waiting for transfers between devices, swap(): return lax.ppermute(x, name, swap_pairs(size, second))  3.45 us
    pallas_call x1, Pallas kernels, on_device(): call('scatter_first', functools.partial(first_kernel, 0, parts), (state_t...  3.2 us
    pallas_call x1, Pallas kernels, on_device(): call('scatter_next', functools.partial(next_kernel, step, links), (state_...  2.15 us
    pallas_call x1, Pallas kernels, on_device(): call('settle_last', functools.partial(last_kernel, STEPS - 1, links), (pl...  1.11 us
  transfers between devices with their start and end apart: 8, of which 2 were waited for; matrix products, arithmetic and copies ran while one was open for 0% of the time, Pallas kernels for 0%

profile of v4, /device:TPU:11, one launch (start us, length us, event | category | flops | bytes accessed | tf_op | source)
XLA Modules:
  0.0 41.5 jit_solution(6268481203751601428)
XLA Ops:
  0.0 3.2 %scatter_first.1 = (f32[12,136,128]{2,1,0:T(8,128)S(1)}, f32[3,72,128]{2,1,0:T(8,128)S(1)}, f32[2,3,24,128]{3,2,1,0:T(8,128)S(1)}, bf16[128,32,256]{2,1,0:T(8,12...) custom-call(s32[2,128]{1,0:T(2,128)} %down_in.1, ...), custom_call_target="tpu_custom_call" | custom-call | tf_op jit(solution)/shard_map/scatter_first/pallas_call | solution.py:554
  3.2 0.7 %collective-permute-start = (f32[3,24,128]{2,1,0:T(8,128)S(1)}, f32[3,24,128]{2,1,0:T(8,128)S(1)}, u32[]{:S(2)}, u32[]{:S(2)}) collective-permute-start(f32[3,24,128]{2,1,0:T(8,128)S(1)} %get-tuple-element.64), channel_id=1, source_target_pairs={{0,2},{2,0},{4,6},{6,4},{8,10},{10,8},{12,14},{14,12},{16,18},{18,... | collective-permute-start | bytes 110600 | tf_op jit(solution)/shard_map/ppermute | solution.py:505
  4.0 4.6 %all_gather.18.band1 = f32[2,3,24,128]{3,2,1,0:T(8,128)S(1)} all-gather(f32[1,3,24,128]{3,2,1,0:T(8,128)S(1)} %get-tuple-element.63), channel_id=1, replica_groups={{0,1},{30,31},{2,4},{3,5},{6,8},{7,9},{10,12},{11,13},{14,16},{15,17},{..., dimensions={0}, use_global_device_ids=true | all-gather | bytes 110592 | tf_op jit(solution)/shard_map/all_gather | solution.py:508
  8.6 0.0 collective-permute-done.band0
  8.6 0.1 add_down.2
  8.6 0.3 collective-permute-start.1
  8.9 2.2 %collective-permute-done.1.rest_0_ = f32[8,128]{1,0:T(8,128)S(1)} collective-permute-done((f32[8,128]{1,0:T(8,128)S(1)}, f32[8,128]{1,0:T(8,128)S(1)}, u32[]{:S(2)}, u32[]{:S(2)}) %collective-permute-start.1) | collective-permute-done | bytes 4128 | tf_op jit(solution)/shard_map/ppermute | solution.py:505
  11.1 1.8 %gather.2 = (f32[12,136,128]{2,1,0:T(8,128)S(1)}, f32[160,128]{1,0:T(8,128)S(1)}, f32[160,128]{1,0:T(8,128)S(1)}, f32[160,128]{1,0:T(8,128)S(1)}) custom-call(s32[2,128]{1,0:T(2,128)S(4)} %get-tuple-element.35.window_row, s32[2,128]{1,0:T(2,128)S(4)} %get-tuple-element.36.window_turn, s32[2,4,13]{2,1,0:T(4,128)S(4)} %get-tuple-element.33.slots, ...), custom_call_target="tpu_custom_call" | custom-call | tf_op jit(solution)/shard_map/gather/pallas_call | solution.py:590
  12.9 1.7 %collective-permute-start.2 = (f32[160,128]{1,0:T(8,128)S(1)}, f32[160,128]{1,0:T(8,128)S(1)}, u32[]{:S(2)}, u32[]{:S(2)}) collective-permute-start(f32[160,128]{1,0:T(8,128)S(1)} %get-tuple-element.47), channel_id=1, source_target_pairs={{0,2},{2,0},{4,6},{6,4},{8,10},{10,8},{12,14},{14,12},{16,18},{18,... | collective-permute-start | bytes 245768 | tf_op jit(solution)/shard_map/ppermute | solution.py:505
  14.7 0.3 collective-permute-start.3
  14.9 5.4 %all-gather = f32[320,128]{1,0:T(8,128)S(1)} all-gather(f32[160,128]{1,0:T(8,128)S(1)} %get-tuple-element.48), channel_id=2, replica_groups={{0,1},{30,31},{2,4},{3,5},{6,8},{7,9},{10,12},{11,13},{14,16},{15,17},{..., dimensions={0}, use_global_device_ids=true | all-gather | bytes 245760 | tf_op jit(solution)/shard_map/all_gather | solution.py:508
  20.3 0.0 collective-permute-done.2.rest_0_
  20.3 0.0 collective-permute-done.3.rest_2_
  20.3 2.1 %scatter_next.1 = (f32[12,136,128]{2,1,0:T(8,128)S(1)}, f32[3,72,128]{2,1,0:T(8,128)S(1)}, f32[2,3,24,128]{3,2,1,0:T(8,128)S(1)}, bf16[128,32,256]{2,1,0:T(8,128)(2,1)S(1)}, f32[128,16,128]{2,1,0:T(8,128)S(1)}) custom-call(s32[2,128]{1,0:T(2,128)S(4)} %get-tuple-element.37.first_row, s32[2,128]{1,0:T(2,128)S(4)} %get-tuple-element.38.first_col, ...), custom_call_target="tpu_custom_call" | custom-call | tf_op jit(solution)/shard_map/scatter_next/pallas_call | solution.py:574
  22.5 0.5 %collective-permute-start.4 = (f32[3,24,128]{2,1,0:T(8,128)S(1)}, f32[3,24,128]{2,1,0:T(8,128)S(1)}, u32[]{:S(2)}, u32[]{:S(2)}) collective-permute-start(f32[3,24,128]{2,1,0:T(8,128)S(1)} %get-tuple-element.62), channel_id=1, source_target_pairs={{0,2},{2,0},{4,6},{6,4},{8,10},{10,8},{12,14},{14,12},{16,18},{18,... | collective-permute-start | bytes 110600 | tf_op jit(solution)/shard_map/ppermute | solution.py:505
  23.0 4.6 %all_gather.21.band1 = f32[2,3,24,128]{3,2,1,0:T(8,128)S(1)} all-gather(f32[1,3,24,128]{3,2,1,0:T(8,128)S(1)} %get-tuple-element.61), channel_id=1, replica_groups={{0,1},{30,31},{2,4},{3,5},{6,8},{7,9},{10,12},{11,13},{14,16},{15,17},{..., dimensions={0}, use_global_device_ids=true | all-gather | bytes 110592 | tf_op jit(solution)/shard_map/all_gather | solution.py:508
  27.6 0.0 collective-permute-done.4.band0
  27.6 0.1 add_down.3
  27.7 1.3 %collective-permute-start.5 = (f32[8,128]{1,0:T(8,128)S(1)}, f32[8,128]{1,0:T(8,128)S(1)}, u32[]{:S(2)}, u32[]{:S(2)}) collective-permute-start(f32[8,128]{1,0:T(8,128)S(1)} %slice_bitcast_fusion.2), channel_id=1, source_target_pairs={{0,1},{1,0},{2,3},{3,2},{4,5},{5,4},{6,7},{7,6},{8,9},{9,8},{10,11... | collective-permute-start | bytes 12296 | tf_op jit(solution)/shard_map/ppermute | solution.py:505
  29.0 1.2 %collective-permute-done.5.rest_0_ = f32[8,128]{1,0:T(8,128)S(1)} collective-permute-done((f32[8,128]{1,0:T(8,128)S(1)}, f32[8,128]{1,0:T(8,128)S(1)}, u32[]{:S(2)}, u32[]{:S(2)}) %collective-permute-start.5) | collective-permute-done | bytes 4128 | tf_op jit(solution)/shard_map/ppermute | solution.py:505
  30.2 1.8 %gather.3 = (f32[12,136,128]{2,1,0:T(8,128)S(1)}, f32[160,128]{1,0:T(8,128)S(1)}, f32[160,128]{1,0:T(8,128)S(1)}, f32[160,128]{1,0:T(8,128)S(1)}) custom-call(s32[2,128]{1,0:T(2,128)S(4)} %get-tuple-element.35.window_row, s32[2,128]{1,0:T(2,128)S(4)} %get-tuple-element.36.window_turn, s32[2,4,13]{2,1,0:T(4,128)S(4)} %get-tuple-element.33.slots, ...), custom_call_target="tpu_custom_call" | custom-call | tf_op jit(solution)/shard_map/gather/pallas_call | solution.py:590
  32.0 1.7 %collective-permute-start.6 = (f32[160,128]{1,0:T(8,128)S(1)}, f32[160,128]{1,0:T(8,128)S(1)}, u32[]{:S(2)}, u32[]{:S(2)}) collective-permute-start(f32[160,128]{1,0:T(8,128)S(1)} %get-tuple-element.58), channel_id=1, source_target_pairs={{0,2},{2,0},{4,6},{6,4},{8,10},{10,8},{12,14},{14,12},{16,18},{18,... | collective-permute-start | bytes 245768 | tf_op jit(solution)/shard_map/ppermute | solution.py:505
  33.7 1.2 %collective-permute-start.7 = (f32[160,128]{1,0:T(8,128)S(1)}, f32[160,128]{1,0:T(8,128)S(1)}, u32[]{:S(2)}, u32[]{:S(2)}) collective-permute-start(f32[160,128]{1,0:T(8,128)S(1)} %get-tuple-element.60), channel_id=1, source_target_pairs={{0,1},{1,0},{2,3},{3,2},{4,5},{5,4},{6,7},{7,6},{8,9},{9,8},{10,11... | collective-permute-start | bytes 245768 | tf_op jit(solution)/shard_map/ppermute | solution.py:505
  35.0 5.4 %all-gather.1 = f32[320,128]{1,0:T(8,128)S(1)} all-gather(f32[160,128]{1,0:T(8,128)S(1)} %get-tuple-element.59), channel_id=3, replica_groups={{0,1},{30,31},{2,4},{3,5},{6,8},{7,9},{10,12},{11,13},{14,16},{15,17},{..., dimensions={0}, use_global_device_ids=true | all-gather | bytes 245760 | tf_op jit(solution)/shard_map/all_gather | solution.py:508
  40.4 0.0 collective-permute-done.6.rest_0_
  40.4 0.0 collective-permute-done.7.rest_2_
  40.4 1.1 %settle_last.1 = f32[12,128,128]{2,1,0:T(8,128)} custom-call(s32[2,4,13]{2,1,0:T(4,128)S(4)} %get-tuple-element.33.slots, s32[2,4]{1,0:T(2,128)S(4)} %get-tuple-element.34.counts, f32[12,136,128]{2,1,0:T(8,128)S(1)} %get-tuple-element.57.old, f32[160,128]{1,0:T(8,128)S(1)} %collective-permute-done.6.rest_0_, f32[2,160,128]{2,1,0:T(8,128)S(1)} %bitcast.14, ...), custom_call_target="tpu_custom_call" | custom-call | tf_op jit(solution)/shard_map/settle_last/pallas_call | solution.py:603
  (4 shorter events, 0.0 us)
Async XLA Ops:
  3.2 5.3 %collective-permute-start = (f32[3,24,128]{2,1,0:T(8,128)S(1)}, f32[3,24,128]{2,1,0:T(8,128)S(1)}, u32[]{:S(2)}, u32[]{:S(2)}) collective-permute-start(f32[3,24,128]{2,1,0:T(8,128)S(1)} %get-tuple-element.64), channel_id=1, source_target_pairs={{0,2},{2,0},{4,6},{6,4},{8,10},{10,8},{12,14},{14,12},{16,18},{18,... | collective-permute-start | bytes 110600 | tf_op jit(solution)/shard_map/ppermute | solution.py:505
  8.6 2.5 %collective-permute-start.1 = (f32[8,128]{1,0:T(8,128)S(1)}, f32[8,128]{1,0:T(8,128)S(1)}, u32[]{:S(2)}, u32[]{:S(2)}) collective-permute-start(f32[8,128]{1,0:T(8,128)S(1)} %slice_bitcast_fusion.3), channel_id=1, source_target_pairs={{0,1},{1,0},{2,3},{3,2},{4,5},{5,4},{6,7},{7,6},{8,9},{9,8},{10,11... | collective-permute-start | bytes 12296 | tf_op jit(solution)/shard_map/ppermute | solution.py:505
  12.9 7.4 %collective-permute-start.2 = (f32[160,128]{1,0:T(8,128)S(1)}, f32[160,128]{1,0:T(8,128)S(1)}, u32[]{:S(2)}, u32[]{:S(2)}) collective-permute-start(f32[160,128]{1,0:T(8,128)S(1)} %get-tuple-element.47), channel_id=1, source_target_pairs={{0,2},{2,0},{4,6},{6,4},{8,10},{10,8},{12,14},{14,12},{16,18},{18,... | collective-permute-start | bytes 245768 | tf_op jit(solution)/shard_map/ppermute | solution.py:505
  14.7 5.7 %collective-permute-start.3 = (f32[160,128]{1,0:T(8,128)S(1)}, f32[160,128]{1,0:T(8,128)S(1)}, u32[]{:S(2)}, u32[]{:S(2)}) collective-permute-start(f32[160,128]{1,0:T(8,128)S(1)} %get-tuple-element.49), channel_id=1, source_target_pairs={{0,1},{1,0},{2,3},{3,2},{4,5},{5,4},{6,7},{7,6},{8,9},{9,8},{10,11... | collective-permute-start | bytes 245768 | tf_op jit(solution)/shard_map/ppermute | solution.py:505
  22.5 5.1 %collective-permute-start.4 = (f32[3,24,128]{2,1,0:T(8,128)S(1)}, f32[3,24,128]{2,1,0:T(8,128)S(1)}, u32[]{:S(2)}, u32[]{:S(2)}) collective-permute-start(f32[3,24,128]{2,1,0:T(8,128)S(1)} %get-tuple-element.62), channel_id=1, source_target_pairs={{0,2},{2,0},{4,6},{6,4},{8,10},{10,8},{12,14},{14,12},{16,18},{18,... | collective-permute-start | bytes 110600 | tf_op jit(solution)/shard_map/ppermute | solution.py:505
  27.7 2.5 %collective-permute-start.5 = (f32[8,128]{1,0:T(8,128)S(1)}, f32[8,128]{1,0:T(8,128)S(1)}, u32[]{:S(2)}, u32[]{:S(2)}) collective-permute-start(f32[8,128]{1,0:T(8,128)S(1)} %slice_bitcast_fusion.2), channel_id=1, source_target_pairs={{0,1},{1,0},{2,3},{3,2},{4,5},{5,4},{6,7},{7,6},{8,9},{9,8},{10,11... | collective-permute-start | bytes 12296 | tf_op jit(solution)/shard_map/ppermute | solution.py:505
  32.0 8.4 %collective-permute-start.6 = (f32[160,128]{1,0:T(8,128)S(1)}, f32[160,128]{1,0:T(8,128)S(1)}, u32[]{:S(2)}, u32[]{:S(2)}) collective-permute-start(f32[160,128]{1,0:T(8,128)S(1)} %get-tuple-element.58), channel_id=1, source_target_pairs={{0,2},{2,0},{4,6},{6,4},{8,10},{10,8},{12,14},{14,12},{16,18},{18,... | collective-permute-start | bytes 245768 | tf_op jit(solution)/shard_map/ppermute | solution.py:505
  33.7 6.7 %collective-permute-start.7 = (f32[160,128]{1,0:T(8,128)S(1)}, f32[160,128]{1,0:T(8,128)S(1)}, u32[]{:S(2)}, u32[]{:S(2)}) collective-permute-start(f32[160,128]{1,0:T(8,128)S(1)} %get-tuple-element.60), channel_id=1, source_target_pairs={{0,1},{1,0},{2,3},{3,2},{4,5},{5,4},{6,7},{7,6},{8,9},{9,8},{10,11... | collective-permute-start | bytes 245768 | tf_op jit(solution)/shard_map/ppermute | solution.py:505

commit v5 on v4

--- a/solution.py
+++ b/solution.py
@@ -105,38 +105,44 @@
     sums[spot, :] = sums[spot, :] + found
 
 
-def scatter_rows(state, loads, sums, weights, slot_of, place, first, count, group):
+def edge_limits(width):
+    index = lax.axis_index("cross")
+    low = jnp.where(index > 0, BAND, 0)
+    high = jnp.where(index < lax.axis_size("cross") - 1, width - BAND - WIN_CROSS, width)
+    return low, high
+
+
+def scatter_rows(state, loads, sums, weights, place, blocks, group, edge, limits):
     rows = node_rows(WIN_DOWN)
     cols = node_rows(WIN_CROSS)
     lane = lax.broadcasted_iota(jnp.int32, (WIN_CROSS, LANES), 1)
     inside = (lane & (STRIDE - 1)) < WIN_DOWN
 
-    def several(q, carry):
+    def several(q, listed):
         for k in range(group):
-            m = first + q * group + k
+            m = q * group + k
             row = pl.ds(m, 1)
-            slot = slot_of(m)
-            first_row, first_col = place(slot)
+            first_row, first_col = place(m)
+            edge[listed] = m
+            at_edge = (first_col < limits[0]) | (first_col > limits[1])
+            listed = listed + at_edge.astype(jnp.int32)
             scatter_block(
                 state[0, row, :],
                 state[1, row, :],
                 lambda f, row=row: loads[f, row, :],
                 sums,
                 weights,
-                slot,
+                m,
                 first_row,
                 first_col,
                 rows,
                 cols,
                 inside,
             )
-        return carry
-
-    steps = count // group
-    if steps == 1:
-        several(0, 0)
-    else:
-        lax.fori_loop(0, steps, several, 0)
+        return listed
+
+    steps = blocks // group
+    edge[blocks] = several(0, 0) if steps == 1 else lax.fori_loop(0, steps, several, 0)
 
 
 def window_place(first, second, step, add=0):
@@ -159,7 +165,7 @@
 
 def first_kernel(
     step,
-    parts,
+    width,
     down_in,
     cross_in,
     slots_in,
@@ -176,6 +182,7 @@
     window_turn,
     slots,
     counts,
+    edge,
     sums,
     loads,
     table,
@@ -184,28 +191,20 @@
     sems,
 ):
     blocks = particles.shape[1]
-    size = blocks // parts
     scalars = [
         pltpu.make_async_copy(src, dst, sems.at[k])
         for k, (src, dst) in enumerate(((down_in, down_scalar), (cross_in, cross_scalar)))
     ]
-    whole = [
-        pltpu.make_async_copy(
-            particles.at[:, pl.ds(k * size, size), :],
-            state.at[:, pl.ds(k * size, size), :],
-            sems.at[2 + k],
-        )
-        for k in range(parts)
-    ]
+    whole = pltpu.make_async_copy(particles, state.at[:, pl.ds(0, blocks), :], sems.at[2])
     anchors = [
-        pltpu.make_async_copy(src, table.at[k], sems.at[2 + parts + k])
+        pltpu.make_async_copy(src, table.at[k], sems.at[3 + k])
         for k, src in enumerate((down_in, cross_in))
     ]
     moves = [
-        pltpu.make_async_copy(src, dst, sems.at[4 + parts + k])
+        pltpu.make_async_copy(src, dst, sems.at[5 + k])
         for k, (src, dst) in enumerate(((slots_in, slots), (counts_in, counts)))
     ]
-    for copy in scalars + whole[:1] + anchors + whole[1:] + moves:
+    for copy in scalars + [whole] + anchors + moves:
         copy.start()
     sums[...] = jnp.zeros_like(sums)
     for copy in anchors:
@@ -217,7 +216,7 @@
     table[2] = (col >> HALF_BITS) * (2 * (TILE_DOWN + 2 * GHOST)) + row
     table[3] = (LANES - (col & (HALF - 1))) & (LANES - 1)
     tables = [
-        pltpu.make_async_copy(table.at[k], dst, sems.at[6 + parts + k])
+        pltpu.make_async_copy(table.at[k], dst, sems.at[7 + k])
         for k, dst in enumerate((first_row, first_col, window_row, window_turn))
     ]
     for copy in tables:
@@ -225,12 +224,11 @@
     for copy in scalars:
         copy.wait()
     place = window_place(down_scalar, cross_scalar, step, GHOST)
-    for k in range(parts):
-        whole[k].wait()
-        particle_loads(state.at[:, pl.ds(k * size, size), :], loads.at[:, pl.ds(k * size, size), :], size)
-        scatter_rows(
-            state, loads, sums, (wide, tall), lambda m: m, place, k * size, size, min(GROUP, size)
-        )
+    whole.wait()
+    particle_loads(state, loads, blocks)
+    scatter_rows(
+        state, loads, sums, (wide, tall), place, blocks, GROUP, edge, edge_limits(width)
+    )
     write_grid(sums, grid, pay)
     for copy in tables + moves:
         copy.wait()
@@ -258,9 +256,9 @@
     return [ref.at[odd] if link == 1 else ref for link, ref in enumerate(refs)]
 
 
-def next_kernel(step, links, first_row, first_col, slots, counts, old, *rest):
+def next_kernel(step, links, width, first_row, first_col, slots, counts, old, *rest):
     arrived = pick_arrived(rest[:links])
-    state, grid, pay, wide, tall, sums, loads = rest[links:]
+    state, grid, pay, wide, tall, edge, sums, loads = rest[links:]
     blocks = loads.shape[1]
     state[:, :blocks, :] = old[:, :blocks, :]
     settle(state, arrived, slots, counts, step - 1, blocks)
@@ -271,11 +269,11 @@
         loads,
         sums,
         (wide, tall),
-        lambda m: m,
         window_place(first_row, first_col, step),
-        0,
         blocks,
-        min(GROUP, blocks),
+        GROUP,
+        edge,
+        edge_limits(width),
     )
     write_grid(sums, grid, pay)
 
@@ -347,18 +345,23 @@
     pay[1 - odd] = jnp.transpose(jnp.concatenate([total[0], pad], axis=0))[:BAND]
 
 
-def node_velocity(total, bands, speed, width):
+def add_across(total, bands, sums, width):
     tiles, rows, _ = total.shape
-    height = rows // CHANNELS
+    sums[...] = total[...]
     odd = lax.rem(lax.axis_index("cross"), 2)
     tile, lane = divmod(width - BAND, LANES)
     pad = jnp.zeros((LANES - BAND, LANES), jnp.float32)
     for link, came in enumerate(bands):
         band = jnp.transpose(jnp.concatenate([came[...], pad], axis=0))[:rows]
         at_first = odd if link == 0 else 1 - odd
-        total[0] = total[0] + jnp.where(at_first == 1, band, 0.0)
+        sums[0] = sums[0] + jnp.where(at_first == 1, band, 0.0)
         shifted = pltpu.roll(band, lane, 1) if lane else band
-        total[tile] = total[tile] + jnp.where(at_first == 0, shifted, 0.0)
+        sums[tile] = sums[tile] + jnp.where(at_first == 0, shifted, 0.0)
+
+
+def node_velocity(total, speed, width):
+    tiles, rows, _ = total.shape
+    height = rows // CHANNELS
     tile_down = height - 2 * GHOST
     tile_cross = width - 2 * GHOST
     row_global = (
@@ -431,48 +434,94 @@
     )
 
 
-def gather_rows(state, speed, weights, slot_of, place, blocks, group, out):
+def gather_eight(weights, speed, slots, place, field, lane, row):
+    terms = [gather_terms(weights, speed, slot, *place(slot), lane) for slot in slots]
+    vel_d, vel_c, l_dd, l_cd, l_dc, l_cc = (row_sums(t, row) for t in zip(*terms))
+    vel_d, vel_c = 0.25 * vel_d, 0.25 * vel_c
+    l_dd, l_cc = 0.5 * l_dd, 0.5 * l_cc
+    rate_dc = 0.25 * (l_dc + l_cd)
+    trace = l_dd + l_cc
+    shear = (2.0 * TIME_STEP) * field[9]
+    spread = (TIME_STEP * field[10]) * trace
+    stretch = TIME_STEP * trace
+    return {
+        0: jnp.clip(field[0] + TIME_STEP * vel_d, 0.5, WIN_DOWN - 1.5),
+        1: jnp.clip(field[1] + TIME_STEP * vel_c, 0.5, WIN_CROSS - 1.5),
+        2: vel_d,
+        3: vel_c,
+        4: field[4] + (spread + shear * l_dd),
+        5: field[5] + shear * rate_dc,
+        6: field[6] + (spread + shear * l_cc),
+        8: field[8] + field[8] * stretch,
+        11: field[11] + TIME_STEP * (l_dd * l_dd + l_cc * l_cc + 2.0 * rate_dc * rate_dc),
+    }
+
+
+def gather_lanes():
     lane = lax.broadcasted_iota(jnp.int32, (2 * WIN_DOWN, LANES), 1)
     row = lax.broadcasted_iota(jnp.int32, (ROWS, LANES), 0)
+    return lane, row
+
+
+def inner_kernel(step, width, window_row, window_turn, state, total, wide, tall, after, speed):
+    blocks = wide.shape[0]
+    node_velocity(total, speed, width)
+    place = window_place(window_row, window_turn, step)
+    lane, row = gather_lanes()
 
     def several(q, carry):
-        for part in range(group // ROWS):
-            base = q * group + part * ROWS
-            terms = []
-            for k in range(ROWS):
-                slot = slot_of(base + k)
-                terms.append(gather_terms(weights, speed, slot, *place(slot), lane))
-            vel_d, vel_c, l_dd, l_cd, l_dc, l_cc = (row_sums(t, row) for t in zip(*terms))
-            vel_d, vel_c = 0.25 * vel_d, 0.25 * vel_c
-            l_dd, l_cc = 0.5 * l_dd, 0.5 * l_cc
-            rate_dc = 0.25 * (l_dc + l_cd)
-            trace = l_dd + l_cc
-            spot = pl.ds(base if isinstance(base, int) else pl.multiple_of(base, ROWS), ROWS)
+        for base in range(0, GROUP, ROWS):
+            slots = [q * GROUP + base + k for k in range(ROWS)]
+            start = base if isinstance(q, int) else pl.multiple_of(slots[0], ROWS)
+            spot = pl.ds(start, ROWS)
             field = [state[f, spot, :] for f in range(FIELDS)]
-            shear = (2.0 * TIME_STEP) * field[9]
-            spread = (TIME_STEP * field[10]) * trace
-            stretch = TIME_STEP * trace
-            result = {
-                0: jnp.clip(field[0] + TIME_STEP * vel_d, 0.5, WIN_DOWN - 1.5),
-                1: jnp.clip(field[1] + TIME_STEP * vel_c, 0.5, WIN_CROSS - 1.5),
-                2: vel_d,
-                3: vel_c,
-                4: field[4] + (spread + shear * l_dd),
-                5: field[5] + shear * rate_dc,
-                6: field[6] + (spread + shear * l_cc),
-                8: field[8] + field[8] * stretch,
-                11: field[11]
-                + TIME_STEP * (l_dd * l_dd + l_cc * l_cc + 2.0 * rate_dc * rate_dc),
-            }
+            result = gather_eight((wide, tall), speed, slots, place, field, lane, row)
             for f in range(FIELDS):
-                out[f, spot, :] = result.get(f, field[f])
+                after[f, spot, :] = result.get(f, field[f])
         return carry
 
-    steps = blocks // group
+    steps = blocks // GROUP
     if steps == 1:
         several(0, 0)
     else:
         lax.fori_loop(0, steps, several, 0)
+
+
+def edge_kernel(step, links, width, window_row, window_turn, slots, edge, state, total, *rest):
+    bands = rest[: links - 2]
+    wide, tall, before, after = rest[links - 2 : links + 2]
+    sent = rest[links + 2 : 2 * links + 2]
+    speed, sums, rows = rest[2 * links + 2 :]
+    blocks = wide.shape[0]
+    after[:, :blocks, :] = before[:, :blocks, :]
+    add_across(total, bands, sums, width)
+    node_velocity(sums, speed, width)
+    place = window_place(window_row, window_turn, step)
+    lane, row = gather_lanes()
+    count = edge[blocks]
+
+    def eight(q, carry):
+        picked = [edge[jnp.minimum(q * ROWS + k, count - 1)] for k in range(ROWS)]
+        for k, slot in enumerate(picked):
+            for f in range(FIELDS):
+                rows[f, k : k + 1, :] = state[f, pl.ds(slot, 1), :]
+        field = [rows[f] for f in range(FIELDS)]
+        result = gather_eight((wide, tall), speed, picked, place, field, lane, row)
+        for f, value in result.items():
+            rows[f] = value
+        for k, slot in enumerate(picked):
+            for f in result:
+                after[f, pl.ds(slot, 1), :] = rows[f, k : k + 1, :]
+        return carry
+
+    lax.fori_loop(0, (count + ROWS - 1) // ROWS, eight, 0)
+    cap = slots.shape[2]
+    for link in range(links):
+        side = link_side(link)
+        for m in range(cap):
+            slot = pl.ds(slots[step, side, m], 1)
+            for f in range(FIELDS):
+                sent[link][f * cap + m : f * cap + m + 1, :] = after[f, slot, :]
 
 
 def swap_pairs(size, first):
@@ -509,7 +558,7 @@
             x, ("down", "cross"), axis_index_groups=odd_groups(size_down, size_cross)
         )
 
-    def call(name, kernel, outs, in_specs, scratch=()):
+    def call(name, kernel, outs, in_specs, scratch=(), flops=0):
         return pl.pallas_call(
             kernel,
             out_shape=outs,
@@ -517,6 +566,7 @@
             out_specs=tuple(pl.BlockSpec(memory_space=x.memory_space) if isinstance(x, pl.MemoryRef) else vmem for x in outs),
             scratch_shapes=scratch,
             compiler_params=pltpu.CompilerParams(vmem_limit_bytes=VMEM_BYTES),
+            cost_estimate=pl.CostEstimate(flops=flops, bytes_accessed=1 << 20, transcendentals=0),
             name=name,
         )
 
@@ -550,31 +600,33 @@
             move_count.reshape(STEPS, 4),
         )
         given = ints + (jnp.transpose(particles, (1, 0, 2)),)
-        parts = 1
+        edge_type = pltpu.SMEM((blocks + 1,), jnp.int32)
+        speed_scratch = pltpu.VMEM((halves * 2 * height, LANES), f32)
         state, grid, pay, *rest = call(
             "scatter_first",
-            functools.partial(first_kernel, 0, parts),
+            functools.partial(first_kernel, 0, width),
             (state_type, grid_type, band_type)
             + weight_types
-            + tuple(pltpu.SMEM(x.shape, x.dtype) for x in ints[:2] * 2 + ints[2:]),
+            + tuple(pltpu.SMEM(x.shape, x.dtype) for x in ints[:2] * 2 + ints[2:])
+            + (edge_type,),
             [hbm] * 5,
             scatter_scratch
             + [
                 pltpu.VMEM((4,) + anchor_down.shape, jnp.int32),
                 pltpu.SMEM(anchor_down.shape, jnp.int32),
                 pltpu.SMEM(anchor_cross.shape, jnp.int32),
-                pltpu.SemaphoreType.DMA((10 + parts,)),
+                pltpu.SemaphoreType.DMA((11,)),
             ],
         )(*(pltpu.with_memory_space_constraint(x, pltpu.HBM) for x in given))
         weights = rest[:2]
         rest = [pltpu.with_memory_space_constraint(x, pltpu.SMEM) for x in rest[2:]]
-        windows, moves = rest[:4], rest[4:]
+        windows, moves, edge = rest[:4], rest[4:6], rest[6]
         for step in range(STEPS):
             if step:
-                state, grid, pay, *weights = call(
+                state, grid, pay, *weights, edge = call(
                     "scatter_next",
-                    functools.partial(next_kernel, step, links),
-                    (state_type, grid_type, band_type) + weight_types,
+                    functools.partial(next_kernel, step, links, width),
+                    (state_type, grid_type, band_type) + weight_types + (edge_type,),
                     [smem] * 4 + [vmem] * (links + 1),
                     scatter_scratch,
                 )(*windows[:2], *moves, state, *arrived)
@@ -587,16 +639,26 @@
                 [vmem] * 3,
             )(grid, band0, band1)
             bands = [swap(pay[k], 2 + k) for k in range(links - 2)]
+            ahead = call(
+                "gather_inner",
+                functools.partial(inner_kernel, step, width),
+                (state_type,),
+                [smem] * 2 + [vmem] * 4,
+                [speed_scratch],
+                1 << 32,
+            )(*windows[2:], state, total, *weights)
+            edge = pltpu.with_memory_space_constraint(edge, pltpu.SMEM)
             state, *sent = call(
-                "gather",
-                functools.partial(gather_kernel, step, links, width),
+                "gather_edge",
+                functools.partial(edge_kernel, step, links, width),
                 (state_type,) + (sent_type,) * links,
-                [smem] * 3 + [vmem] * (2 + links),
+                [smem] * 4 + [vmem] * (3 + links),
                 [
-                    pltpu.VMEM((halves * 2 * height, LANES), f32),
+                    speed_scratch,
                     pltpu.VMEM(grid_type.shape, f32),
+                    pltpu.VMEM((FIELDS, ROWS, LANES), f32),
                 ],
-            )(*windows[2:], moves[0], state, total, *bands, *weights)
+            )(*windows[2:], moves[0], edge, state, total, *bands, *weights, *ahead)
             arrived = [
                 gather_pairs(x) if link == 1 else swap(x, link) for link, x in enumerate(sent)
             ]

time: 41.7 us -> 40 us (0.959)
  waiting for transfers between devices: 3.45 us -> 0.64 us
  Pallas kernels: 10.2 us -> 11.5 us
    ppermute x8, waiting for transfers between devices: 3.45 us -> 0.64 us  [swap(): return lax.ppermute(x, name, swap_pairs(size, second))]
    pallas_call x4 -> x6, Pallas kernels: 8.97 us -> 10.2 us  [the longest x1 3.48 us: on_device(): call('scatter_first', functools.partial(first_kernel, 0, width), (state_t...]
  transfers between devices with their start and end apart: 8 -> 8, of which waited for: 2 -> 1; matrix products, arithmetic and copies ran while one was open for 0% -> 0% of each run, Pallas kernels for 0% -> 8%
where the time goes in v5:
time: 40 us; the launch traced here: 39.6 us
  blocking collectives  20 us (50%)
  Pallas kernels  11.5 us (29%)
  starting transfers between devices  7.41 us (19%)
  waiting for transfers between devices  0.64 us (2%)
    all_gather x4, blocking collectives, gather_pairs(): lax.all_gather(x, ('down', 'cross'), axis_index_groups=odd_groups(size_do...  20 us
    ppermute x8, starting transfers between devices, swap(): return lax.ppermute(x, name, swap_pairs(size, second))  7.41 us
    pallas_call x1, Pallas kernels, on_device(): call('scatter_first', functools.partial(first_kernel, 0, width), (state_t...  3.48 us
    pallas_call x2, Pallas kernels, on_device(): call('gather_inner', functools.partial(inner_kernel, step, width), (state...  3.14 us
    pallas_call x1, Pallas kernels, on_device(): call('scatter_next', functools.partial(next_kernel, step, links, width),...  2.14 us
    pallas_call x2, Pallas kernels, on_device(): call('gather_edge', functools.partial(edge_kernel, step, links, width), (...  1.45 us
    pallas_call x1, Pallas kernels, on_device(): call('settle_last', functools.partial(last_kernel, STEPS - 1, links), (pl...  1.11 us
  transfers between devices with their start and end apart: 8, of which 1 were waited for; matrix products, arithmetic and copies ran while one was open for 0% of the time, Pallas kernels for 8%

profile of v5, /device:TPU:11, one launch (start us, length us, event | category | flops | bytes accessed | tf_op | source)
XLA Modules:
  0.0 39.6 jit_solution(14861834840155306497)
XLA Ops:
  0.0 3.5 %scatter_first.1 = (f32[12,136,128]{2,1,0:T(8,128)S(1)}, f32[3,72,128]{2,1,0:T(8,128)S(1)}, f32[2,3,24,128]{3,2,1,0:T(8,128)S(1)}, bf16[128,32,256]{2,1,0:T(8,12...) custom-call(s32[2,128]{1,0:T(2,128)} %down_in.1, ...), custom_call_target="tpu_custom_call" | custom-call | bytes 1048576 | tf_op jit(solution)/shard_map/scatter_first/pallas_call | solution.py:605
  3.5 0.7 %collective-permute-start = (f32[3,24,128]{2,1,0:T(8,128)S(1)}, f32[3,24,128]{2,1,0:T(8,128)S(1)}, u32[]{:S(2)}, u32[]{:S(2)}) collective-permute-start(f32[3,24,128]{2,1,0:T(8,128)S(1)} %get-tuple-element.68), channel_id=1, source_target_pairs={{0,2},{2,0},{4,6},{6,4},{8,10},{10,8},{12,14},{14,12},{16,18},{18,... | collective-permute-start | bytes 110600 | tf_op jit(solution)/shard_map/ppermute | solution.py:554
  4.2 4.6 %all_gather.18.band1 = f32[2,3,24,128]{3,2,1,0:T(8,128)S(1)} all-gather(f32[1,3,24,128]{3,2,1,0:T(8,128)S(1)} %get-tuple-element.67), channel_id=1, replica_groups={{0,1},{30,31},{2,4},{3,5},{6,8},{7,9},{10,12},{11,13},{14,16},{15,17},{..., dimensions={0}, use_global_device_ids=true | all-gather | bytes 110592 | tf_op jit(solution)/shard_map/all_gather | solution.py:557
  8.8 0.0 collective-permute-done.band0
  8.8 0.1 add_down.2
  8.9 0.3 collective-permute-start.1
  9.2 1.6 %gather_inner.2.rest_3_ = f32[12,136,128]{2,1,0:T(8,128)S(1)} custom-call(s32[2,128]{1,0:T(2,128)S(4)} %get-tuple-element.37.window_row, s32[2,128]{1,0:T(2,128)S(4)} %get-tuple-element.38.window_turn, f32[12,136,128]{2,1,0:T(8,128)S(1)} %get-tuple-element.42.state, f32[3,72,128]{2,1,0:T(8,128)S(1)} %get-tuple-element.45.total, ...), custom_call_target="tpu_custom_call" | custom-call | flops 4294967296 | bytes 1048576 | tf_op jit(solution)/shard_map/gather_inner/pallas_call | solution.py:642
  10.8 0.6 %collective-permute-done.1.rest_0_ = f32[8,128]{1,0:T(8,128)S(1)} collective-permute-done((f32[8,128]{1,0:T(8,128)S(1)}, f32[8,128]{1,0:T(8,128)S(1)}, u32[]{:S(2)}, u32[]{:S(2)}) %collective-permute-start.1) | collective-permute-done | bytes 4128 | tf_op jit(solution)/shard_map/ppermute | solution.py:554
  11.4 0.7 %gather_edge.2 = (f32[12,136,128]{2,1,0:T(8,128)S(1)}, f32[160,128]{1,0:T(8,128)S(1)}, f32[160,128]{1,0:T(8,128)S(1)}, f32[160,128]{1,0:T(8,128)S(1)}) custom-call(s32[2,128]{1,0:T(2,128)S(4)} %get-tuple-element.37.window_row, s32[2,128]{1,0:T(2,128)S(4)} %get-tuple-element.38.window_turn, s32[2,4,13]{2,1,0:T(4,128)S(4)} %get-tuple-element.35.slots, ...), custom_call_target="tpu_custom_call" | custom-call | bytes 1048576 | tf_op jit(solution)/shard_map/gather_edge/pallas_call | solution.py:651
  12.1 1.7 %collective-permute-start.2 = (f32[160,128]{1,0:T(8,128)S(1)}, f32[160,128]{1,0:T(8,128)S(1)}, u32[]{:S(2)}, u32[]{:S(2)}) collective-permute-start(f32[160,128]{1,0:T(8,128)S(1)} %get-tuple-element.50), channel_id=1, source_target_pairs={{0,2},{2,0},{4,6},{6,4},{8,10},{10,8},{12,14},{14,12},{16,18},{18,... | collective-permute-start | bytes 245768 | tf_op jit(solution)/shard_map/ppermute | solution.py:554
  13.9 0.3 collective-permute-start.3
  14.1 5.4 %all-gather = f32[320,128]{1,0:T(8,128)S(1)} all-gather(f32[160,128]{1,0:T(8,128)S(1)} %get-tuple-element.51), channel_id=2, replica_groups={{0,1},{30,31},{2,4},{3,5},{6,8},{7,9},{10,12},{11,13},{14,16},{15,17},{..., dimensions={0}, use_global_device_ids=true | all-gather | bytes 245760 | tf_op jit(solution)/shard_map/all_gather | solution.py:557
  19.5 0.0 collective-permute-done.2.rest_0_
  19.5 0.0 collective-permute-done.3.rest_2_
  19.5 2.1 %scatter_next.1 = (f32[12,136,128]{2,1,0:T(8,128)S(1)}, f32[3,72,128]{2,1,0:T(8,128)S(1)}, f32[2,3,24,128]{3,2,1,0:T(8,128)S(1)}, bf16[128,32,256]{2,1,0:T(8,128...) custom-call(s32[2,128]{1,0:T(2,128)S(4)} %get-tuple-element.39.first_row, ...), custom_call_target="tpu_custom_call" | custom-call | bytes 1048576 | tf_op jit(solution)/shard_map/scatter_next/pallas_call | solution.py:626
  21.7 0.5 %collective-permute-start.4 = (f32[3,24,128]{2,1,0:T(8,128)S(1)}, f32[3,24,128]{2,1,0:T(8,128)S(1)}, u32[]{:S(2)}, u32[]{:S(2)}) collective-permute-start(f32[3,24,128]{2,1,0:T(8,128)S(1)} %get-tuple-element.66), channel_id=1, source_target_pairs={{0,2},{2,0},{4,6},{6,4},{8,10},{10,8},{12,14},{14,12},{16,18},{18,... | collective-permute-start | bytes 110600 | tf_op jit(solution)/shard_map/ppermute | solution.py:554
  22.2 4.6 %all_gather.21.band1 = f32[2,3,24,128]{3,2,1,0:T(8,128)S(1)} all-gather(f32[1,3,24,128]{3,2,1,0:T(8,128)S(1)} %get-tuple-element.65), channel_id=1, replica_groups={{0,1},{30,31},{2,4},{3,5},{6,8},{7,9},{10,12},{11,13},{14,16},{15,17},{..., dimensions={0}, use_global_device_ids=true | all-gather | bytes 110592 | tf_op jit(solution)/shard_map/all_gather | solution.py:557
  26.8 0.0 collective-permute-done.4.band0
  26.8 0.1 add_down.3
  26.9 1.2 %collective-permute-start.5 = (f32[8,128]{1,0:T(8,128)S(1)}, f32[8,128]{1,0:T(8,128)S(1)}, u32[]{:S(2)}, u32[]{:S(2)}) collective-permute-start(f32[8,128]{1,0:T(8,128)S(1)} %slice_bitcast_fusion.2), channel_id=1, source_target_pairs={{0,1},{1,0},{2,3},{3,2},{4,5},{5,4},{6,7},{7,6},{8,9},{9,8},{10,11... | collective-permute-start | bytes 12296 | tf_op jit(solution)/shard_map/ppermute | solution.py:554
  28.2 1.6 %gather_inner.3.rest_3_ = f32[12,136,128]{2,1,0:T(8,128)S(1)} custom-call(s32[2,128]{1,0:T(2,128)S(4)} %get-tuple-element.37.window_row, s32[2,128]{1,0:T(2,128)S(4)} %get-tuple-element.38.window_turn, f32[12,136,128]{2,1,0:T(8,128)S(1)} %get-tuple-element.54.state, f32[3,72,128]{2,1,0:T(8,128)S(1)} %get-tuple-element.57.total, ...), custom_call_target="tpu_custom_call" | custom-call | flops 4294967296 | bytes 1048576 | tf_op jit(solution)/shard_map/gather_inner/pallas_call | solution.py:642
  29.7 0.0 collective-permute-done.5.rest_0_
  29.7 0.7 %gather_edge.3 = (f32[12,136,128]{2,1,0:T(8,128)S(1)}, f32[160,128]{1,0:T(8,128)S(1)}, f32[160,128]{1,0:T(8,128)S(1)}, f32[160,128]{1,0:T(8,128)S(1)}) custom-call(s32[2,128]{1,0:T(2,128)S(4)} %get-tuple-element.37.window_row, s32[2,128]{1,0:T(2,128)S(4)} %get-tuple-element.38.window_turn, s32[2,4,13]{2,1,0:T(4,128)S(4)} %get-tuple-element.35.slots, ...), custom_call_target="tpu_custom_call" | custom-call | bytes 1048576 | tf_op jit(solution)/shard_map/gather_edge/pallas_call | solution.py:651
  30.5 1.4 %collective-permute-start.6 = (f32[160,128]{1,0:T(8,128)S(1)}, f32[160,128]{1,0:T(8,128)S(1)}, u32[]{:S(2)}, u32[]{:S(2)}) collective-permute-start(f32[160,128]{1,0:T(8,128)S(1)} %get-tuple-element.62), channel_id=1, source_target_pairs={{0,2},{2,0},{4,6},{6,4},{8,10},{10,8},{12,14},{14,12},{16,18},{18,... | collective-permute-start | bytes 245768 | tf_op jit(solution)/shard_map/ppermute | solution.py:554
  31.8 1.2 %collective-permute-start.7 = (f32[160,128]{1,0:T(8,128)S(1)}, f32[160,128]{1,0:T(8,128)S(1)}, u32[]{:S(2)}, u32[]{:S(2)}) collective-permute-start(f32[160,128]{1,0:T(8,128)S(1)} %get-tuple-element.64), channel_id=1, source_target_pairs={{0,1},{1,0},{2,3},{3,2},{4,5},{5,4},{6,7},{7,6},{8,9},{9,8},{10,11... | collective-permute-start | bytes 245768 | tf_op jit(solution)/shard_map/ppermute | solution.py:554
  33.1 5.4 %all-gather.1 = f32[320,128]{1,0:T(8,128)S(1)} all-gather(f32[160,128]{1,0:T(8,128)S(1)} %get-tuple-element.63), channel_id=3, replica_groups={{0,1},{30,31},{2,4},{3,5},{6,8},{7,9},{10,12},{11,13},{14,16},{15,17},{..., dimensions={0}, use_global_device_ids=true | all-gather | bytes 245760 | tf_op jit(solution)/shard_map/all_gather | solution.py:557
  38.5 0.0 collective-permute-done.6.rest_0_
  38.5 0.0 collective-permute-done.7.rest_2_
  38.5 1.1 %settle_last.1 = f32[12,128,128]{2,1,0:T(8,128)} custom-call(s32[2,4,13]{2,1,0:T(4,128)S(4)} %get-tuple-element.35.slots, s32[2,4]{1,0:T(2,128)S(4)} %get-tuple-element.36.counts, f32[12,136,128]{2,1,0:T(8,128)S(1)} %get-tuple-element.61.old, f32[160,128]{1,0:T(8,128)S(1)} %collective-permute-done.6.rest_0_, f32[2,160,128]{2,1,0:T(8,128)S(1)} %bitcast.14, ...), custom_call_target="tpu_custom_call" | custom-call | bytes 1048576 | tf_op jit(solution)/shard_map/settle_last/pallas_call | solution.py:665
  (4 shorter events, 0.0 us)
Async XLA Ops:
  3.5 5.3 %collective-permute-start = (f32[3,24,128]{2,1,0:T(8,128)S(1)}, f32[3,24,128]{2,1,0:T(8,128)S(1)}, u32[]{:S(2)}, u32[]{:S(2)}) collective-permute-start(f32[3,24,128]{2,1,0:T(8,128)S(1)} %get-tuple-element.68), channel_id=1, source_target_pairs={{0,2},{2,0},{4,6},{6,4},{8,10},{10,8},{12,14},{14,12},{16,18},{18,... | collective-permute-start | bytes 110600 | tf_op jit(solution)/shard_map/ppermute | solution.py:554
  8.9 2.5 %collective-permute-start.1 = (f32[8,128]{1,0:T(8,128)S(1)}, f32[8,128]{1,0:T(8,128)S(1)}, u32[]{:S(2)}, u32[]{:S(2)}) collective-permute-start(f32[8,128]{1,0:T(8,128)S(1)} %slice_bitcast_fusion.3), channel_id=1, source_target_pairs={{0,1},{1,0},{2,3},{3,2},{4,5},{5,4},{6,7},{7,6},{8,9},{9,8},{10,11... | collective-permute-start | bytes 12296 | tf_op jit(solution)/shard_map/ppermute | solution.py:554
  12.1 7.4 %collective-permute-start.2 = (f32[160,128]{1,0:T(8,128)S(1)}, f32[160,128]{1,0:T(8,128)S(1)}, u32[]{:S(2)}, u32[]{:S(2)}) collective-permute-start(f32[160,128]{1,0:T(8,128)S(1)} %get-tuple-element.50), channel_id=1, source_target_pairs={{0,2},{2,0},{4,6},{6,4},{8,10},{10,8},{12,14},{14,12},{16,18},{18,... | collective-permute-start | bytes 245768 | tf_op jit(solution)/shard_map/ppermute | solution.py:554
  13.9 5.7 %collective-permute-start.3 = (f32[160,128]{1,0:T(8,128)S(1)}, f32[160,128]{1,0:T(8,128)S(1)}, u32[]{:S(2)}, u32[]{:S(2)}) collective-permute-start(f32[160,128]{1,0:T(8,128)S(1)} %get-tuple-element.52), channel_id=1, source_target_pairs={{0,1},{1,0},{2,3},{3,2},{4,5},{5,4},{6,7},{7,6},{8,9},{9,8},{10,11... | collective-permute-start | bytes 245768 | tf_op jit(solution)/shard_map/ppermute | solution.py:554
  21.7 5.1 %collective-permute-start.4 = (f32[3,24,128]{2,1,0:T(8,128)S(1)}, f32[3,24,128]{2,1,0:T(8,128)S(1)}, u32[]{:S(2)}, u32[]{:S(2)}) collective-permute-start(f32[3,24,128]{2,1,0:T(8,128)S(1)} %get-tuple-element.66), channel_id=1, source_target_pairs={{0,2},{2,0},{4,6},{6,4},{8,10},{10,8},{12,14},{14,12},{16,18},{18,... | collective-permute-start | bytes 110600 | tf_op jit(solution)/shard_map/ppermute | solution.py:554
  26.9 2.8 %collective-permute-start.5 = (f32[8,128]{1,0:T(8,128)S(1)}, f32[8,128]{1,0:T(8,128)S(1)}, u32[]{:S(2)}, u32[]{:S(2)}) collective-permute-start(f32[8,128]{1,0:T(8,128)S(1)} %slice_bitcast_fusion.2), channel_id=1, source_target_pairs={{0,1},{1,0},{2,3},{3,2},{4,5},{5,4},{6,7},{7,6},{8,9},{9,8},{10,11... | collective-permute-start | bytes 12296 | tf_op jit(solution)/shard_map/ppermute | solution.py:554
  30.5 8.0 %collective-permute-start.6 = (f32[160,128]{1,0:T(8,128)S(1)}, f32[160,128]{1,0:T(8,128)S(1)}, u32[]{:S(2)}, u32[]{:S(2)}) collective-permute-start(f32[160,128]{1,0:T(8,128)S(1)} %get-tuple-element.62), channel_id=1, source_target_pairs={{0,2},{2,0},{4,6},{6,4},{8,10},{10,8},{12,14},{14,12},{16,18},{18,... | collective-permute-start | bytes 245768 | tf_op jit(solution)/shard_map/ppermute | solution.py:554
  31.8 6.6 %collective-permute-start.7 = (f32[160,128]{1,0:T(8,128)S(1)}, f32[160,128]{1,0:T(8,128)S(1)}, u32[]{:S(2)}, u32[]{:S(2)}) collective-permute-start(f32[160,128]{1,0:T(8,128)S(1)} %get-tuple-element.64), channel_id=1, source_target_pairs={{0,1},{1,0},{2,3},{3,2},{4,5},{5,4},{6,7},{7,6},{8,9},{9,8},{10,11... | collective-permute-start | bytes 245768 | tf_op jit(solution)/shard_map/ppermute | solution.py:554

commit v6 on v5

--- a/solution.py
+++ b/solution.py
@@ -112,20 +112,17 @@
     return low, high
 
 
-def scatter_rows(state, loads, sums, weights, place, blocks, group, edge, limits):
+def scatter_rows(state, loads, sums, weights, place, blocks, group):
     rows = node_rows(WIN_DOWN)
     cols = node_rows(WIN_CROSS)
     lane = lax.broadcasted_iota(jnp.int32, (WIN_CROSS, LANES), 1)
     inside = (lane & (STRIDE - 1)) < WIN_DOWN
 
-    def several(q, listed):
+    def several(q, carry):
         for k in range(group):
             m = q * group + k
             row = pl.ds(m, 1)
             first_row, first_col = place(m)
-            edge[listed] = m
-            at_edge = (first_col < limits[0]) | (first_col > limits[1])
-            listed = listed + at_edge.astype(jnp.int32)
             scatter_block(
                 state[0, row, :],
                 state[1, row, :],
@@ -139,14 +136,26 @@
                 cols,
                 inside,
             )
-        return listed
+        return carry
 
     steps = blocks // group
-    edge[blocks] = several(0, 0) if steps == 1 else lax.fori_loop(0, steps, several, 0)
-
-
-def window_place(first, second, step, add=0):
-    return lambda b: (first[step, b] + add, second[step, b] + add)
+    if steps == 1:
+        several(0, 0)
+    else:
+        lax.fori_loop(0, steps, several, 0)
+
+
+def grid_place(anchor_down, anchor_cross, step):
+    return lambda b: (anchor_down[step, b] + GHOST, anchor_cross[step, b] + GHOST)
+
+
+def speed_place(anchor_down, anchor_cross, step):
+    def place(b):
+        col = anchor_cross[step, b] + GHOST
+        row = (col >> HALF_BITS) * (2 * (TILE_DOWN + 2 * GHOST)) + anchor_down[step, b] + GHOST
+        return row, (LANES - (col & (HALF - 1))) & (LANES - 1)
+
+    return place
 
 
 def write_grid(sums, grid, pay):
@@ -165,7 +174,6 @@
 
 def first_kernel(
     step,
-    width,
     down_in,
     cross_in,
     slots_in,
@@ -176,61 +184,38 @@
     pay,
     wide,
     tall,
-    first_row,
-    first_col,
-    window_row,
-    window_turn,
+    anchor_down,
+    anchor_cross,
     slots,
     counts,
-    edge,
     sums,
     loads,
-    table,
-    down_scalar,
-    cross_scalar,
     sems,
 ):
     blocks = particles.shape[1]
-    scalars = [
-        pltpu.make_async_copy(src, dst, sems.at[k])
-        for k, (src, dst) in enumerate(((down_in, down_scalar), (cross_in, cross_scalar)))
+    whole = pltpu.make_async_copy(particles, state.at[:, pl.ds(0, blocks), :], sems.at[0])
+    ints = [
+        pltpu.make_async_copy(src, dst, sems.at[1 + k])
+        for k, (src, dst) in enumerate(
+            (
+                (down_in, anchor_down),
+                (cross_in, anchor_cross),
+                (slots_in, slots),
+                (counts_in, counts),
+            )
+        )
     ]
-    whole = pltpu.make_async_copy(particles, state.at[:, pl.ds(0, blocks), :], sems.at[2])
-    anchors = [
-        pltpu.make_async_copy(src, table.at[k], sems.at[3 + k])
-        for k, src in enumerate((down_in, cross_in))
-    ]
-    moves = [
-        pltpu.make_async_copy(src, dst, sems.at[5 + k])
-        for k, (src, dst) in enumerate(((slots_in, slots), (counts_in, counts)))
-    ]
-    for copy in scalars + [whole] + anchors + moves:
+    for copy in ints[:2] + [whole] + ints[2:]:
         copy.start()
     sums[...] = jnp.zeros_like(sums)
-    for copy in anchors:
+    for copy in ints[:2]:
         copy.wait()
-    row = table[0] + GHOST
-    col = table[1] + GHOST
-    table[0] = row
-    table[1] = col
-    table[2] = (col >> HALF_BITS) * (2 * (TILE_DOWN + 2 * GHOST)) + row
-    table[3] = (LANES - (col & (HALF - 1))) & (LANES - 1)
-    tables = [
-        pltpu.make_async_copy(table.at[k], dst, sems.at[7 + k])
-        for k, dst in enumerate((first_row, first_col, window_row, window_turn))
-    ]
-    for copy in tables:
-        copy.start()
-    for copy in scalars:
-        copy.wait()
-    place = window_place(down_scalar, cross_scalar, step, GHOST)
     whole.wait()
     particle_loads(state, loads, blocks)
-    scatter_rows(
-        state, loads, sums, (wide, tall), place, blocks, GROUP, edge, edge_limits(width)
-    )
+    place = grid_place(anchor_down, anchor_cross, step)
+    scatter_rows(state, loads, sums, (wide, tall), place, blocks, GROUP)
     write_grid(sums, grid, pay)
-    for copy in tables + moves:
+    for copy in ints[2:]:
         copy.wait()
 
 
@@ -256,9 +241,9 @@
     return [ref.at[odd] if link == 1 else ref for link, ref in enumerate(refs)]
 
 
-def next_kernel(step, links, width, first_row, first_col, slots, counts, old, *rest):
+def next_kernel(step, links, anchor_down, anchor_cross, slots, counts, old, *rest):
     arrived = pick_arrived(rest[:links])
-    state, grid, pay, wide, tall, edge, sums, loads = rest[links:]
+    state, grid, pay, wide, tall, sums, loads = rest[links:]
     blocks = loads.shape[1]
     state[:, :blocks, :] = old[:, :blocks, :]
     settle(state, arrived, slots, counts, step - 1, blocks)
@@ -269,11 +254,9 @@
         loads,
         sums,
         (wide, tall),
-        window_place(first_row, first_col, step),
+        grid_place(anchor_down, anchor_cross, step),
         blocks,
         GROUP,
-        edge,
-        edge_limits(width),
     )
     write_grid(sums, grid, pay)
 
@@ -463,13 +446,30 @@
     return lane, row
 
 
-def inner_kernel(step, width, window_row, window_turn, state, total, wide, tall, after, speed):
+def inner_kernel(
+    step,
+    links,
+    width,
+    anchor_down,
+    anchor_cross,
+    slots,
+    state,
+    total,
+    wide,
+    tall,
+    after,
+    edge,
+    rank,
+    *rest,
+):
+    sent, speed = rest[:-1], rest[-1]
     blocks = wide.shape[0]
     node_velocity(total, speed, width)
-    place = window_place(window_row, window_turn, step)
+    place = speed_place(anchor_down, anchor_cross, step)
     lane, row = gather_lanes()
-
-    def several(q, carry):
+    low, high = edge_limits(width)
+
+    def several(q, listed):
         for base in range(0, GROUP, ROWS):
             slots = [q * GROUP + base + k for k in range(ROWS)]
             start = base if isinstance(q, int) else pl.multiple_of(slots[0], ROWS)
@@ -478,25 +478,42 @@
             result = gather_eight((wide, tall), speed, slots, place, field, lane, row)
             for f in range(FIELDS):
                 after[f, spot, :] = result.get(f, field[f])
-        return carry
+            for slot in slots:
+                edge[listed] = slot
+                col = anchor_cross[step, slot] + GHOST
+                listed = listed + ((col < low) | (col > high)).astype(jnp.int32)
+        return listed
 
     steps = blocks // GROUP
-    if steps == 1:
-        several(0, 0)
-    else:
-        lax.fori_loop(0, steps, several, 0)
-
-
-def edge_kernel(step, links, width, window_row, window_turn, slots, edge, state, total, *rest):
+    edge[blocks] = several(0, 0) if steps == 1 else lax.fori_loop(0, steps, several, 0)
+    cap = slots.shape[2]
+    plane = sent[0].shape[0]
+    for b in range(blocks):
+        rank[b] = links * plane
+    for link in range(links):
+        side = link_side(link)
+        for m in range(cap):
+            slot = slots[step, side, m]
+            rank[slot] = link * plane + m
+            for f in range(FIELDS):
+                start = f * cap + m
+                sent[link][start : start + 1, :] = after[f, pl.ds(slot, 1), :]
+
+
+def edge_kernel(step, links, width, cap, anchor_down, anchor_cross, edge, rank, state, total, *rest):
     bands = rest[: links - 2]
-    wide, tall, before, after = rest[links - 2 : links + 2]
-    sent = rest[links + 2 : 2 * links + 2]
-    speed, sums, rows = rest[2 * links + 2 :]
+    wide, tall, before = rest[links - 2 : links + 1]
+    picked_before, after = rest[links + 1 : 2 * links + 1], rest[2 * links + 1]
+    sent = rest[2 * links + 2 : 3 * links + 2]
+    speed, sums, rows = rest[3 * links + 2 :]
+    plane = picked_before[0].shape[0]
     blocks = wide.shape[0]
     after[:, :blocks, :] = before[:, :blocks, :]
+    for out, given in zip(sent, picked_before):
+        out[:plane, :] = given[...]
     add_across(total, bands, sums, width)
     node_velocity(sums, speed, width)
-    place = window_place(window_row, window_turn, step)
+    place = speed_place(anchor_down, anchor_cross, step)
     lane, row = gather_lanes()
     count = edge[blocks]
 
@@ -510,18 +527,18 @@
         for f, value in result.items():
             rows[f] = value
         for k, slot in enumerate(picked):
+            start = rank[slot]
             for f in result:
                 after[f, pl.ds(slot, 1), :] = rows[f, k : k + 1, :]
+            for link in range(links):
+                leaves = (start >= link * plane) & (start < (link + 1) * plane)
+                first = jnp.where(leaves, start - link * plane, plane - 1)
+                between = jnp.where(leaves, cap, 0)
+                for f in result:
+                    sent[link][pl.ds(first + f * between, 1), :] = rows[f, k : k + 1, :]
         return carry
 
     lax.fori_loop(0, (count + ROWS - 1) // ROWS, eight, 0)
-    cap = slots.shape[2]
-    for link in range(links):
-        side = link_side(link)
-        for m in range(cap):
-            slot = pl.ds(slots[step, side, m], 1)
-            for f in range(FIELDS):
-                sent[link][f * cap + m : f * cap + m + 1, :] = after[f, slot, :]
 
 
 def swap_pairs(size, first):
@@ -584,7 +601,8 @@
         grid_type = array(tiles, CHANNELS * height, LANES)
         band_type = array(2, tiles, CHANNELS * BAND, LANES)
         state_type = array(FIELDS, blocks + ROWS, LANES)
-        sent_type = array(-(-FIELDS * cap // 8) * 8, LANES)
+        plane = (FIELDS * cap // 8 + 1) * 8
+        sent_type = array(plane, LANES)
         weight_types = (
             array(blocks, 2 * WIN_CROSS, 2 * LANES, dtype=jnp.bfloat16),
             array(blocks, 2 * WIN_DOWN, LANES),
@@ -604,32 +622,28 @@
         speed_scratch = pltpu.VMEM((halves * 2 * height, LANES), f32)
         state, grid, pay, *rest = call(
             "scatter_first",
-            functools.partial(first_kernel, 0, width),
+            functools.partial(first_kernel, 0),
             (state_type, grid_type, band_type)
             + weight_types
-            + tuple(pltpu.SMEM(x.shape, x.dtype) for x in ints[:2] * 2 + ints[2:])
-            + (edge_type,),
+            + tuple(pltpu.SMEM(x.shape, x.dtype) for x in ints),
             [hbm] * 5,
             scatter_scratch
             + [
-                pltpu.VMEM((4,) + anchor_down.shape, jnp.int32),
-                pltpu.SMEM(anchor_down.shape, jnp.int32),
-                pltpu.SMEM(anchor_cross.shape, jnp.int32),
-                pltpu.SemaphoreType.DMA((11,)),
+                pltpu.SemaphoreType.DMA((5,)),
             ],
         )(*(pltpu.with_memory_space_constraint(x, pltpu.HBM) for x in given))
         weights = rest[:2]
         rest = [pltpu.with_memory_space_constraint(x, pltpu.SMEM) for x in rest[2:]]
-        windows, moves, edge = rest[:4], rest[4:6], rest[6]
+        anchors, moves = rest[:2], rest[2:]
         for step in range(STEPS):
             if step:
-                state, grid, pay, *weights, edge = call(
+                state, grid, pay, *weights = call(
                     "scatter_next",
-                    functools.partial(next_kernel, step, links, width),
-                    (state_type, grid_type, band_type) + weight_types + (edge_type,),
+                    functools.partial(next_kernel, step, links),
+                    (state_type, grid_type, band_type) + weight_types,
                     [smem] * 4 + [vmem] * (links + 1),
                     scatter_scratch,
-                )(*windows[:2], *moves, state, *arrived)
+                )(*anchors, *moves, state, *arrived)
             band0 = swap(pay[0], 0)
             band1 = gather_pairs(pay[1])
             total, pay = call(
@@ -639,26 +653,26 @@
                 [vmem] * 3,
             )(grid, band0, band1)
             bands = [swap(pay[k], 2 + k) for k in range(links - 2)]
-            ahead = call(
+            ahead, edge, rank, *picked = call(
                 "gather_inner",
-                functools.partial(inner_kernel, step, width),
-                (state_type,),
-                [smem] * 2 + [vmem] * 4,
+                functools.partial(inner_kernel, step, links, width),
+                (state_type, edge_type, edge_type) + (sent_type,) * links,
+                [smem] * 3 + [vmem] * 4,
                 [speed_scratch],
                 1 << 32,
-            )(*windows[2:], state, total, *weights)
-            edge = pltpu.with_memory_space_constraint(edge, pltpu.SMEM)
+            )(*anchors, moves[0], state, total, *weights)
+            edge, rank = (pltpu.with_memory_space_constraint(x, pltpu.SMEM) for x in (edge, rank))
             state, *sent = call(
                 "gather_edge",
-                functools.partial(edge_kernel, step, links, width),
+                functools.partial(edge_kernel, step, links, width, cap),
                 (state_type,) + (sent_type,) * links,
-                [smem] * 4 + [vmem] * (3 + links),
+                [smem] * 4 + [vmem] * (3 + 2 * links),
                 [
                     speed_scratch,
                     pltpu.VMEM(grid_type.shape, f32),
                     pltpu.VMEM((FIELDS, ROWS, LANES), f32),
                 ],
-            )(*windows[2:], moves[0], edge, state, total, *bands, *weights, *ahead)
+            )(*anchors, edge, rank, state, total, *bands, *weights, ahead, *picked)
             arrived = [
                 gather_pairs(x) if link == 1 else swap(x, link) for link, x in enumerate(sent)
             ]

time: 40 us -> 39.4 us (0.985)
  transfers between devices with their start and end apart: 8 -> 8, of which waited for: 1 -> 1; matrix products, arithmetic and copies ran while one was open for 0% -> 0% of each run, Pallas kernels for 8% -> 9%
where the time goes in v6:
time: 39.4 us; the launch traced here: 39.2 us
  blocking collectives  20 us (51%)
  Pallas kernels  11.5 us (29%)
  starting transfers between devices  7.2 us (18%)
  waiting for transfers between devices  0.42 us (1%)
    all_gather x4, blocking collectives, gather_pairs(): lax.all_gather(x, ('down', 'cross'), axis_index_groups=odd_groups(size_do...  20 us
    ppermute x8, starting transfers between devices, swap(): return lax.ppermute(x, name, swap_pairs(size, second))  7.2 us
    pallas_call x2, Pallas kernels, on_device(): call('gather_inner', functools.partial(inner_kernel, step, links, width),...  3.57 us
    pallas_call x1, Pallas kernels, on_device(): call('scatter_first', functools.partial(first_kernel, 0), (state_type, gr...  3.11 us
    pallas_call x1, Pallas kernels, on_device(): call('scatter_next', functools.partial(next_kernel, step, links), (state_...  2.14 us
    pallas_call x2, Pallas kernels, on_device(): call('gather_edge', functools.partial(edge_kernel, step, links, width, ca...  1.4 us
    pallas_call x1, Pallas kernels, on_device(): call('settle_last', functools.partial(last_kernel, STEPS - 1, links), (pl...  1.11 us
  transfers between devices with their start and end apart: 8, of which 1 were waited for; matrix products, arithmetic and copies ran while one was open for 0% of the time, Pallas kernels for 9%

profile of v6, /device:TPU:11, one launch (start us, length us, event | category | flops | bytes accessed | tf_op | source)
XLA Modules:
  0.0 39.2 jit_solution(2230456025353742878)
XLA Ops:
  0.0 3.1 %scatter_first.1 = (f32[12,136,128]{2,1,0:T(8,128)S(1)}, f32[3,72,128]{2,1,0:T(8,128)S(1)}, f32[2,3,24,128]{3,2,1,0:T(8,128)S(1)}, bf16[128,32,256]{2,1,0:T(8,12...) custom-call(s32[2,128]{1,0:T(2,128)} %down_in.1, ...), custom_call_target="tpu_custom_call" | custom-call | bytes 1048576 | tf_op jit(solution)/shard_map/scatter_first/pallas_call | solution.py:623
  3.1 0.7 %collective-permute-start = (f32[3,24,128]{2,1,0:T(8,128)S(1)}, f32[3,24,128]{2,1,0:T(8,128)S(1)}, u32[]{:S(2)}, u32[]{:S(2)}) collective-permute-start(f32[3,24,128]{2,1,0:T(8,128)S(1)} %get-tuple-element.84), channel_id=1, source_target_pairs={{0,2},{2,0},{4,6},{6,4},{8,10},{10,8},{12,14},{14,12},{16,18},{18,... | collective-permute-start | bytes 110600 | tf_op jit(solution)/shard_map/ppermute | solution.py:571
  3.9 4.6 %all_gather.18.band1 = f32[2,3,24,128]{3,2,1,0:T(8,128)S(1)} all-gather(f32[1,3,24,128]{3,2,1,0:T(8,128)S(1)} %get-tuple-element.83), channel_id=1, replica_groups={{0,1},{30,31},{2,4},{3,5},{6,8},{7,9},{10,12},{11,13},{14,16},{15,17},{..., dimensions={0}, use_global_device_ids=true | all-gather | bytes 110592 | tf_op jit(solution)/shard_map/all_gather | solution.py:574
  8.5 0.0 collective-permute-done.band0
  8.5 0.1 add_down.2
  8.6 0.3 collective-permute-start.1
  8.8 1.8 %gather_inner.2 = (f32[12,136,128]{2,1,0:T(8,128)S(1)}, s32[129]{0:T(256)S(4)}, s32[129]{0:T(256)S(4)}, f32[160,128]{1,0:T(8,128)S(1)}, f32[160,128]{1,0:T(8,128)S(1)}, /*index=5*/f32[160,128]{1,0:T(8,128)S(1)}) custom-call(s32[2,128]{1,0:T(2,128)S(4)} %get-tuple-element.45.anchor_down, s32[2,128]{1,0:T(2,128)S(4)} %get-tuple-element.46.anchor_cross, ...), custom_call_target="tpu_custom_call" | custom-call | flops 4294967296 | bytes 1048576 | tf_op jit(solution)/shard_map/gather_inner/pallas_call | solution.py:656
  10.6 0.4 %collective-permute-done.1.rest_0_ = f32[8,128]{1,0:T(8,128)S(1)} collective-permute-done((f32[8,128]{1,0:T(8,128)S(1)}, f32[8,128]{1,0:T(8,128)S(1)}, u32[]{:S(2)}, u32[]{:S(2)}) %collective-permute-start.1) | collective-permute-done | bytes 4128 | tf_op jit(solution)/shard_map/ppermute | solution.py:571
  11.0 0.7 %gather_edge.2 = (f32[12,136,128]{2,1,0:T(8,128)S(1)}, f32[160,128]{1,0:T(8,128)S(1)}, f32[160,128]{1,0:T(8,128)S(1)}, f32[160,128]{1,0:T(8,128)S(1)}) custom-call(s32[2,128]{1,0:T(2,128)S(4)} %get-tuple-element.45.anchor_down, s32[2,128]{1,0:T(2,128)S(4)} %get-tuple-element.46.anchor_cross, s32[129]{0:T(256)S(4)} %get-tuple-element.53.edge, ...), custom_call_target="tpu_custom_call" | custom-call | bytes 1048576 | tf_op jit(solution)/shard_map/gather_edge/pallas_call | solution.py:665
  11.7 1.7 %collective-permute-start.2 = (f32[160,128]{1,0:T(8,128)S(1)}, f32[160,128]{1,0:T(8,128)S(1)}, u32[]{:S(2)}, u32[]{:S(2)}) collective-permute-start(f32[160,128]{1,0:T(8,128)S(1)} %get-tuple-element.61), channel_id=1, source_target_pairs={{0,2},{2,0},{4,6},{6,4},{8,10},{10,8},{12,14},{14,12},{16,18},{18,... | collective-permute-start | bytes 245768 | tf_op jit(solution)/shard_map/ppermute | solution.py:571
  13.5 0.3 collective-permute-start.3
  13.7 5.4 %all-gather = f32[320,128]{1,0:T(8,128)S(1)} all-gather(f32[160,128]{1,0:T(8,128)S(1)} %get-tuple-element.62), channel_id=2, replica_groups={{0,1},{30,31},{2,4},{3,5},{6,8},{7,9},{10,12},{11,13},{14,16},{15,17},{..., dimensions={0}, use_global_device_ids=true | all-gather | bytes 245760 | tf_op jit(solution)/shard_map/all_gather | solution.py:574
  19.1 0.0 collective-permute-done.2.rest_0_
  19.2 0.0 collective-permute-done.3.rest_2_
  19.2 2.1 %scatter_next.1 = (f32[12,136,128]{2,1,0:T(8,128)S(1)}, f32[3,72,128]{2,1,0:T(8,128)S(1)}, f32[2,3,24,128]{3,2,1,0:T(8,128)S(1)}, bf16[128,32,256]{2,1,0:T(8,128)(2,1)S(1)}, f32[128,16,128]{2,1,0:T(8,128)S(1)}) custom-call(s32[2,128]{1,0:T(2,128)S(4)} %get-tuple-element.45.anchor_down, s32[2,128]{1,0:T(2,128)S(4)} %get-tuple-element.46.anchor_cross, ...), custom_call_target="tpu_custom_call" | custom-call | bytes 1048576 | tf_op jit(solution)/shard_map/scatter_next/pallas_call | solution.py:640
  21.3 0.5 %collective-permute-start.4 = (f32[3,24,128]{2,1,0:T(8,128)S(1)}, f32[3,24,128]{2,1,0:T(8,128)S(1)}, u32[]{:S(2)}, u32[]{:S(2)}) collective-permute-start(f32[3,24,128]{2,1,0:T(8,128)S(1)} %get-tuple-element.82), channel_id=1, source_target_pairs={{0,2},{2,0},{4,6},{6,4},{8,10},{10,8},{12,14},{14,12},{16,18},{18,... | collective-permute-start | bytes 110600 | tf_op jit(solution)/shard_map/ppermute | solution.py:571
  21.9 4.6 %all_gather.21.band1 = f32[2,3,24,128]{3,2,1,0:T(8,128)S(1)} all-gather(f32[1,3,24,128]{3,2,1,0:T(8,128)S(1)} %get-tuple-element.81), channel_id=1, replica_groups={{0,1},{30,31},{2,4},{3,5},{6,8},{7,9},{10,12},{11,13},{14,16},{15,17},{..., dimensions={0}, use_global_device_ids=true | all-gather | bytes 110592 | tf_op jit(solution)/shard_map/all_gather | solution.py:574
  26.4 0.0 collective-permute-done.4.band0
  26.4 0.1 add_down.3
  26.5 1.2 %collective-permute-start.5 = (f32[8,128]{1,0:T(8,128)S(1)}, f32[8,128]{1,0:T(8,128)S(1)}, u32[]{:S(2)}, u32[]{:S(2)}) collective-permute-start(f32[8,128]{1,0:T(8,128)S(1)} %slice_bitcast_fusion.2), channel_id=1, source_target_pairs={{0,1},{1,0},{2,3},{3,2},{4,5},{5,4},{6,7},{7,6},{8,9},{9,8},{10,11... | collective-permute-start | bytes 12296 | tf_op jit(solution)/shard_map/ppermute | solution.py:571
  27.8 1.8 %gather_inner.3 = (f32[12,136,128]{2,1,0:T(8,128)S(1)}, s32[129]{0:T(256)S(4)}, s32[129]{0:T(256)S(4)}, f32[160,128]{1,0:T(8,128)S(1)}, f32[160,128]{1,0:T(8,128)S(1)}, /*index=5*/f32[160,128]{1,0:T(8,128)S(1)}) custom-call(s32[2,128]{1,0:T(2,128)S(4)} %get-tuple-element.45.anchor_down, s32[2,128]{1,0:T(2,128)S(4)} %get-tuple-element.46.anchor_cross, ...), custom_call_target="tpu_custom_call" | custom-call | flops 4294967296 | bytes 1048576 | tf_op jit(solution)/shard_map/gather_inner/pallas_call | solution.py:656
  29.6 0.0 collective-permute-done.5.rest_0_
  29.6 0.7 %gather_edge.3 = (f32[12,136,128]{2,1,0:T(8,128)S(1)}, f32[160,128]{1,0:T(8,128)S(1)}, f32[160,128]{1,0:T(8,128)S(1)}, f32[160,128]{1,0:T(8,128)S(1)}) custom-call(s32[2,128]{1,0:T(2,128)S(4)} %get-tuple-element.45.anchor_down, s32[2,128]{1,0:T(2,128)S(4)} %get-tuple-element.46.anchor_cross, s32[129]{0:T(256)S(4)} %get-tuple-element.70.edge, ...), custom_call_target="tpu_custom_call" | custom-call | bytes 1048576 | tf_op jit(solution)/shard_map/gather_edge/pallas_call | solution.py:665
  30.3 1.2 %collective-permute-start.6 = (f32[160,128]{1,0:T(8,128)S(1)}, f32[160,128]{1,0:T(8,128)S(1)}, u32[]{:S(2)}, u32[]{:S(2)}) collective-permute-start(f32[160,128]{1,0:T(8,128)S(1)} %get-tuple-element.78), channel_id=1, source_target_pairs={{0,2},{2,0},{4,6},{6,4},{8,10},{10,8},{12,14},{14,12},{16,18},{18,... | collective-permute-start | bytes 245768 | tf_op jit(solution)/shard_map/ppermute | solution.py:571
  31.4 1.2 %collective-permute-start.7 = (f32[160,128]{1,0:T(8,128)S(1)}, f32[160,128]{1,0:T(8,128)S(1)}, u32[]{:S(2)}, u32[]{:S(2)}) collective-permute-start(f32[160,128]{1,0:T(8,128)S(1)} %get-tuple-element.80), channel_id=1, source_target_pairs={{0,1},{1,0},{2,3},{3,2},{4,5},{5,4},{6,7},{7,6},{8,9},{9,8},{10,11... | collective-permute-start | bytes 245768 | tf_op jit(solution)/shard_map/ppermute | solution.py:571
  32.7 5.4 %all-gather.1 = f32[320,128]{1,0:T(8,128)S(1)} all-gather(f32[160,128]{1,0:T(8,128)S(1)} %get-tuple-element.79), channel_id=3, replica_groups={{0,1},{30,31},{2,4},{3,5},{6,8},{7,9},{10,12},{11,13},{14,16},{15,17},{..., dimensions={0}, use_global_device_ids=true | all-gather | bytes 245760 | tf_op jit(solution)/shard_map/all_gather | solution.py:574
  38.1 0.0 collective-permute-done.6.rest_0_
  38.1 0.0 collective-permute-done.7.rest_2_
  38.1 1.1 %settle_last.1 = f32[12,128,128]{2,1,0:T(8,128)} custom-call(s32[2,4,13]{2,1,0:T(4,128)S(4)} %get-tuple-element.43.slots, s32[2,4]{1,0:T(2,128)S(4)} %get-tuple-element.44.counts, f32[12,136,128]{2,1,0:T(8,128)S(1)} %get-tuple-element.77.old, f32[160,128]{1,0:T(8,128)S(1)} %collective-permute-done.6.rest_0_, f32[2,160,128]{2,1,0:T(8,128)S(1)} %bitcast.14, ...), custom_call_target="tpu_custom_call" | custom-call | bytes 1048576 | tf_op jit(solution)/shard_map/settle_last/pallas_call | solution.py:679
  (4 shorter events, 0.0 us)
Async XLA Ops:
  3.1 5.3 %collective-permute-start = (f32[3,24,128]{2,1,0:T(8,128)S(1)}, f32[3,24,128]{2,1,0:T(8,128)S(1)}, u32[]{:S(2)}, u32[]{:S(2)}) collective-permute-start(f32[3,24,128]{2,1,0:T(8,128)S(1)} %get-tuple-element.84), channel_id=1, source_target_pairs={{0,2},{2,0},{4,6},{6,4},{8,10},{10,8},{12,14},{14,12},{16,18},{18,... | collective-permute-start | bytes 110600 | tf_op jit(solution)/shard_map/ppermute | solution.py:571
  8.6 2.5 %collective-permute-start.1 = (f32[8,128]{1,0:T(8,128)S(1)}, f32[8,128]{1,0:T(8,128)S(1)}, u32[]{:S(2)}, u32[]{:S(2)}) collective-permute-start(f32[8,128]{1,0:T(8,128)S(1)} %slice_bitcast_fusion.3), channel_id=1, source_target_pairs={{0,1},{1,0},{2,3},{3,2},{4,5},{5,4},{6,7},{7,6},{8,9},{9,8},{10,11... | collective-permute-start | bytes 12296 | tf_op jit(solution)/shard_map/ppermute | solution.py:571
  11.7 7.4 %collective-permute-start.2 = (f32[160,128]{1,0:T(8,128)S(1)}, f32[160,128]{1,0:T(8,128)S(1)}, u32[]{:S(2)}, u32[]{:S(2)}) collective-permute-start(f32[160,128]{1,0:T(8,128)S(1)} %get-tuple-element.61), channel_id=1, source_target_pairs={{0,2},{2,0},{4,6},{6,4},{8,10},{10,8},{12,14},{14,12},{16,18},{18,... | collective-permute-start | bytes 245768 | tf_op jit(solution)/shard_map/ppermute | solution.py:571
  13.5 5.7 %collective-permute-start.3 = (f32[160,128]{1,0:T(8,128)S(1)}, f32[160,128]{1,0:T(8,128)S(1)}, u32[]{:S(2)}, u32[]{:S(2)}) collective-permute-start(f32[160,128]{1,0:T(8,128)S(1)} %get-tuple-element.63), channel_id=1, source_target_pairs={{0,1},{1,0},{2,3},{3,2},{4,5},{5,4},{6,7},{7,6},{8,9},{9,8},{10,11... | collective-permute-start | bytes 245768 | tf_op jit(solution)/shard_map/ppermute | solution.py:571
  21.3 5.1 %collective-permute-start.4 = (f32[3,24,128]{2,1,0:T(8,128)S(1)}, f32[3,24,128]{2,1,0:T(8,128)S(1)}, u32[]{:S(2)}, u32[]{:S(2)}) collective-permute-start(f32[3,24,128]{2,1,0:T(8,128)S(1)} %get-tuple-element.82), channel_id=1, source_target_pairs={{0,2},{2,0},{4,6},{6,4},{8,10},{10,8},{12,14},{14,12},{16,18},{18,... | collective-permute-start | bytes 110600 | tf_op jit(solution)/shard_map/ppermute | solution.py:571
  26.5 3.0 %collective-permute-start.5 = (f32[8,128]{1,0:T(8,128)S(1)}, f32[8,128]{1,0:T(8,128)S(1)}, u32[]{:S(2)}, u32[]{:S(2)}) collective-permute-start(f32[8,128]{1,0:T(8,128)S(1)} %slice_bitcast_fusion.2), channel_id=1, source_target_pairs={{0,1},{1,0},{2,3},{3,2},{4,5},{5,4},{6,7},{7,6},{8,9},{9,8},{10,11... | collective-permute-start | bytes 12296 | tf_op jit(solution)/shard_map/ppermute | solution.py:571
  30.3 7.8 %collective-permute-start.6 = (f32[160,128]{1,0:T(8,128)S(1)}, f32[160,128]{1,0:T(8,128)S(1)}, u32[]{:S(2)}, u32[]{:S(2)}) collective-permute-start(f32[160,128]{1,0:T(8,128)S(1)} %get-tuple-element.78), channel_id=1, source_target_pairs={{0,2},{2,0},{4,6},{6,4},{8,10},{10,8},{12,14},{14,12},{16,18},{18,... | collective-permute-start | bytes 245768 | tf_op jit(solution)/shard_map/ppermute | solution.py:571
  31.4 6.6 %collective-permute-start.7 = (f32[160,128]{1,0:T(8,128)S(1)}, f32[160,128]{1,0:T(8,128)S(1)}, u32[]{:S(2)}, u32[]{:S(2)}) collective-permute-start(f32[160,128]{1,0:T(8,128)S(1)} %get-tuple-element.80), channel_id=1, source_target_pairs={{0,1},{1,0},{2,3},{3,2},{4,5},{5,4},{6,7},{7,6},{8,9},{9,8},{10,11... | collective-permute-start | bytes 245768 | tf_op jit(solution)/shard_map/ppermute | solution.py:571

commit v7 on v6

--- a/solution.py
+++ b/solution.py
@@ -505,40 +505,39 @@
     wide, tall, before = rest[links - 2 : links + 1]
     picked_before, after = rest[links + 1 : 2 * links + 1], rest[2 * links + 1]
     sent = rest[2 * links + 2 : 3 * links + 2]
-    speed, sums, rows = rest[3 * links + 2 :]
+    speed, sums, rows, mail = rest[3 * links + 2 :]
     plane = picked_before[0].shape[0]
     blocks = wide.shape[0]
     after[:, :blocks, :] = before[:, :blocks, :]
-    for out, given in zip(sent, picked_before):
-        out[:plane, :] = given[...]
+    for link, given in enumerate(picked_before):
+        mail[link * plane : (link + 1) * plane, :] = given[...]
     add_across(total, bands, sums, width)
     node_velocity(sums, speed, width)
     place = speed_place(anchor_down, anchor_cross, step)
     lane, row = gather_lanes()
     count = edge[blocks]
+    used = [f for f in range(FIELDS) if f not in (2, 3, 7)]
 
     def eight(q, carry):
         picked = [edge[jnp.minimum(q * ROWS + k, count - 1)] for k in range(ROWS)]
         for k, slot in enumerate(picked):
-            for f in range(FIELDS):
+            for f in used:
                 rows[f, k : k + 1, :] = state[f, pl.ds(slot, 1), :]
-        field = [rows[f] for f in range(FIELDS)]
+        field = {f: rows[f] for f in used}
         result = gather_eight((wide, tall), speed, picked, place, field, lane, row)
         for f, value in result.items():
             rows[f] = value
         for k, slot in enumerate(picked):
             start = rank[slot]
             for f in result:
-                after[f, pl.ds(slot, 1), :] = rows[f, k : k + 1, :]
-            for link in range(links):
-                leaves = (start >= link * plane) & (start < (link + 1) * plane)
-                first = jnp.where(leaves, start - link * plane, plane - 1)
-                between = jnp.where(leaves, cap, 0)
-                for f in result:
-                    sent[link][pl.ds(first + f * between, 1), :] = rows[f, k : k + 1, :]
+                value = rows[f, k : k + 1, :]
+                after[f, pl.ds(slot, 1), :] = value
+                mail[pl.ds(start + f * cap, 1), :] = value
         return carry
 
     lax.fori_loop(0, (count + ROWS - 1) // ROWS, eight, 0)
+    for link, out in enumerate(sent):
+        out[...] = mail[link * plane : (link + 1) * plane, :]
 
 
 def swap_pairs(size, first):
@@ -601,7 +600,7 @@
         grid_type = array(tiles, CHANNELS * height, LANES)
         band_type = array(2, tiles, CHANNELS * BAND, LANES)
         state_type = array(FIELDS, blocks + ROWS, LANES)
-        plane = (FIELDS * cap // 8 + 1) * 8
+        plane = -(-FIELDS * cap // 8) * 8
         sent_type = array(plane, LANES)
         weight_types = (
             array(blocks, 2 * WIN_CROSS, 2 * LANES, dtype=jnp.bfloat16),
@@ -671,6 +670,7 @@
                     speed_scratch,
                     pltpu.VMEM(grid_type.shape, f32),
                     pltpu.VMEM((FIELDS, ROWS, LANES), f32),
+                    pltpu.VMEM(((links + 1) * plane, LANES), f32),
                 ],
             )(*anchors, edge, rank, state, total, *bands, *weights, ahead, *picked)
             arrived = [

time: 39.4 us -> 39.3 us (level)
  no operation moved by 1% of the time
where the time goes in v7:
time: 39.3 us; the launch traced here: 39 us
  blocking collectives  20 us (51%)
  Pallas kernels  11.3 us (29%)
  starting transfers between devices  7.16 us (18%)
  waiting for transfers between devices  0.43 us (1%)
    all_gather x4, blocking collectives, gather_pairs(): lax.all_gather(x, ('down', 'cross'), axis_index_groups=odd_groups(size_do...  20 us
    ppermute x8, starting transfers between devices, swap(): return lax.ppermute(x, name, swap_pairs(size, second))  7.16 us
    pallas_call x2, Pallas kernels, on_device(): call('gather_inner', functools.partial(inner_kernel, step, links, width),...  3.57 us
    pallas_call x1, Pallas kernels, on_device(): call('scatter_first', functools.partial(first_kernel, 0), (state_type, gr...  3.12 us
    pallas_call x1, Pallas kernels, on_device(): call('scatter_next', functools.partial(next_kernel, step, links), (state_...  2.15 us
    pallas_call x2, Pallas kernels, on_device(): call('gather_edge', functools.partial(edge_kernel, step, links, width, ca...  1.17 us
    pallas_call x1, Pallas kernels, on_device(): call('settle_last', functools.partial(last_kernel, STEPS - 1, links), (pl...  1.11 us
  transfers between devices with their start and end apart: 8, of which 1 were waited for; matrix products, arithmetic and copies ran while one was open for 0% of the time, Pallas kernels for 9%

profile of v7, /device:TPU:11, one launch (start us, length us, event | category | flops | bytes accessed | tf_op | source)
XLA Modules:
  0.0 39.0 jit_solution(10396290114408677036)
XLA Ops:
  0.0 3.1 %scatter_first.1 = (f32[12,136,128]{2,1,0:T(8,128)S(1)}, f32[3,72,128]{2,1,0:T(8,128)S(1)}, f32[2,3,24,128]{3,2,1,0:T(8,128)S(1)}, bf16[128,32,256]{2,1,0:T(8,12...) custom-call(s32[2,128]{1,0:T(2,128)} %down_in.1, ...), custom_call_target="tpu_custom_call" | custom-call | bytes 1048576 | tf_op jit(solution)/shard_map/scatter_first/pallas_call | solution.py:622
  3.1 0.7 %collective-permute-start = (f32[3,24,128]{2,1,0:T(8,128)S(1)}, f32[3,24,128]{2,1,0:T(8,128)S(1)}, u32[]{:S(2)}, u32[]{:S(2)}) collective-permute-start(f32[3,24,128]{2,1,0:T(8,128)S(1)} %get-tuple-element.84), channel_id=1, source_target_pairs={{0,2},{2,0},{4,6},{6,4},{8,10},{10,8},{12,14},{14,12},{16,18},{18,... | collective-permute-start | bytes 110600 | tf_op jit(solution)/shard_map/ppermute | solution.py:570
  3.9 4.6 %all_gather.18.band1 = f32[2,3,24,128]{3,2,1,0:T(8,128)S(1)} all-gather(f32[1,3,24,128]{3,2,1,0:T(8,128)S(1)} %get-tuple-element.83), channel_id=1, replica_groups={{0,1},{30,31},{2,4},{3,5},{6,8},{7,9},{10,12},{11,13},{14,16},{15,17},{..., dimensions={0}, use_global_device_ids=true | all-gather | bytes 110592 | tf_op jit(solution)/shard_map/all_gather | solution.py:573
  8.5 0.0 collective-permute-done.band0
  8.5 0.1 add_down.2
  8.6 0.3 collective-permute-start.1
  8.8 1.8 %gather_inner.2 = (f32[12,136,128]{2,1,0:T(8,128)S(1)}, s32[129]{0:T(256)S(4)}, s32[129]{0:T(256)S(4)}, f32[160,128]{1,0:T(8,128)S(1)}, f32[160,128]{1,0:T(8,128)S(1)}, /*index=5*/f32[160,128]{1,0:T(8,128)S(1)}) custom-call(s32[2,128]{1,0:T(2,128)S(4)} %get-tuple-element.45.anchor_down, s32[2,128]{1,0:T(2,128)S(4)} %get-tuple-element.46.anchor_cross, ...), custom_call_target="tpu_custom_call" | custom-call | flops 4294967296 | bytes 1048576 | tf_op jit(solution)/shard_map/gather_inner/pallas_call | solution.py:655
  10.6 0.4 %collective-permute-done.1.rest_0_ = f32[8,128]{1,0:T(8,128)S(1)} collective-permute-done((f32[8,128]{1,0:T(8,128)S(1)}, f32[8,128]{1,0:T(8,128)S(1)}, u32[]{:S(2)}, u32[]{:S(2)}) %collective-permute-start.1) | collective-permute-done | bytes 4128 | tf_op jit(solution)/shard_map/ppermute | solution.py:570
  11.0 0.6 %gather_edge.2 = (f32[12,136,128]{2,1,0:T(8,128)S(1)}, f32[160,128]{1,0:T(8,128)S(1)}, f32[160,128]{1,0:T(8,128)S(1)}, f32[160,128]{1,0:T(8,128)S(1)}) custom-call(s32[2,128]{1,0:T(2,128)S(4)} %get-tuple-element.45.anchor_down, s32[2,128]{1,0:T(2,128)S(4)} %get-tuple-element.46.anchor_cross, s32[129]{0:T(256)S(4)} %get-tuple-element.53.edge, ...), custom_call_target="tpu_custom_call" | custom-call | bytes 1048576 | tf_op jit(solution)/shard_map/gather_edge/pallas_call | solution.py:664
  11.6 1.7 %collective-permute-start.2 = (f32[160,128]{1,0:T(8,128)S(1)}, f32[160,128]{1,0:T(8,128)S(1)}, u32[]{:S(2)}, u32[]{:S(2)}) collective-permute-start(f32[160,128]{1,0:T(8,128)S(1)} %get-tuple-element.61), channel_id=1, source_target_pairs={{0,2},{2,0},{4,6},{6,4},{8,10},{10,8},{12,14},{14,12},{16,18},{18,... | collective-permute-start | bytes 245768 | tf_op jit(solution)/shard_map/ppermute | solution.py:570
  13.3 0.7 %collective-permute-start.3 = (f32[160,128]{1,0:T(8,128)S(1)}, f32[160,128]{1,0:T(8,128)S(1)}, u32[]{:S(2)}, u32[]{:S(2)}) collective-permute-start(f32[160,128]{1,0:T(8,128)S(1)} %get-tuple-element.63), channel_id=1, source_target_pairs={{0,1},{1,0},{2,3},{3,2},{4,5},{5,4},{6,7},{7,6},{8,9},{9,8},{10,11... | collective-permute-start | bytes 245768 | tf_op jit(solution)/shard_map/ppermute | solution.py:570
  14.0 5.4 %all-gather = f32[320,128]{1,0:T(8,128)S(1)} all-gather(f32[160,128]{1,0:T(8,128)S(1)} %get-tuple-element.62), channel_id=2, replica_groups={{0,1},{30,31},{2,4},{3,5},{6,8},{7,9},{10,12},{11,13},{14,16},{15,17},{..., dimensions={0}, use_global_device_ids=true | all-gather | bytes 245760 | tf_op jit(solution)/shard_map/all_gather | solution.py:573
  19.4 0.0 collective-permute-done.2.rest_0_
  19.4 0.0 collective-permute-done.3.rest_2_
  19.4 2.1 %scatter_next.1 = (f32[12,136,128]{2,1,0:T(8,128)S(1)}, f32[3,72,128]{2,1,0:T(8,128)S(1)}, f32[2,3,24,128]{3,2,1,0:T(8,128)S(1)}, bf16[128,32,256]{2,1,0:T(8,128)(2,1)S(1)}, f32[128,16,128]{2,1,0:T(8,128)S(1)}) custom-call(s32[2,128]{1,0:T(2,128)S(4)} %get-tuple-element.45.anchor_down, s32[2,128]{1,0:T(2,128)S(4)} %get-tuple-element.46.anchor_cross, ...), custom_call_target="tpu_custom_call" | custom-call | bytes 1048576 | tf_op jit(solution)/shard_map/scatter_next/pallas_call | solution.py:639
  21.6 0.5 %collective-permute-start.4 = (f32[3,24,128]{2,1,0:T(8,128)S(1)}, f32[3,24,128]{2,1,0:T(8,128)S(1)}, u32[]{:S(2)}, u32[]{:S(2)}) collective-permute-start(f32[3,24,128]{2,1,0:T(8,128)S(1)} %get-tuple-element.82), channel_id=1, source_target_pairs={{0,2},{2,0},{4,6},{6,4},{8,10},{10,8},{12,14},{14,12},{16,18},{18,... | collective-permute-start | bytes 110600 | tf_op jit(solution)/shard_map/ppermute | solution.py:570
  22.1 4.6 %all_gather.21.band1 = f32[2,3,24,128]{3,2,1,0:T(8,128)S(1)} all-gather(f32[1,3,24,128]{3,2,1,0:T(8,128)S(1)} %get-tuple-element.81), channel_id=1, replica_groups={{0,1},{30,31},{2,4},{3,5},{6,8},{7,9},{10,12},{11,13},{14,16},{15,17},{..., dimensions={0}, use_global_device_ids=true | all-gather | bytes 110592 | tf_op jit(solution)/shard_map/all_gather | solution.py:573
  26.7 0.0 collective-permute-done.4.band0
  26.7 0.1 add_down.3
  26.8 0.8 %collective-permute-start.5 = (f32[8,128]{1,0:T(8,128)S(1)}, f32[8,128]{1,0:T(8,128)S(1)}, u32[]{:S(2)}, u32[]{:S(2)}) collective-permute-start(f32[8,128]{1,0:T(8,128)S(1)} %slice_bitcast_fusion.2), channel_id=1, source_target_pairs={{0,1},{1,0},{2,3},{3,2},{4,5},{5,4},{6,7},{7,6},{8,9},{9,8},{10,11... | collective-permute-start | bytes 12296 | tf_op jit(solution)/shard_map/ppermute | solution.py:570
  27.6 1.8 %gather_inner.3 = (f32[12,136,128]{2,1,0:T(8,128)S(1)}, s32[129]{0:T(256)S(4)}, s32[129]{0:T(256)S(4)}, f32[160,128]{1,0:T(8,128)S(1)}, f32[160,128]{1,0:T(8,128)S(1)}, /*index=5*/f32[160,128]{1,0:T(8,128)S(1)}) custom-call(s32[2,128]{1,0:T(2,128)S(4)} %get-tuple-element.45.anchor_down, s32[2,128]{1,0:T(2,128)S(4)} %get-tuple-element.46.anchor_cross, ...), custom_call_target="tpu_custom_call" | custom-call | flops 4294967296 | bytes 1048576 | tf_op jit(solution)/shard_map/gather_inner/pallas_call | solution.py:655
  29.4 0.0 collective-permute-done.5.rest_0_
  29.4 0.6 %gather_edge.3 = (f32[12,136,128]{2,1,0:T(8,128)S(1)}, f32[160,128]{1,0:T(8,128)S(1)}, f32[160,128]{1,0:T(8,128)S(1)}, f32[160,128]{1,0:T(8,128)S(1)}) custom-call(s32[2,128]{1,0:T(2,128)S(4)} %get-tuple-element.45.anchor_down, s32[2,128]{1,0:T(2,128)S(4)} %get-tuple-element.46.anchor_cross, s32[129]{0:T(256)S(4)} %get-tuple-element.70.edge, ...), custom_call_target="tpu_custom_call" | custom-call | bytes 1048576 | tf_op jit(solution)/shard_map/gather_edge/pallas_call | solution.py:664
  30.0 1.5 %collective-permute-start.6 = (f32[160,128]{1,0:T(8,128)S(1)}, f32[160,128]{1,0:T(8,128)S(1)}, u32[]{:S(2)}, u32[]{:S(2)}) collective-permute-start(f32[160,128]{1,0:T(8,128)S(1)} %get-tuple-element.78), channel_id=1, source_target_pairs={{0,2},{2,0},{4,6},{6,4},{8,10},{10,8},{12,14},{14,12},{16,18},{18,... | collective-permute-start | bytes 245768 | tf_op jit(solution)/shard_map/ppermute | solution.py:570
  31.6 0.8 %collective-permute-start.7 = (f32[160,128]{1,0:T(8,128)S(1)}, f32[160,128]{1,0:T(8,128)S(1)}, u32[]{:S(2)}, u32[]{:S(2)}) collective-permute-start(f32[160,128]{1,0:T(8,128)S(1)} %get-tuple-element.80), channel_id=1, source_target_pairs={{0,1},{1,0},{2,3},{3,2},{4,5},{5,4},{6,7},{7,6},{8,9},{9,8},{10,11... | collective-permute-start | bytes 245768 | tf_op jit(solution)/shard_map/ppermute | solution.py:570
  32.4 5.4 %all-gather.1 = f32[320,128]{1,0:T(8,128)S(1)} all-gather(f32[160,128]{1,0:T(8,128)S(1)} %get-tuple-element.79), channel_id=3, replica_groups={{0,1},{30,31},{2,4},{3,5},{6,8},{7,9},{10,12},{11,13},{14,16},{15,17},{..., dimensions={0}, use_global_device_ids=true | all-gather | bytes 245760 | tf_op jit(solution)/shard_map/all_gather | solution.py:573
  37.8 0.0 collective-permute-done.6.rest_0_
  37.8 0.0 collective-permute-done.7.rest_2_
  37.8 1.1 %settle_last.1 = f32[12,128,128]{2,1,0:T(8,128)} custom-call(s32[2,4,13]{2,1,0:T(4,128)S(4)} %get-tuple-element.43.slots, s32[2,4]{1,0:T(2,128)S(4)} %get-tuple-element.44.counts, f32[12,136,128]{2,1,0:T(8,128)S(1)} %get-tuple-element.77.old, f32[160,128]{1,0:T(8,128)S(1)} %collective-permute-done.6.rest_0_, f32[2,160,128]{2,1,0:T(8,128)S(1)} %bitcast.14, ...), custom_call_target="tpu_custom_call" | custom-call | bytes 1048576 | tf_op jit(solution)/shard_map/settle_last/pallas_call | solution.py:679
  (4 shorter events, 0.0 us)
Async XLA Ops:
  3.1 5.3 %collective-permute-start = (f32[3,24,128]{2,1,0:T(8,128)S(1)}, f32[3,24,128]{2,1,0:T(8,128)S(1)}, u32[]{:S(2)}, u32[]{:S(2)}) collective-permute-start(f32[3,24,128]{2,1,0:T(8,128)S(1)} %get-tuple-element.84), channel_id=1, source_target_pairs={{0,2},{2,0},{4,6},{6,4},{8,10},{10,8},{12,14},{14,12},{16,18},{18,... | collective-permute-start | bytes 110600 | tf_op jit(solution)/shard_map/ppermute | solution.py:570
  8.6 2.5 %collective-permute-start.1 = (f32[8,128]{1,0:T(8,128)S(1)}, f32[8,128]{1,0:T(8,128)S(1)}, u32[]{:S(2)}, u32[]{:S(2)}) collective-permute-start(f32[8,128]{1,0:T(8,128)S(1)} %slice_bitcast_fusion.3), channel_id=1, source_target_pairs={{0,1},{1,0},{2,3},{3,2},{4,5},{5,4},{6,7},{7,6},{8,9},{9,8},{10,11... | collective-permute-start | bytes 12296 | tf_op jit(solution)/shard_map/ppermute | solution.py:570
  11.6 7.8 %collective-permute-start.2 = (f32[160,128]{1,0:T(8,128)S(1)}, f32[160,128]{1,0:T(8,128)S(1)}, u32[]{:S(2)}, u32[]{:S(2)}) collective-permute-start(f32[160,128]{1,0:T(8,128)S(1)} %get-tuple-element.61), channel_id=1, source_target_pairs={{0,2},{2,0},{4,6},{6,4},{8,10},{10,8},{12,14},{14,12},{16,18},{18,... | collective-permute-start | bytes 245768 | tf_op jit(solution)/shard_map/ppermute | solution.py:570
  13.3 6.1 %collective-permute-start.3 = (f32[160,128]{1,0:T(8,128)S(1)}, f32[160,128]{1,0:T(8,128)S(1)}, u32[]{:S(2)}, u32[]{:S(2)}) collective-permute-start(f32[160,128]{1,0:T(8,128)S(1)} %get-tuple-element.63), channel_id=1, source_target_pairs={{0,1},{1,0},{2,3},{3,2},{4,5},{5,4},{6,7},{7,6},{8,9},{9,8},{10,11... | collective-permute-start | bytes 245768 | tf_op jit(solution)/shard_map/ppermute | solution.py:570
  21.6 5.1 %collective-permute-start.4 = (f32[3,24,128]{2,1,0:T(8,128)S(1)}, f32[3,24,128]{2,1,0:T(8,128)S(1)}, u32[]{:S(2)}, u32[]{:S(2)}) collective-permute-start(f32[3,24,128]{2,1,0:T(8,128)S(1)} %get-tuple-element.82), channel_id=1, source_target_pairs={{0,2},{2,0},{4,6},{6,4},{8,10},{10,8},{12,14},{14,12},{16,18},{18,... | collective-permute-start | bytes 110600 | tf_op jit(solution)/shard_map/ppermute | solution.py:570
  26.8 2.6 %collective-permute-start.5 = (f32[8,128]{1,0:T(8,128)S(1)}, f32[8,128]{1,0:T(8,128)S(1)}, u32[]{:S(2)}, u32[]{:S(2)}) collective-permute-start(f32[8,128]{1,0:T(8,128)S(1)} %slice_bitcast_fusion.2), channel_id=1, source_target_pairs={{0,1},{1,0},{2,3},{3,2},{4,5},{5,4},{6,7},{7,6},{8,9},{9,8},{10,11... | collective-permute-start | bytes 12296 | tf_op jit(solution)/shard_map/ppermute | solution.py:570
  30.0 7.8 %collective-permute-start.6 = (f32[160,128]{1,0:T(8,128)S(1)}, f32[160,128]{1,0:T(8,128)S(1)}, u32[]{:S(2)}, u32[]{:S(2)}) collective-permute-start(f32[160,128]{1,0:T(8,128)S(1)} %get-tuple-element.78), channel_id=1, source_target_pairs={{0,2},{2,0},{4,6},{6,4},{8,10},{10,8},{12,14},{14,12},{16,18},{18,... | collective-permute-start | bytes 245768 | tf_op jit(solution)/shard_map/ppermute | solution.py:570
  31.6 6.3 %collective-permute-start.7 = (f32[160,128]{1,0:T(8,128)S(1)}, f32[160,128]{1,0:T(8,128)S(1)}, u32[]{:S(2)}, u32[]{:S(2)}) collective-permute-start(f32[160,128]{1,0:T(8,128)S(1)} %get-tuple-element.80), channel_id=1, source_target_pairs={{0,1},{1,0},{2,3},{3,2},{4,5},{5,4},{6,7},{7,6},{8,9},{9,8},{10,11... | collective-permute-start | bytes 245768 | tf_op jit(solution)/shard_map/ppermute | solution.py:570

commit v8 on v7

--- a/solution.py
+++ b/solution.py
@@ -162,14 +162,31 @@
     tiles, rows, _ = grid.shape
     height = rows // CHANNELS
     odd = lax.rem(lax.axis_index("down"), 2)
+    ends = [0.0, 0.0]
     for t in range(tiles):
         turned = jnp.transpose(sums[t * LANES : (t + 1) * LANES, :])
         for c in range(CHANNELS):
             part = turned[c * STRIDE : c * STRIDE + height]
             grid[t, c * height : (c + 1) * height, :] = part
-            spot = slice(c * BAND, (c + 1) * BAND)
-            pay[odd, t, spot, :] = part[height - BAND :]
-            pay[1 - odd, t, spot, :] = part[:BAND]
+            last, first = part[height - BAND :], part[:BAND]
+            if t < tiles - 1:
+                spot = slice((t * CHANNELS + c) * BAND, (t * CHANNELS + c + 1) * BAND)
+                pay[odd, spot, :] = last
+                pay[1 - odd, spot, :] = first
+            else:
+                moved = [pltpu.roll(x, c * BAND, 1) if c else x for x in (last, first)]
+                ends = [end + x for end, x in zip(ends, moved)]
+    spot = slice((tiles - 1) * CHANNELS * BAND, pay.shape[1])
+    pay[odd, spot, :] = ends[0]
+    pay[1 - odd, spot, :] = ends[1]
+
+
+def band_part(band, t, c, tiles):
+    if t < tiles - 1:
+        return band[(t * CHANNELS + c) * BAND : (t * CHANNELS + c + 1) * BAND, :]
+    end = band[(tiles - 1) * CHANNELS * BAND :, :]
+    lane = lax.broadcasted_iota(jnp.int32, (BAND, LANES), 1)
+    return jnp.where(lane < BAND, pltpu.roll(end, LANES - c * BAND, 1) if c else end, 0.0)
 
 
 def first_kernel(
@@ -310,12 +327,11 @@
     there = (partner >= 0) & (partner < size)
     for t in range(tiles):
         for c in range(CHANNELS):
-            spot = slice(c * BAND, (c + 1) * BAND)
             for link in range(2):
                 if link == 0:
-                    band = band0[t, spot, :]
+                    band = band_part(band0, t, c, tiles)
                 else:
-                    band = jnp.where(there, band1[odd, t, spot, :], 0.0)
+                    band = jnp.where(there, band_part(band1.at[odd], t, c, tiles), 0.0)
                 at_first = odd if link == 0 else 1 - odd
                 start = c * height + (1 - at_first) * (height - BAND)
                 place = pl.ds(pl.multiple_of(start, 8), BAND)
@@ -598,7 +614,7 @@
             return jax.ShapeDtypeStruct(shape, dtype)
 
         grid_type = array(tiles, CHANNELS * height, LANES)
-        band_type = array(2, tiles, CHANNELS * BAND, LANES)
+        band_type = array(2, ((tiles - 1) * CHANNELS + 1) * BAND, LANES)
         state_type = array(FIELDS, blocks + ROWS, LANES)
         plane = -(-FIELDS * cap // 8) * 8
         sent_type = array(plane, LANES)

time: 39.3 us -> 39.3 us (level)
  blocking collectives: 20 us -> 19.3 us
    all_gather x4, blocking collectives: 20 us -> 19.3 us  [gather_pairs(): lax.all_gather(x, ('down', 'cross'), axis_index_groups=odd_groups(size_do...]
where the time goes in v8:
time: 39.3 us; the launch traced here: 38.9 us
  blocking collectives  19.3 us (49%)
  Pallas kernels  11.5 us (29%)
  starting transfers between devices  7.55 us (19%)
  waiting for transfers between devices  0.42 us (1%)
    all_gather x4, blocking collectives, gather_pairs(): lax.all_gather(x, ('down', 'cross'), axis_index_groups=odd_groups(size_do...  19.3 us
    ppermute x8, starting transfers between devices, swap(): return lax.ppermute(x, name, swap_pairs(size, second))  7.55 us
    pallas_call x2, Pallas kernels, on_device(): call('gather_inner', functools.partial(inner_kernel, step, links, width),...  3.57 us
    pallas_call x1, Pallas kernels, on_device(): call('scatter_first', functools.partial(first_kernel, 0), (state_type, gr...  3.18 us
    pallas_call x1, Pallas kernels, on_device(): call('scatter_next', functools.partial(next_kernel, step, links), (state_...  2.21 us
    pallas_call x2, Pallas kernels, on_device(): call('gather_edge', functools.partial(edge_kernel, step, links, width, ca...  1.17 us
    pallas_call x1, Pallas kernels, on_device(): call('settle_last', functools.partial(last_kernel, STEPS - 1, links), (pl...  1.11 us
  transfers between devices with their start and end apart: 8, of which 1 were waited for; matrix products, arithmetic and copies ran while one was open for 0% of the time, Pallas kernels for 9%

profile of v8, /device:TPU:11, one launch (start us, length us, event | category | flops | bytes accessed | tf_op | source)
XLA Modules:
  0.0 38.9 jit_solution(5223885078610756727)
XLA Ops:
  0.0 3.2 %scatter_first.1 = (f32[12,136,128]{2,1,0:T(8,128)S(1)}, f32[3,72,128]{2,1,0:T(8,128)S(1)}, f32[2,56,128]{2,1,0:T(8,128)S(1)}, bf16[128,32,256]{2,1,0:T(8,128)(2...) custom-call(s32[2,128]{1,0:T(2,128)} %down_in.1, ...), custom_call_target="tpu_custom_call" | custom-call | bytes 1048576 | tf_op jit(solution)/shard_map/scatter_first/pallas_call | solution.py:638
  3.2 0.7 %collective-permute-start = (f32[56,128]{1,0:T(8,128)S(1)}, f32[56,128]{1,0:T(8,128)S(1)}, u32[]{:S(2)}, u32[]{:S(2)}) collective-permute-start(f32[56,128]{1,0:T(8,128)S(1)} %get-tuple-element.84), channel_id=1, source_target_pairs={{0,2},{2,0},{4,6},{6,4},{8,10},{10,8},{12,14},{14,12},{16,18},{18,... | collective-permute-start | bytes 86024 | tf_op jit(solution)/shard_map/ppermute | solution.py:586
  3.9 4.3 %all_gather.18.band1 = f32[2,56,128]{2,1,0:T(8,128)S(1)} all-gather(f32[1,56,128]{2,1,0:T(8,128)S(1)} %get-tuple-element.83), channel_id=1, replica_groups={{0,1},{30,31},{2,4},{3,5},{6,8},{7,9},{10,12},{11,13},{14,16},{15,17},{..., dimensions={0}, use_global_device_ids=true | all-gather | bytes 86016 | tf_op jit(solution)/shard_map/all_gather | solution.py:589
  8.2 0.0 collective-permute-done.band0
  8.2 0.1 add_down.2
  8.4 0.3 collective-permute-start.1
  8.6 1.8 %gather_inner.2 = (f32[12,136,128]{2,1,0:T(8,128)S(1)}, s32[129]{0:T(256)S(4)}, s32[129]{0:T(256)S(4)}, f32[160,128]{1,0:T(8,128)S(1)}, f32[160,128]{1,0:T(8,128)S(1)}, /*index=5*/f32[160,128]{1,0:T(8,128)S(1)}) custom-call(s32[2,128]{1,0:T(2,128)S(4)} %get-tuple-element.45.anchor_down, s32[2,128]{1,0:T(2,128)S(4)} %get-tuple-element.46.anchor_cross, ...), custom_call_target="tpu_custom_call" | custom-call | flops 4294967296 | bytes 1048576 | tf_op jit(solution)/shard_map/gather_inner/pallas_call | solution.py:671
  10.4 0.4 %collective-permute-done.1.rest_0_ = f32[8,128]{1,0:T(8,128)S(1)} collective-permute-done((f32[8,128]{1,0:T(8,128)S(1)}, f32[8,128]{1,0:T(8,128)S(1)}, u32[]{:S(2)}, u32[]{:S(2)}) %collective-permute-start.1) | collective-permute-done | bytes 4128 | tf_op jit(solution)/shard_map/ppermute | solution.py:586
  10.8 0.6 %gather_edge.2 = (f32[12,136,128]{2,1,0:T(8,128)S(1)}, f32[160,128]{1,0:T(8,128)S(1)}, f32[160,128]{1,0:T(8,128)S(1)}, f32[160,128]{1,0:T(8,128)S(1)}) custom-call(s32[2,128]{1,0:T(2,128)S(4)} %get-tuple-element.45.anchor_down, s32[2,128]{1,0:T(2,128)S(4)} %get-tuple-element.46.anchor_cross, s32[129]{0:T(256)S(4)} %get-tuple-element.53.edge, ...), custom_call_target="tpu_custom_call" | custom-call | bytes 1048576 | tf_op jit(solution)/shard_map/gather_edge/pallas_call | solution.py:680
  11.4 1.9 %collective-permute-start.2 = (f32[160,128]{1,0:T(8,128)S(1)}, f32[160,128]{1,0:T(8,128)S(1)}, u32[]{:S(2)}, u32[]{:S(2)}) collective-permute-start(f32[160,128]{1,0:T(8,128)S(1)} %get-tuple-element.61), channel_id=1, source_target_pairs={{0,2},{2,0},{4,6},{6,4},{8,10},{10,8},{12,14},{14,12},{16,18},{18,... | collective-permute-start | bytes 245768 | tf_op jit(solution)/shard_map/ppermute | solution.py:586
  13.3 0.3 collective-permute-start.3
  13.6 5.4 %all-gather = f32[320,128]{1,0:T(8,128)S(1)} all-gather(f32[160,128]{1,0:T(8,128)S(1)} %get-tuple-element.62), channel_id=2, replica_groups={{0,1},{30,31},{2,4},{3,5},{6,8},{7,9},{10,12},{11,13},{14,16},{15,17},{..., dimensions={0}, use_global_device_ids=true | all-gather | bytes 245760 | tf_op jit(solution)/shard_map/all_gather | solution.py:589
  19.0 0.0 collective-permute-done.2.rest_0_
  19.0 0.0 collective-permute-done.3.rest_2_
  19.0 2.2 %scatter_next.1 = (f32[12,136,128]{2,1,0:T(8,128)S(1)}, f32[3,72,128]{2,1,0:T(8,128)S(1)}, f32[2,56,128]{2,1,0:T(8,128)S(1)}, bf16[128,32,256]{2,1,0:T(8,128)(2,1)S(1)}, f32[128,16,128]{2,1,0:T(8,128)S(1)}) custom-call(s32[2,128]{1,0:T(2,128)S(4)} %get-tuple-element.45.anchor_down, s32[2,128]{1,0:T(2,128)S(4)} %get-tuple-element.46.anchor_cross, ...), custom_call_target="tpu_custom_call" | custom-call | bytes 1048576 | tf_op jit(solution)/shard_map/scatter_next/pallas_call | solution.py:655
  21.3 0.5 %collective-permute-start.4 = (f32[56,128]{1,0:T(8,128)S(1)}, f32[56,128]{1,0:T(8,128)S(1)}, u32[]{:S(2)}, u32[]{:S(2)}) collective-permute-start(f32[56,128]{1,0:T(8,128)S(1)} %get-tuple-element.82), channel_id=1, source_target_pairs={{0,2},{2,0},{4,6},{6,4},{8,10},{10,8},{12,14},{14,12},{16,18},{18,... | collective-permute-start | bytes 86024 | tf_op jit(solution)/shard_map/ppermute | solution.py:586
  21.8 4.3 %all_gather.21.band1 = f32[2,56,128]{2,1,0:T(8,128)S(1)} all-gather(f32[1,56,128]{2,1,0:T(8,128)S(1)} %get-tuple-element.81), channel_id=1, replica_groups={{0,1},{30,31},{2,4},{3,5},{6,8},{7,9},{10,12},{11,13},{14,16},{15,17},{..., dimensions={0}, use_global_device_ids=true | all-gather | bytes 86016 | tf_op jit(solution)/shard_map/all_gather | solution.py:589
  26.1 0.0 collective-permute-done.4.band0
  26.1 0.1 add_down.3
  26.2 1.2 %collective-permute-start.5 = (f32[8,128]{1,0:T(8,128)S(1)}, f32[8,128]{1,0:T(8,128)S(1)}, u32[]{:S(2)}, u32[]{:S(2)}) collective-permute-start(f32[8,128]{1,0:T(8,128)S(1)} %slice_bitcast_fusion.2), channel_id=1, source_target_pairs={{0,1},{1,0},{2,3},{3,2},{4,5},{5,4},{6,7},{7,6},{8,9},{9,8},{10,11... | collective-permute-start | bytes 12296 | tf_op jit(solution)/shard_map/ppermute | solution.py:586
  27.4 1.8 %gather_inner.3 = (f32[12,136,128]{2,1,0:T(8,128)S(1)}, s32[129]{0:T(256)S(4)}, s32[129]{0:T(256)S(4)}, f32[160,128]{1,0:T(8,128)S(1)}, f32[160,128]{1,0:T(8,128)S(1)}, /*index=5*/f32[160,128]{1,0:T(8,128)S(1)}) custom-call(s32[2,128]{1,0:T(2,128)S(4)} %get-tuple-element.45.anchor_down, s32[2,128]{1,0:T(2,128)S(4)} %get-tuple-element.46.anchor_cross, ...), custom_call_target="tpu_custom_call" | custom-call | flops 4294967296 | bytes 1048576 | tf_op jit(solution)/shard_map/gather_inner/pallas_call | solution.py:671
  29.2 0.0 collective-permute-done.5.rest_0_
  29.2 0.6 %gather_edge.3 = (f32[12,136,128]{2,1,0:T(8,128)S(1)}, f32[160,128]{1,0:T(8,128)S(1)}, f32[160,128]{1,0:T(8,128)S(1)}, f32[160,128]{1,0:T(8,128)S(1)}) custom-call(s32[2,128]{1,0:T(2,128)S(4)} %get-tuple-element.45.anchor_down, s32[2,128]{1,0:T(2,128)S(4)} %get-tuple-element.46.anchor_cross, s32[129]{0:T(256)S(4)} %get-tuple-element.70.edge, ...), custom_call_target="tpu_custom_call" | custom-call | bytes 1048576 | tf_op jit(solution)/shard_map/gather_edge/pallas_call | solution.py:680
  29.8 1.4 %collective-permute-start.6 = (f32[160,128]{1,0:T(8,128)S(1)}, f32[160,128]{1,0:T(8,128)S(1)}, u32[]{:S(2)}, u32[]{:S(2)}) collective-permute-start(f32[160,128]{1,0:T(8,128)S(1)} %get-tuple-element.78), channel_id=1, source_target_pairs={{0,2},{2,0},{4,6},{6,4},{8,10},{10,8},{12,14},{14,12},{16,18},{18,... | collective-permute-start | bytes 245768 | tf_op jit(solution)/shard_map/ppermute | solution.py:586
  31.2 1.2 %collective-permute-start.7 = (f32[160,128]{1,0:T(8,128)S(1)}, f32[160,128]{1,0:T(8,128)S(1)}, u32[]{:S(2)}, u32[]{:S(2)}) collective-permute-start(f32[160,128]{1,0:T(8,128)S(1)} %get-tuple-element.80), channel_id=1, source_target_pairs={{0,1},{1,0},{2,3},{3,2},{4,5},{5,4},{6,7},{7,6},{8,9},{9,8},{10,11... | collective-permute-start | bytes 245768 | tf_op jit(solution)/shard_map/ppermute | solution.py:586
  32.4 5.4 %all-gather.1 = f32[320,128]{1,0:T(8,128)S(1)} all-gather(f32[160,128]{1,0:T(8,128)S(1)} %get-tuple-element.79), channel_id=3, replica_groups={{0,1},{30,31},{2,4},{3,5},{6,8},{7,9},{10,12},{11,13},{14,16},{15,17},{..., dimensions={0}, use_global_device_ids=true | all-gather | bytes 245760 | tf_op jit(solution)/shard_map/all_gather | solution.py:589
  37.8 0.0 collective-permute-done.6.rest_0_
  37.8 0.0 collective-permute-done.7.rest_2_
  37.8 1.1 %settle_last.1 = f32[12,128,128]{2,1,0:T(8,128)} custom-call(s32[2,4,13]{2,1,0:T(4,128)S(4)} %get-tuple-element.43.slots, s32[2,4]{1,0:T(2,128)S(4)} %get-tuple-element.44.counts, f32[12,136,128]{2,1,0:T(8,128)S(1)} %get-tuple-element.77.old, f32[160,128]{1,0:T(8,128)S(1)} %collective-permute-done.6.rest_0_, f32[2,160,128]{2,1,0:T(8,128)S(1)} %bitcast.14, ...), custom_call_target="tpu_custom_call" | custom-call | bytes 1048576 | tf_op jit(solution)/shard_map/settle_last/pallas_call | solution.py:695
  (4 shorter events, 0.0 us)
Async XLA Ops:
  3.2 5.0 %collective-permute-start = (f32[56,128]{1,0:T(8,128)S(1)}, f32[56,128]{1,0:T(8,128)S(1)}, u32[]{:S(2)}, u32[]{:S(2)}) collective-permute-start(f32[56,128]{1,0:T(8,128)S(1)} %get-tuple-element.84), channel_id=1, source_target_pairs={{0,2},{2,0},{4,6},{6,4},{8,10},{10,8},{12,14},{14,12},{16,18},{18,... | collective-permute-start | bytes 86024 | tf_op jit(solution)/shard_map/ppermute | solution.py:586
  8.4 2.5 %collective-permute-start.1 = (f32[8,128]{1,0:T(8,128)S(1)}, f32[8,128]{1,0:T(8,128)S(1)}, u32[]{:S(2)}, u32[]{:S(2)}) collective-permute-start(f32[8,128]{1,0:T(8,128)S(1)} %slice_bitcast_fusion.3), channel_id=1, source_target_pairs={{0,1},{1,0},{2,3},{3,2},{4,5},{5,4},{6,7},{7,6},{8,9},{9,8},{10,11... | collective-permute-start | bytes 12296 | tf_op jit(solution)/shard_map/ppermute | solution.py:586
  11.4 7.6 %collective-permute-start.2 = (f32[160,128]{1,0:T(8,128)S(1)}, f32[160,128]{1,0:T(8,128)S(1)}, u32[]{:S(2)}, u32[]{:S(2)}) collective-permute-start(f32[160,128]{1,0:T(8,128)S(1)} %get-tuple-element.61), channel_id=1, source_target_pairs={{0,2},{2,0},{4,6},{6,4},{8,10},{10,8},{12,14},{14,12},{16,18},{18,... | collective-permute-start | bytes 245768 | tf_op jit(solution)/shard_map/ppermute | solution.py:586
  13.3 5.7 %collective-permute-start.3 = (f32[160,128]{1,0:T(8,128)S(1)}, f32[160,128]{1,0:T(8,128)S(1)}, u32[]{:S(2)}, u32[]{:S(2)}) collective-permute-start(f32[160,128]{1,0:T(8,128)S(1)} %get-tuple-element.63), channel_id=1, source_target_pairs={{0,1},{1,0},{2,3},{3,2},{4,5},{5,4},{6,7},{7,6},{8,9},{9,8},{10,11... | collective-permute-start | bytes 245768 | tf_op jit(solution)/shard_map/ppermute | solution.py:586
  21.3 4.8 %collective-permute-start.4 = (f32[56,128]{1,0:T(8,128)S(1)}, f32[56,128]{1,0:T(8,128)S(1)}, u32[]{:S(2)}, u32[]{:S(2)}) collective-permute-start(f32[56,128]{1,0:T(8,128)S(1)} %get-tuple-element.82), channel_id=1, source_target_pairs={{0,2},{2,0},{4,6},{6,4},{8,10},{10,8},{12,14},{14,12},{16,18},{18,... | collective-permute-start | bytes 86024 | tf_op jit(solution)/shard_map/ppermute | solution.py:586
  26.2 3.0 %collective-permute-start.5 = (f32[8,128]{1,0:T(8,128)S(1)}, f32[8,128]{1,0:T(8,128)S(1)}, u32[]{:S(2)}, u32[]{:S(2)}) collective-permute-start(f32[8,128]{1,0:T(8,128)S(1)} %slice_bitcast_fusion.2), channel_id=1, source_target_pairs={{0,1},{1,0},{2,3},{3,2},{4,5},{5,4},{6,7},{7,6},{8,9},{9,8},{10,11... | collective-permute-start | bytes 12296 | tf_op jit(solution)/shard_map/ppermute | solution.py:586
  29.8 8.0 %collective-permute-start.6 = (f32[160,128]{1,0:T(8,128)S(1)}, f32[160,128]{1,0:T(8,128)S(1)}, u32[]{:S(2)}, u32[]{:S(2)}) collective-permute-start(f32[160,128]{1,0:T(8,128)S(1)} %get-tuple-element.78), channel_id=1, source_target_pairs={{0,2},{2,0},{4,6},{6,4},{8,10},{10,8},{12,14},{14,12},{16,18},{18,... | collective-permute-start | bytes 245768 | tf_op jit(solution)/shard_map/ppermute | solution.py:586
  31.2 6.6 %collective-permute-start.7 = (f32[160,128]{1,0:T(8,128)S(1)}, f32[160,128]{1,0:T(8,128)S(1)}, u32[]{:S(2)}, u32[]{:S(2)}) collective-permute-start(f32[160,128]{1,0:T(8,128)S(1)} %get-tuple-element.80), channel_id=1, source_target_pairs={{0,1},{1,0},{2,3},{3,2},{4,5},{5,4},{6,7},{7,6},{8,9},{9,8},{10,11... | collective-permute-start | bytes 245768 | tf_op jit(solution)/shard_map/ppermute | solution.py:586
